TPU v7x, 512 devices: a whole 4x4x16 slice. The times are simulated.
512 devices in a mesh: blade: 64 (over z_lo, y, x), span: 8 (over z_hi, core).
Axes of the slice: x: 4, y: 4, z: 16 (z_hi: 4, z_lo: 4; z = z_hi * 4 + z_lo), core: 2. Of those that a mesh axis runs over, the one named last changes fastest.
Arguments:
- particles: float32 [11, 128, 256, 128], P(None, 'blade', 'span')
- filled: int32 [128, 256], P('blade', 'span'), may hold values from 2 to 96, as said below
- contact_pairs: int32 [2, 128, 256, 128], P(None, 'blade', 'span'), may hold values from 0 to 639, as said below
- contact_count: int32 [128, 256], P('blade', 'span'), may hold values from 32 to 128
- movers_out: int32 [2, 2, 64, 128], P(None, None, 'blade', 'span'), may hold values from 0 to 95, as said below
- movers_in: int32 [2, 2, 64, 128], P(None, None, 'blade', 'span'), may hold values from 0 to 127, as said below
- move_count: int32 [2, 64, 8], P(None, 'blade', 'span'), may hold values from 0 to 16, as said below
Outputs:
- advanced: float32 [11, 128, 256, 128], P(None, 'blade', 'span')
Inputs may be any that keep to these rules, and one draw needn't show every extreme that they name: Live slots of a cell are its first filled ones. `contact_pairs`: every entry, counted or not, joins two live particles; direction 0 joins a slot with a higher slot of the same cell; directions never point outside the grid. The same pair may be listed more than once and then acts once per entry. `movers_out`: component 0 holds cells of the block (0 to 63), component 1 slots (below 96). Forward leavers sit in the block's last blade row, backward leavers in its first; within a device block and direction each leaver has its own cell, and each is a live slot. `movers_in`: component 0 holds cells of the block (0 to 63), component 1 slots. Arrivals from behind land in the block's first blade row, from ahead in its last; every slot is 96 or higher, and the 32 slots of one device block are all different. `move_count`: zero in the forward direction on the last blade device and in the backward direction on the first.
All inputs are finite; a program needn't handle non-finite values.
Results may differ from a plain program's by a relative error of at most 0.0001.
Values sent between devices are 32-bit elements; how exact they have to be, the bound alone decides.
No kernel may reach another device: no remote copies, remote signals or barrier semaphores. Data moves between devices by JAX's collectives and lax.ppermute only.
A program may use at most 64 MiB of HBM per device.

v0:
```python
import jax
import jax.numpy as jnp
from jax import lax
from jax.sharding import PartitionSpec as P

spring = 4.0
normal_damp = 0.5
tangent_damp = 0.3
conduct = 40.0
timestep_length = 0.05
density = 100.0
gravity = 9.81
soft_len = 0.05
row_steps = (0, 1, 0, 1, 1)
col_steps = (0, 0, 1, 1, -1)


def passed_along(block, axis, distance):
    devices = range(lax.axis_size(axis))
    route = [(i - distance, i) for i in devices if i - distance in devices]
    return lax.ppermute(block, axis, route)


def extended(block, sides, width):
    for axis, dim in sides:
        count = lax.axis_size(axis)
        forward = [(i, i + 1) for i in range(count - 1)]
        backward = [(target, source) for source, target in forward]
        low = lax.ppermute(
            lax.slice_in_dim(block, block.shape[dim] - width, None, axis=dim), axis, forward
        )
        high = lax.ppermute(lax.slice_in_dim(block, 0, width, axis=dim), axis, backward)
        block = jnp.concatenate([low, block, high], axis=dim)
    return block


def cross_product(left_vec, right_vec):
    return jnp.stack(
        [
            left_vec[1] * right_vec[2] - left_vec[2] * right_vec[1],
            left_vec[2] * right_vec[0] - left_vec[0] * right_vec[2],
            left_vec[0] * right_vec[1] - left_vec[1] * right_vec[0],
        ]
    )


def pair_terms(first_state, second, row_shift, col_shift, occupancy_marks):
    offset = jnp.stack([row_shift, col_shift, jnp.zeros_like(row_shift)])
    gap_vec = second[0:3] + offset - first_state[0:3]
    distance = jnp.sqrt(jnp.sum(gap_vec * gap_vec, axis=0) + soft_len * soft_len)
    normal = gap_vec / distance
    rad_first = first_state[9]
    rad_second = second[9]
    intersection = rad_first + rad_second - distance
    spin_sum = rad_first * first_state[6:9] + rad_second * second[6:9]
    relative = second[3:6] - first_state[3:6] - cross_product(spin_sum, normal)
    normal_speed = jnp.sum(relative * normal, axis=0)
    friction = tangent_damp * (relative - normal_speed * normal)
    contact_force = (normal_damp * normal_speed - spring * intersection) * normal + friction
    torque_dir = cross_product(normal, friction)
    denom = jnp.where(occupancy_marks > 0, rad_first + rad_second, 1.0)
    heat_flow = 2.0 * conduct * rad_first * rad_second / denom * (second[10] - first_state[10])
    on_first = (
        jnp.concatenate([contact_force, rad_first * torque_dir, heat_flow[None]], 0)
        * occupancy_marks
    )
    on_second = (
        jnp.concatenate([-contact_force, rad_second * torque_dir, -heat_flow[None]], 0)
        * occupancy_marks
    )
    return (on_first, on_second)


def accumulate(ghosted, pairs, occupancy_marks, row_base, col_base):
    components = ghosted.shape[0]
    total_rows = ghosted.shape[1]
    total_cols = ghosted.shape[2]
    tile_slots = ghosted.shape[3]
    region_rows = pairs.shape[1]
    region_cols = pairs.shape[2]
    slot_ids = jnp.arange(tile_slots, dtype=jnp.int32)
    heading_ids = jnp.arange(5, dtype=jnp.int32)
    highest = lax.Precision.HIGHEST

    def row_pass(carry, tile_row):
        firsts = lax.dynamic_index_in_dim(pairs[0], tile_row, 0, keepdims=False)
        seconds = lax.dynamic_index_in_dim(pairs[1], tile_row, 0, keepdims=False)
        weights = lax.dynamic_index_in_dim(occupancy_marks, tile_row, 0, keepdims=False)
        heading = seconds // tile_slots
        target = seconds % tile_slots
        own_hot = (firsts[..., None] == slot_ids).astype(jnp.float32)
        far_hot = (target[..., None] == slot_ids).astype(jnp.float32)
        chooser = (heading[:, None, :] == heading_ids[None, :, None]).astype(jnp.float32)
        neighbours = jnp.stack(
            [
                lax.dynamic_slice(
                    ghosted,
                    (0, row_base + tile_row + row_steps[which], col_base + col_steps[which], 0),
                    (components, 1, region_cols, tile_slots),
                )[:, 0]
                for which in range(5)
            ],
            2,
        )
        first_state = jnp.einsum("cgs,gks->cgk", neighbours[:, :, 0], own_hot, precision=highest)
        spread_states = jnp.einsum("cgds,gks->cgdk", neighbours, far_hot, precision=highest)
        second = jnp.sum(spread_states * chooser[None], axis=2)
        row_shift = jnp.where((heading == 0) | (heading == 2), 0.0, 1.0).astype(jnp.float32)
        col_shift = jnp.where(
            (heading == 2) | (heading == 3), 1.0, jnp.where(heading == 4, -1.0, 0.0)
        ).astype(jnp.float32)
        on_first, on_second = pair_terms(first_state, second, row_shift, col_shift, weights)
        own_sum = jnp.einsum("cgk,gks->cgs", on_first, own_hot, precision=highest)
        far_sum = jnp.einsum(
            "cgdk,gks->cgds", on_second[:, :, None, :] * chooser[None], far_hot, precision=highest
        )
        pieces = (own_sum + far_sum[:, :, 0],) + tuple(
            (far_sum[:, :, which] for which in range(1, 5))
        )
        return (carry, pieces)

    _, stacked = lax.scan(
        row_pass, jnp.zeros((), jnp.float32), jnp.arange(region_rows, dtype=jnp.int32)
    )
    totals = jnp.zeros((7, total_rows, total_cols, tile_slots), jnp.float32)
    for which in range(5):
        placed = jnp.transpose(stacked[which], (1, 0, 2, 3))
        low_row = row_base + row_steps[which]
        low_col = col_base + col_steps[which]
        totals = totals + jnp.pad(
            placed,
            (
                (0, 0),
                (low_row, total_rows - low_row - region_rows),
                (low_col, total_cols - low_col - region_cols),
                (0, 0),
            ),
        )
    return totals


def advance(grain_record, cumulative_sums, occupancy_marks):
    grain_halfwidth = grain_record[9]
    safe_radius = grain_halfwidth + (1.0 - occupancy_marks)
    grain_inertia = density * safe_radius**3
    accel_vec = cumulative_sums[0:3] / grain_inertia
    accel_vec = jnp.concatenate([accel_vec[0:2], accel_vec[2:3] - gravity], 0)
    translational_rate = grain_record[3:6] + timestep_length * accel_vec
    spin_rate = grain_record[6:9] + timestep_length * cumulative_sums[3:6] / (
        0.4 * grain_inertia * safe_radius * safe_radius
    )
    grain_location = grain_record[0:3] + timestep_length * translational_rate
    grain_warmth = grain_record[10] + timestep_length * cumulative_sums[6] / grain_inertia
    return (
        jnp.concatenate(
            [
                grain_location,
                translational_rate,
                spin_rate,
                grain_halfwidth[None],
                grain_warmth[None],
            ],
            0,
        )
        * occupancy_marks
    )


def body(particles, filled, contact_pairs, contact_count, movers_out, movers_in, move_count):
    components = particles.shape[0]
    blade_cells = particles.shape[1]
    span_cells = particles.shape[2]
    tile_slots = particles.shape[3]
    pair_slots = contact_pairs.shape[3]
    listed = jnp.arange(pair_slots, dtype=jnp.int32) < contact_count[..., None]
    next_row = passed_along(particles[:, 0:1], "blade", -1)
    ghosted = extended(jnp.concatenate([particles, next_row], 1), (("span", 2),), 1)
    cumulative_sums = accumulate(ghosted, contact_pairs, listed.astype(jnp.float32), 0, 1)
    lower_rim = passed_along(cumulative_sums[:, :, 0:1], "span", -1)
    upper_rim = passed_along(cumulative_sums[:, :, span_cells + 1 :], "span", 1)
    folded = cumulative_sums[:, :, 1 : span_cells + 1]
    folded = folded.at[:, :, span_cells - 1 :].add(lower_rim).at[:, :, 0:1].add(upper_rim)
    passed_on = passed_along(folded[:, blade_cells:], "blade", 1)
    forces = folded[:, :blade_cells].at[:, 0:1].add(passed_on)
    occupancy_marks = (jnp.arange(tile_slots, dtype=jnp.int32) < filled[..., None]).astype(
        jnp.float32
    )
    stepped = advance(particles, forces, occupancy_marks)
    flattened = stepped.reshape(components, -1)
    leaving = movers_out.reshape(2, 2, -1)
    movers = leaving.shape[2]
    sources_at = leaving[:, 0] * tile_slots + leaving[:, 1]
    moving = (jnp.arange(movers, dtype=jnp.int32) < move_count.reshape(2, 1)).astype(jnp.float32)
    initial = jnp.take(flattened, sources_at.reshape(-1), axis=1).reshape(components, 2, movers)
    sent = initial * moving
    signs_dir = jnp.array([-1.0, 1.0], jnp.float32)[:, None]
    sent = sent.at[0].add(signs_dir * moving)
    flattened = flattened.at[:, sources_at.reshape(-1)].set(
        (initial * (1.0 - moving)).reshape(components, -1)
    )
    from_behind = passed_along(sent[:, 0], "blade", 1)
    from_ahead = passed_along(sent[:, 1], "blade", -1)
    arriving = movers_in.reshape(2, 2, -1)
    targets = arriving[:, 0] * tile_slots + arriving[:, 1]
    flattened = flattened.at[:, targets[0]].set(from_behind).at[:, targets[1]].set(from_ahead)
    return flattened.reshape(particles.shape)


def solution(mesh):
    return jax.shard_map(
        body,
        mesh=mesh,
        in_specs=(
            P(None, "blade", "span", None),
            P("blade", "span"),
            P(None, "blade", "span", None),
            P("blade", "span"),
            P(None, None, "blade", "span"),
            P(None, None, "blade", "span"),
            P(None, "blade", "span"),
        ),
        out_specs=P(None, "blade", "span", None),
        check_vma=False,
    )
```

profile of v0, /device:TPU:416, one launch (start us, length us, event | category | flops | bytes accessed | tf_op | source)
XLA Modules:
  0.0 127.8 jit_solution(16084310115775243239)
XLA Ops:
  1.1 7.6 %collective-permute-start = (f32[11,1,32,128]{3,0,2,1:T(8,128)S(1)}, f32[11,1,32,128]{3,0,2,1:T(8,128)S(1)}, u32[]{:S(2)}, u32[]{:S(2)}) collective-permute-start(f32[11,1,32,128]{3,0,2,1:T(8,128)S(1)} %copy.80), channel_id=1, source_target_pairs={{8,0},{16,8},{24,16},{32,24},{40,32},{48,40},{56,48},{64,56},{72,6... | collective-permute-start | bytes 540680 | tf_op jit(solution)/shard_map/ppermute | solution.py:21
  8.7 1.2 copy_dynamic-update-slice_fusion.5
  11.3 1.4 %fusion.60 = f32[2,32,128]{2,1,0:T(8,128)} fusion(s32[2,32]{1,0:T(2,128)} %param.19), kind=kLoop, calls=%fused_computation.132 | loop fusion | flops 16384 | bytes 33024 | tf_op jit(solution)/shard_map/convert_element_type | solution.py:185
  14.9 1.4 %fusion.79 = (s32[2,16]{1,0:T(2,128)S(1)}, s32[2,1,16]{2,1,0:T(1,128)S(1)}) fusion(s32[]{:T(128)} %broadcast.757, s32[2,2,16]{2,1,0:T(2,128)} %bitcast.258), kind=kLoop, calls=%fused_computation.177 | loop fusion | flops 64 | bytes 516 | tf_op jit(solution)/shard_map/add | solution.py:192
  16.3 1.3 %compare_convert_fusion.1 = (f32[2,16]{1,0:T(2,128)}, pred[2,16]{1,0:T(4,128)(4,1)}) fusion(s32[2]{0:T(128)} %bitcast.255, s32[2,16]{1,0:T(2,128)S(1)} %bitcast.252), kind=kLoop, calls=%fused_computation.161 | loop fusion | flops 256 | bytes 296 | tf_op jit(solution)/shard_map/convert_element_type | solution.py:193
  18.2 4.6 %collective-permute-start.2 = (f32[11,3,1,128]{3,0,2,1:T(8,128)S(1)}, f32[11,3,1,128]{3,0,2,1:T(8,128)S(1)}, u32[]{:S(2)}, u32[]{:S(2)}) collective-permute-start(f32[11,3,1,128]{3,0,2,1:T(8,128)S(1)} %get-tuple-element.328), channel_id=1, source_target_pairs={{1,0},{2,1},{3,2},{4,3},{5,4},{6,5},{7,6},{9,8},{10,9},{11,10},{12... | collective-permute-start | bytes 50696 | tf_op jit(solution)/shard_map/ppermute | solution.py:32
  22.8 1.9 %collective-permute-start.1 = (f32[11,3,1,128]{3,0,2,1:T(8,128)S(1)}, f32[11,3,1,128]{3,0,2,1:T(8,128)S(1)}, u32[]{:S(2)}, u32[]{:S(2)}) collective-permute-start(f32[11,3,1,128]{3,0,2,1:T(8,128)S(1)} %get-tuple-element.327), channel_id=1, source_target_pairs={{0,1},{1,2},{2,3},{3,4},{4,5},{5,6},{6,7},{8,9},{9,10},{10,11},{11... | collective-permute-start | bytes 50696 | tf_op jit(solution)/shard_map/ppermute | solution.py:29
  25.8 6.2 %collective-permute-done.1 = f32[11,3,1,128]{3,0,2,1:T(8,128)S(1)} collective-permute-done((f32[11,3,1,128]{3,0,2,1:T(8,128)S(1)}, f32[11,3,1,128]{3,0,2,1:T(8,128)S(1)}, u32[]{:S(2)}, u32[]{:S(2)}) %collective-permute-start.1) | collective-permute-done | bytes 16928 | tf_op jit(solution)/shard_map/ppermute | solution.py:29
  32.1 32.4 %while.26 = (s32[]{:T(128)}, f32[2,7,32,128]{3,2,0,1:T(8,128)S(1)}, f32[2,7,32,128]{3,2,0,1:T(8,128)S(1)}, f32[2,7,32,128]{3,2,0,1:T(8,128)S(1)}, f32[2,7,32,128...) while((s32[]{:T(128)}, f32[2,7,32,128]{3,2,0,1:T(8,128)S(1)}, ...), condition=%wide.region_4.5_spmd.clone.clone, body=%wide.region_0.4_spmd.clone.clone.sunk | while | flops 683089920 | bytes 12190282 | solution.py:122
  36.0 2.4 %fusion.105 = f32[11,32,128]{2,0,1:T(8,128)S(1)} fusion(s32[32,128]{1,0:T(8,128)S(1)} %dynamic-slice_bitcast_fusion.2, f32[11,3,34,128]{3,0,2,1:T(8,128)S(1)} %get-tuple-element.507, s32[]{:T(128)S(6)} %select_n.249), kind=kOutput, calls=%fused_computation.18.clone.1 | convolution fusion | flops 69730304 | bytes 458756 | tf_op jit(solution)/shard_map/while/body/eval_jaxpr/cgs,gks->cgk/dot_general | solution.py:105
  39.9 2.5 %fusion.106 = f32[11,32,128]{2,0,1:T(8,128)S(1)} fusion(f32[11,32,5,128]{3,0,2,1:T(8,128)S(1)} %bitcast_dynamic-update-slice_fusion.14, s32[32,128]{1,0:T(8,128)S(1)} %add_select_fusion.5, f32[32,5,128]{2,1,0:T(8,128)S(1)} %fusion.104), kind=kOutput, calls=%fused_computation.16.clone.1 | convolution fusion | flops 346959872 | bytes 1179648 | tf_op jit(solution)/shard_map/while/body/eval_jaxpr/cgds,gks->cgdk/dot_general | solution.py:106
  43.4 2.1 %fusion.110 = f32[7,32,5,128]{3,0,1,2:T(8,128)S(1)} fusion(s32[32,128]{1,0:T(8,128)S(1)} %add_select_fusion.5, f32[32,5,128]{2,1,0:T(8,128)S(1)} %fusion.104, f32[7,32,128]{2,0,1:T(8,128)S(1)} %maximum_multiply_fusion.7), kind=kOutput, calls=%fused_computation.17.clone.1 | convolution fusion | flops 220868608 | bytes 786432 | tf_op jit(solution)/shard_map/while/body/eval_jaxpr/cgdk,gks->cgds/dot_general | solution.py:114
  45.5 1.8 %fusion.111 = f32[1,7,32,128]{3,1,2,0:T(8,128)S(1)} fusion(s32[32,128]{1,0:T(8,128)S(1)} %copy-done.6, f32[7,32,5,128]{3,0,1,2:T(8,128)S(1)} %fusion.110, f32[1,32,128]{2,0,1:T(1,128)S(1)} %get-tuple-element.456, f32[3,32,128]{2,0,1:T(4,128)S(1)} %get-tuple-element.457, f32[3,32,128]{2,0,1:T(4,128)S(1)} %get-tuple-element.458, ...), kind=kOutput, calls=%fused_computation.21.clone.1 | convolution fusion | flops 44679168 | bytes 376832 | tf_op jit(solution)/shard_map/while/body/eval_jaxpr/cgk,gks->cgs/dot_general | solution.py:113
  52.2 2.4 %fusion.105 = f32[11,32,128]{2,0,1:T(8,128)S(1)} fusion(s32[32,128]{1,0:T(8,128)S(1)} %dynamic-slice_bitcast_fusion.2, f32[11,3,34,128]{3,0,2,1:T(8,128)S(1)} %get-tuple-element.507, s32[]{:T(128)S(6)} %select_n.249), kind=kOutput, calls=%fused_computation.18.clone.1 | convolution fusion | flops 69730304 | bytes 458756 | tf_op jit(solution)/shard_map/while/body/eval_jaxpr/cgs,gks->cgk/dot_general | solution.py:105
  56.1 2.5 %fusion.106 = f32[11,32,128]{2,0,1:T(8,128)S(1)} fusion(f32[11,32,5,128]{3,0,2,1:T(8,128)S(1)} %bitcast_dynamic-update-slice_fusion.14, s32[32,128]{1,0:T(8,128)S(1)} %add_select_fusion.5, f32[32,5,128]{2,1,0:T(8,128)S(1)} %fusion.104), kind=kOutput, calls=%fused_computation.16.clone.1 | convolution fusion | flops 346959872 | bytes 1179648 | tf_op jit(solution)/shard_map/while/body/eval_jaxpr/cgds,gks->cgdk/dot_general | solution.py:106
  59.6 2.0 %fusion.110 = f32[7,32,5,128]{3,0,1,2:T(8,128)S(1)} fusion(s32[32,128]{1,0:T(8,128)S(1)} %add_select_fusion.5, f32[32,5,128]{2,1,0:T(8,128)S(1)} %fusion.104, f32[7,32,128]{2,0,1:T(8,128)S(1)} %maximum_multiply_fusion.7), kind=kOutput, calls=%fused_computation.17.clone.1 | convolution fusion | flops 220868608 | bytes 786432 | tf_op jit(solution)/shard_map/while/body/eval_jaxpr/cgdk,gks->cgds/dot_general | solution.py:114
  61.7 1.8 %fusion.111 = f32[1,7,32,128]{3,1,2,0:T(8,128)S(1)} fusion(s32[32,128]{1,0:T(8,128)S(1)} %copy-done.6, f32[7,32,5,128]{3,0,1,2:T(8,128)S(1)} %fusion.110, f32[1,32,128]{2,0,1:T(1,128)S(1)} %get-tuple-element.456, f32[3,32,128]{2,0,1:T(4,128)S(1)} %get-tuple-element.457, f32[3,32,128]{2,0,1:T(4,128)S(1)} %get-tuple-element.458, ...), kind=kOutput, calls=%fused_computation.21.clone.1 | convolution fusion | flops 44679168 | bytes 376832 | tf_op jit(solution)/shard_map/while/body/eval_jaxpr/cgk,gks->cgs/dot_general | solution.py:113
  65.4 2.1 %collective-permute-start.3 = (f32[7,3,1,128]{3,2,1,0:T(1,128)S(1)}, f32[7,3,1,128]{3,2,1,0:T(1,128)S(1)}, u32[]{:S(2)}, u32[]{:S(2)}) collective-permute-start(f32[7,3,1,128]{3,2,1,0:T(1,128)S(1)} %get-tuple-element.326), channel_id=1, source_target_pairs={{1,0},{2,1},{3,2},{4,3},{5,4},{6,5},{7,6},{9,8},{10,9},{11,10},{12... | collective-permute-start | bytes 32264 | tf_op jit(solution)/shard_map/ppermute | solution.py:21
  67.5 1.1 pad_add_fusion
  68.6 2.4 %collective-permute-start.4 = (f32[7,3,1,128]{3,2,1,0:T(1,128)S(1)}, f32[7,3,1,128]{3,2,1,0:T(1,128)S(1)}, u32[]{:S(2)}, u32[]{:S(2)}) collective-permute-start(f32[7,3,1,128]{3,2,1,0:T(1,128)S(1)} %get-tuple-element.325), channel_id=1, source_target_pairs={{0,1},{1,2},{2,3},{3,4},{4,5},{5,6},{6,7},{8,9},{9,10},{10,11},{11... | collective-permute-start | bytes 32264 | tf_op jit(solution)/shard_map/ppermute | solution.py:21
  71.2 6.4 %collective-permute-done.4 = f32[7,3,1,128]{3,2,1,0:T(1,128)S(1)} collective-permute-done((f32[7,3,1,128]{3,2,1,0:T(1,128)S(1)}, f32[7,3,1,128]{3,2,1,0:T(1,128)S(1)}, u32[]{:S(2)}, u32[]{:S(2)}) %collective-permute-start.4) | collective-permute-done | bytes 10784 | tf_op jit(solution)/shard_map/ppermute | solution.py:21
  77.7 1.9 %collective-permute-start.5 = (f32[7,1,32,128]{3,2,1,0:T(8,128)S(1)}, f32[7,1,32,128]{3,2,1,0:T(8,128)S(1)}, u32[]{:S(2)}, u32[]{:S(2)}) collective-permute-start(f32[7,1,32,128]{3,2,1,0:T(8,128)S(1)} %slice.477), channel_id=1, source_target_pairs={{0,8},{8,16},{16,24},{24,32},{32,40},{40,48},{48,56},{56,64},{64,7... | collective-permute-start | bytes 344072 | tf_op jit(solution)/shard_map/ppermute | solution.py:21
  79.7 8.8 %collective-permute-done.5 = f32[7,1,32,128]{3,2,1,0:T(8,128)S(1)} collective-permute-done((f32[7,1,32,128]{3,2,1,0:T(8,128)S(1)}, f32[7,1,32,128]{3,2,1,0:T(8,128)S(1)}, u32[]{:S(2)}, u32[]{:S(2)}) %collective-permute-start.5) | collective-permute-done | bytes 114720 | tf_op jit(solution)/shard_map/ppermute | solution.py:21
  89.7 2.7 %copy.46 = f32[11,8192]{0,1:T(8,128)} copy(f32[11,8192]{1,0:T(8,128)S(1)} %concatenate.59) | data formatting | bytes 720896 | tf_op jit(solution)/shard_map/concatenate | solution.py:155
  92.4 4.2 %broadcast_multiply_fusion.2 = f32[11,8192]{0,1:T(8,128)} fusion(f32[11,8192]{0,1:T(8,128)} %copy.46, f32[8192]{0:T(1024)S(1)} %bitcast.248), kind=kLoop, calls=%fused_computation.105 | loop fusion | flops 90112 | bytes 753664 | tf_op jit(solution)/shard_map/mul | solution.py:155
  96.6 2.8 %gather_fusion = f32[32,11]{1,0:T(8,128)S(1)} fusion(f32[11,8192]{0,1:T(8,128)} %broadcast_multiply_fusion.2, s32[1024]{0:T(1024)S(1)} %pad_clamp_fusion), kind=kCustom, calls=%fused_computation | custom fusion | bytes 2944 | tf_op jit(solution)/shard_map/jit(_take)/gather | solution.py:194
  99.6 1.9 %collective-permute-start.6 = (f32[11,16]{0,1:T(8,128)S(1)}, f32[11,16]{0,1:T(8,128)S(1)}, u32[]{:S(2)}, u32[]{:S(2)}) collective-permute-start(f32[11,16]{0,1:T(8,128)S(1)} %get-tuple-element.335), channel_id=1, source_target_pairs={{0,8},{8,16},{16,24},{24,32},{32,40},{40,48},{48,56},{56,64},{64,7... | collective-permute-start | bytes 2120 | tf_op jit(solution)/shard_map/ppermute | solution.py:21
  101.5 8.1 %collective-permute-start.7 = (f32[11,16]{0,1:T(8,128)S(1)}, f32[11,16]{0,1:T(8,128)S(1)}, u32[]{:S(2)}, u32[]{:S(2)}) collective-permute-start(f32[11,16]{0,1:T(8,128)S(1)} %get-tuple-element.334), channel_id=1, source_target_pairs={{8,0},{16,8},{24,16},{32,24},{40,32},{48,40},{56,48},{64,56},{72,6... | collective-permute-start | bytes 2120 | tf_op jit(solution)/shard_map/ppermute | solution.py:21
  109.7 4.8 %scatter_custom_fusion = f32[11,8192]{0,1:T(8,128)} fusion(f32[11,8192]{0,1:T(8,128)} %broadcast_multiply_fusion.2, s32[32]{0:T(128)S(1)} %fusion.73, f32[32,11]{1,0:T(8,128)S(1)} %gather_fusion, f32[32]{0:T(128)S(1)} %copy-done.16, f32[]{:T(128)} %constant.281.clone.1, pred[32]{0:T(512)(128)(4,1)S(1)} %compare_and_fusion.1), kind=kCustom, calls=%fused_computation.135 | custom fusion | flops 704 | bytes 378368 | tf_op jit(solution)/shard_map/scatter | solution.py:198
  114.6 4.9 %scatter_custom_fusion.1 = f32[11,8192]{0,1:T(8,128)} fusion(f32[11,8192]{0,1:T(8,128)} %scatter_custom_fusion, s32[16]{0:T(128)} %get-tuple-element.337, f32[11,16]{0,1:T(8,128)S(1)} %collective-permute-done.6), kind=kCustom, calls=%fused_computation.149 | custom fusion | bytes 361152 | tf_op jit(solution)/shard_map/scatter | solution.py:205
  119.4 4.9 %scatter_custom_fusion.2 = f32[11,8192]{0,1:T(8,128)} fusion(f32[11,8192]{0,1:T(8,128)} %scatter_custom_fusion.1, s32[16]{0:T(128)} %get-tuple-element.336, f32[11,16]{0,1:T(8,128)S(1)} %collective-permute-done.7), kind=kCustom, calls=%fused_computation.147 | custom fusion | bytes 361152 | tf_op jit(solution)/shard_map/scatter | solution.py:205
  124.3 3.5 %copy.47 = f32[11,2,32,128]{3,2,1,0:T(8,128)} copy(f32[11,2,32,128]{0,3,2,1:T(8,128)} %bitcast.218) | data formatting | bytes 720896 | tf_op jit(solution)/shard_map/reshape | solution.py:206
  (168 shorter events, 14.3 us)
Async XLA Ops:
  0.0 32.1 %copy-start.4 = (s32[2,2,32,128]{3,2,1,0:T(8,128)S(1)}, s32[2,2,32,128]{3,2,1,0:T(8,128)}, u32[]{:S(2)}) copy-start(s32[2,2,32,128]{3,2,1,0:T(8,128)} %param.20) | copy-start | bytes 196612
  1.1 17.1 %collective-permute-start = (f32[11,1,32,128]{3,0,2,1:T(8,128)S(1)}, f32[11,1,32,128]{3,0,2,1:T(8,128)S(1)}, u32[]{:S(2)}, u32[]{:S(2)}) collective-permute-start(f32[11,1,32,128]{3,0,2,1:T(8,128)S(1)} %copy.80), channel_id=1, source_target_pairs={{8,0},{16,8},{24,16},{32,24},{40,32},{48,40},{56,48},{64,56},{72,6... | collective-permute-start | bytes 540680 | tf_op jit(solution)/shard_map/ppermute | solution.py:21
  16.3 8.9 %copy-start.11 = (s32[2,1,16]{2,1,0:T(1,128)}, s32[2,1,16]{2,1,0:T(1,128)S(1)}, u32[]{:S(2)}) copy-start(s32[2,1,16]{2,1,0:T(1,128)S(1)} %get-tuple-element.302) | copy-start | bytes 388
  18.2 7.6 %collective-permute-start.2 = (f32[11,3,1,128]{3,0,2,1:T(8,128)S(1)}, f32[11,3,1,128]{3,0,2,1:T(8,128)S(1)}, u32[]{:S(2)}, u32[]{:S(2)}) collective-permute-start(f32[11,3,1,128]{3,0,2,1:T(8,128)S(1)} %get-tuple-element.328), channel_id=1, source_target_pairs={{1,0},{2,1},{3,2},{4,3},{5,4},{6,5},{7,6},{9,8},{10,9},{11,10},{12... | collective-permute-start | bytes 50696 | tf_op jit(solution)/shard_map/ppermute | solution.py:32
  22.8 9.2 %collective-permute-start.1 = (f32[11,3,1,128]{3,0,2,1:T(8,128)S(1)}, f32[11,3,1,128]{3,0,2,1:T(8,128)S(1)}, u32[]{:S(2)}, u32[]{:S(2)}) collective-permute-start(f32[11,3,1,128]{3,0,2,1:T(8,128)S(1)} %get-tuple-element.327), channel_id=1, source_target_pairs={{0,1},{1,2},{2,3},{3,4},{4,5},{5,6},{6,7},{8,9},{9,10},{10,11},{11... | collective-permute-start | bytes 50696 | tf_op jit(solution)/shard_map/ppermute | solution.py:29
  32.1 2.6 %copy-start.18 = (s32[2]{0:T(128)}, s32[2]{0:T(128)S(1)}, u32[]{:S(2)}) copy-start(s32[2]{0:T(128)S(1)} %get-tuple-element.506) | copy-start | bytes 28 | tf_op jit(solution)/shard_map/while
  34.6 1.4 %copy-start.5 = (s32[32,128]{1,0:T(8,128)}, s32[32,128]{1,0:T(8,128)S(1)}, u32[]{:S(2)}) copy-start(s32[32,128]{1,0:T(8,128)S(1)} %dynamic-slice_bitcast_fusion.2) | copy-start | bytes 49156 | tf_op jit(solution)/shard_map/while
  39.8 3.2 %copy-start.7 = (f32[2,32,128]{2,0,1:T(2,128)S(1)}, f32[2,32,128]{2,0,1:T(2,128)}, u32[]{:S(2)}) copy-start(f32[2,32,128]{2,0,1:T(2,128)} %get-tuple-element.508) | copy-start | bytes 98308 | tf_op jit(solution)/shard_map/while
  43.4 2.2 %copy-start.6 = (s32[32,128]{1,0:T(8,128)S(1)}, s32[32,128]{1,0:T(8,128)}, u32[]{:S(2)}) copy-start(s32[32,128]{1,0:T(8,128)} %copy-done.5) | copy-start | bytes 49156 | tf_op jit(solution)/shard_map/while
  45.5 2.0 %copy-start.1 = (f32[2,7,32,128]{3,2,0,1:T(8,128)S(1)}, f32[2,7,32,128]{3,2,0,1:T(8,128)}, u32[]{:S(2)}) copy-start(f32[2,7,32,128]{3,2,0,1:T(8,128)} %get-tuple-element.488) | copy-start | bytes 688132 | tf_op jit(solution)/shard_map/while
  45.5 2.8 %copy-start.19 = (s32[2]{0:T(128)S(1)}, s32[2]{0:T(128)}, u32[]{:S(2)}) copy-start(s32[2]{0:T(128)} %copy-done.18) | copy-start | bytes 28 | tf_op jit(solution)/shard_map/while
  48.3 2.6 %copy-start.18 = (s32[2]{0:T(128)}, s32[2]{0:T(128)S(1)}, u32[]{:S(2)}) copy-start(s32[2]{0:T(128)S(1)} %get-tuple-element.506) | copy-start | bytes 28 | tf_op jit(solution)/shard_map/while
  56.0 3.2 %copy-start.7 = (f32[2,32,128]{2,0,1:T(2,128)S(1)}, f32[2,32,128]{2,0,1:T(2,128)}, u32[]{:S(2)}) copy-start(f32[2,32,128]{2,0,1:T(2,128)} %get-tuple-element.508) | copy-start | bytes 98308 | tf_op jit(solution)/shard_map/while
  59.6 2.2 %copy-start.6 = (s32[32,128]{1,0:T(8,128)S(1)}, s32[32,128]{1,0:T(8,128)}, u32[]{:S(2)}) copy-start(s32[32,128]{1,0:T(8,128)} %copy-done.5) | copy-start | bytes 49156 | tf_op jit(solution)/shard_map/while
  61.7 2.0 %copy-start.1 = (f32[2,7,32,128]{3,2,0,1:T(8,128)S(1)}, f32[2,7,32,128]{3,2,0,1:T(8,128)}, u32[]{:S(2)}) copy-start(f32[2,7,32,128]{3,2,0,1:T(8,128)} %get-tuple-element.488) | copy-start | bytes 688132 | tf_op jit(solution)/shard_map/while
  61.7 2.8 %copy-start.19 = (s32[2]{0:T(128)S(1)}, s32[2]{0:T(128)}, u32[]{:S(2)}) copy-start(s32[2]{0:T(128)} %copy-done.18) | copy-start | bytes 28 | tf_op jit(solution)/shard_map/while
  64.5 6.6 %copy-start.3 = (f32[2,7,32,128]{3,2,0,1:T(8,128)S(1)}, f32[2,7,32,128]{3,2,0,1:T(8,128)}, u32[]{:S(2)}) copy-start(f32[2,7,32,128]{3,2,0,1:T(8,128)} %get-tuple-element.217) | copy-start | bytes 688132
  65.4 14.2 %copy-start.17 = (s32[32,1]{0,1:T(1,128)S(1)}, s32[32,1]{0,1:T(1,128)}, u32[]{:S(2)}) copy-start(s32[32,1]{0,1:T(1,128)} %add.294) | copy-start | bytes 388
  65.4 14.2 %copy-start.12 = (s32[2,1,16]{2,1,0:T(1,128)S(1)}, s32[2,1,16]{2,1,0:T(1,128)}, u32[]{:S(2)}) copy-start(s32[2,1,16]{2,1,0:T(1,128)} %copy-done.11) | copy-start | bytes 388
  65.4 23.2 %copy-start = (f32[11,2,32,128]{3,2,1,0:T(8,128)S(1)}, f32[11,2,32,128]{3,2,1,0:T(8,128)}, u32[]{:S(2)}) copy-start(f32[11,2,32,128]{3,2,1,0:T(8,128)} %param.18) | copy-start | bytes 1081348
  65.4 23.2 %copy-start.9 = (s32[2,32]{1,0:T(2,128)S(1)}, s32[2,32]{1,0:T(2,128)}, u32[]{:S(2)}) copy-start(s32[2,32]{1,0:T(2,128)} %param.19) | copy-start | bytes 772
  65.4 5.6 %collective-permute-start.3 = (f32[7,3,1,128]{3,2,1,0:T(1,128)S(1)}, f32[7,3,1,128]{3,2,1,0:T(1,128)S(1)}, u32[]{:S(2)}, u32[]{:S(2)}) collective-permute-start(f32[7,3,1,128]{3,2,1,0:T(1,128)S(1)} %get-tuple-element.326), channel_id=1, source_target_pairs={{1,0},{2,1},{3,2},{4,3},{5,4},{6,5},{7,6},{9,8},{10,9},{11,10},{12... | collective-permute-start | bytes 32264 | tf_op jit(solution)/shard_map/ppermute | solution.py:21
  68.6 8.9 %collective-permute-start.4 = (f32[7,3,1,128]{3,2,1,0:T(1,128)S(1)}, f32[7,3,1,128]{3,2,1,0:T(1,128)S(1)}, u32[]{:S(2)}, u32[]{:S(2)}) collective-permute-start(f32[7,3,1,128]{3,2,1,0:T(1,128)S(1)} %get-tuple-element.325), channel_id=1, source_target_pairs={{0,1},{1,2},{2,3},{3,4},{4,5},{5,6},{6,7},{8,9},{9,10},{10,11},{11... | collective-permute-start | bytes 32264 | tf_op jit(solution)/shard_map/ppermute | solution.py:21
  77.7 10.9 %collective-permute-start.5 = (f32[7,1,32,128]{3,2,1,0:T(8,128)S(1)}, f32[7,1,32,128]{3,2,1,0:T(8,128)S(1)}, u32[]{:S(2)}, u32[]{:S(2)}) collective-permute-start(f32[7,1,32,128]{3,2,1,0:T(8,128)S(1)} %slice.477), channel_id=1, source_target_pairs={{0,8},{8,16},{16,24},{24,32},{32,40},{40,48},{48,56},{56,64},{64,7... | collective-permute-start | bytes 344072 | tf_op jit(solution)/shard_map/ppermute | solution.py:21
  89.7 2.7 %copy-start.8 = (f32[2,32,128]{2,1,0:T(8,128)S(1)}, f32[2,32,128]{2,1,0:T(8,128)}, u32[]{:S(2)}) copy-start(f32[2,32,128]{2,1,0:T(8,128)} %fusion.60) | copy-start | bytes 98308
  92.4 7.0 %copy-start.10 = (f32[2,16]{1,0:T(2,128)S(1)}, f32[2,16]{1,0:T(2,128)}, u32[]{:S(2)}) copy-start(f32[2,16]{1,0:T(2,128)} %get-tuple-element.340) | copy-start | bytes 388
  92.4 7.0 %copy-start.14 = (pred[2,16]{1,0:T(4,128)(4,1)S(1)}, pred[2,16]{1,0:T(4,128)(4,1)}, u32[]{:S(2)}) copy-start(pred[2,16]{1,0:T(4,128)(4,1)} %get-tuple-element.341) | copy-start | bytes 100
  92.4 7.1 %copy-start.13 = (s32[2,1,1]{0,2,1:T(1,128)S(1)}, s32[2,1,1]{0,2,1:T(1,128)}, u32[]{:S(2)}) copy-start(s32[2,1,1]{0,2,1:T(1,128)} %param.24) | copy-start | bytes 28
  92.4 7.1 %copy-start.15 = (f32[2]{0:T(128)S(1)}, f32[2]{0:T(128)}, u32[]{:S(2)}) copy-start(f32[2]{0:T(128)} %constant.282.clone) | copy-start | bytes 28
  92.4 17.3 %copy-start.16 = (f32[32]{0:T(128)S(1)}, f32[32]{0:T(128)}, u32[]{:S(2)}) copy-start(f32[32]{0:T(128)} %fusion.72) | copy-start | bytes 388
  99.6 14.9 %collective-permute-start.6 = (f32[11,16]{0,1:T(8,128)S(1)}, f32[11,16]{0,1:T(8,128)S(1)}, u32[]{:S(2)}, u32[]{:S(2)}) collective-permute-start(f32[11,16]{0,1:T(8,128)S(1)} %get-tuple-element.335), channel_id=1, source_target_pairs={{0,8},{8,16},{16,24},{24,32},{32,40},{40,48},{48,56},{56,64},{64,7... | collective-permute-start | bytes 2120 | tf_op jit(solution)/shard_map/ppermute | solution.py:21
  101.5 17.9 %collective-permute-start.7 = (f32[11,16]{0,1:T(8,128)S(1)}, f32[11,16]{0,1:T(8,128)S(1)}, u32[]{:S(2)}, u32[]{:S(2)}) collective-permute-start(f32[11,16]{0,1:T(8,128)S(1)} %get-tuple-element.334), channel_id=1, source_target_pairs={{8,0},{16,8},{24,16},{32,24},{40,32},{48,40},{56,48},{64,56},{72,6... | collective-permute-start | bytes 2120 | tf_op jit(solution)/shard_map/ppermute | solution.py:21
  (3 other events, 2.7 us)
where the time goes:
time: 129 us; the launch traced here: 128 us
  starting transfers between devices  30.5 us (24%)
  local copies, waits for them, and re-layouts  28.4 us (22%)
  waiting for transfers between devices  21.4 us (17%)
  other arithmetic  20 us (16%)
  matrix products  17.5 us (14%)
  loops' own time  9.58 us (7%)
    ppermute x6, starting transfers between devices, passed_along(): return lax.ppermute(block, axis, route)  24 us
    ppermute x6, waiting for transfers between devices, passed_along(): return lax.ppermute(block, axis, route)  15.2 us
    scatter x2, local copies, waits for them, and re-layouts, body(): flattened.at[:, targets[0]].set(from_behind).at[:, targets[1]]  9.71 us
    another operation x1, loops' own time, accumulate(): lax.scan(row_pass, jnp.zeros((), jnp.float32), jnp.arange(region_rows, dt...  9.58 us
    ppermute x1, waiting for transfers between devices, extended(): lax.ppermute(lax.slice_in_dim(block, block.shape[dim] - width, None, axis...  6.15 us
    dot_general x2, matrix products, row_pass(): jnp.einsum('cgds,gks->cgdk', neighbours, far_hot, precision=highest)  4.95 us
    scatter x1, other arithmetic, body(): flattened.at[:, sources_at.reshape(-1)]  4.84 us
    dot_general x2, matrix products, row_pass(): jnp.einsum('cgs,gks->cgk', neighbours[:, :, 0], own_hot, precision=highest)  4.76 us
  transfers between devices with their start and end apart: 8, of which 3 were waited for; matrix products, arithmetic and copies ran while one was open for 17% of the time, Pallas kernels for 0%

commit v1 on v0

v1 whole, which is shorter than its diff:
```python
import functools

import jax
import jax.numpy as jnp
from jax import lax
from jax.experimental import pallas as pl
from jax.experimental.pallas import tpu as pltpu
from jax.sharding import PartitionSpec as P

spring = 4.0
normal_damp = 0.5
tangent_damp = 0.3
conduct = 40.0
timestep = 0.05
density = 100.0
gravity = 9.81
soft_len = 0.05

COMPS = 11
LANES = 128
LIVE = 96
COLS = 32
SLAB = 40
EXT = 56
BASE = 8
SOURCES = 34
row_steps = (0, 1, 0, 1, 1)
col_steps = (0, 0, 1, 1, -1)


def iota(shape, dim):
    return lax.broadcasted_iota(jnp.int32, shape, dim)


def pick(values, index):
    return jnp.take_along_axis(values, index, axis=1, mode="promise_in_bounds")


def to_column(row, size):
    n = row.shape[1]
    spread = jnp.where(iota((size, n), 0) == iota((size, n), 1), row, 0)
    return jnp.sum(spread, axis=1, keepdims=True)


def cross(a, b):
    return (
        a[1] * b[2] - a[2] * b[1],
        a[2] * b[0] - a[0] * b[2],
        a[0] * b[1] - a[1] * b[0],
    )


def pair_terms(first, second, row_shift, col_shift, listed):
    gap = (second[0] + row_shift - first[0], second[1] + col_shift - first[1], second[2] - first[2])
    dist = jnp.sqrt(gap[0] * gap[0] + gap[1] * gap[1] + gap[2] * gap[2] + soft_len * soft_len)
    inverse = 1.0 / dist
    n = tuple(g * inverse for g in gap)
    r1, r2 = first[9], second[9]
    intersection = r1 + r2 - dist
    spin = tuple(r1 * first[6 + i] + r2 * second[6 + i] for i in range(3))
    turn = cross(spin, n)
    w = tuple(second[3 + i] - first[3 + i] - turn[i] for i in range(3))
    u = w[0] * n[0] + w[1] * n[1] + w[2] * n[2]
    fric = tuple(tangent_damp * (w[i] - u * n[i]) for i in range(3))
    push = normal_damp * u - spring * intersection
    force = tuple(push * n[i] + fric[i] for i in range(3))
    torque = cross(n, fric)
    denom = jnp.where(listed, r1 + r2, 1.0)
    heat = 2.0 * conduct * r1 * r2 / denom * (second[10] - first[10])
    on_first = [*force, *(r1 * t for t in torque), heat]
    on_second = [*(-f for f in force), *(r2 * t for t in torque), -heat]
    return (
        [jnp.where(listed, t, 0.0) for t in on_first],
        [jnp.where(listed, t, 0.0) for t in on_second],
    )


def stepped(state, totals, live):
    r = state[9] + jnp.where(live, 0.0, 1.0)
    mass = density * r * r * r
    per_mass = timestep / mass
    per_inertia = timestep / (0.4 * mass * r * r)
    v = [state[3] + per_mass * totals[0], state[4] + per_mass * totals[1]]
    v.append(state[5] + per_mass * totals[2] - timestep * gravity)
    spin = [state[6 + i] + per_inertia * totals[3 + i] for i in range(3)]
    x = [state[i] + timestep * v[i] for i in range(3)]
    warmth = state[10] + per_mass * totals[6]
    return [jnp.where(live, t, 0.0) for t in [*x, *v, *spin, state[9], warmth]]


def second_states(ext, row, heading, target, headings):
    out = []
    for j in range(COMPS):
        value = None
        for d in headings:
            where = BASE + col_steps[d]
            got = pick(ext[j, row + row_steps[d], where : where + SLAB, :], target)
            value = got if value is None else jnp.where(heading == d, got, value)
        out.append(value)
    return out


def shifts(heading):
    row_shift = jnp.where((heading == 0) | (heading == 2), 0.0, 1.0)
    col_shift = jnp.where(
        (heading == 2) | (heading == 3), 1.0, jnp.where(heading == 4, -1.0, 0.0)
    )
    return row_shift, col_shift


def keep(ref, base, terms):
    for j in range(7):
        ref[base + j * SLAB : base + (j + 1) * SLAB, :] = terms[j]
    ref[base + 7 * SLAB : base + 8 * SLAB, :] = jnp.zeros((SLAB, LANES), jnp.float32)


def halves(x):
    high = x.astype(jnp.bfloat16).astype(jnp.float32)
    return jnp.concatenate([high, x - high], 0).astype(jnp.bfloat16)


def one_hot(index_row):
    hot = iota((LANES, LANES), 0) == index_row
    return jnp.where(hot, 1.0, 0.0).astype(jnp.bfloat16)


def spread(left, right):
    out = lax.dot_general(
        halves(left), right, (((1,), (1,)), ((), ())), preferred_element_type=jnp.float32
    )
    rows = left.shape[0]
    return out[:rows] + out[rows:]


def add_tile(totals, row, col, tile):
    at = pl.ds(pl.multiple_of((row * SLAB + col + 1) * 8, 8), 8)
    totals[at, :] += tile


def pack_columns(west_p, east_p, west_c, east_c, count, near, far):
    odd = lax.rem(lax.axis_index("span"), 2) == 1
    lane = iota((1, LANES), 1)
    near[...] = jnp.zeros(near.shape, jnp.float32)
    far[...] = jnp.zeros(far.shape, jnp.float32)
    for r in range(2):
        for j in range(COMPS):
            sides = []
            for p, c, at, cell in ((west_p, west_c, 0, 0), (east_p, east_c, 7, COLS - 1)):
                value = p[j, r, at : at + 1, :]
                if j < 8:
                    extra = c[j // 4, r, at : at + 1, :].astype(jnp.float32)
                    if j % 4 != 3:
                        extra = pltpu.roll(extra, LIVE - 32 * (j % 4), 1)
                    value = jnp.where(lane < LIVE, value, extra)
                elif j == 8:
                    here = jnp.where(iota((1, COLS), 1) == cell, count[r : r + 1, :], 0)
                    here = jnp.sum(here, axis=1, keepdims=True).astype(jnp.float32)
                    value = jnp.where(lane < LIVE, value, here)
                sides.append(value)
            west, east = sides
            row = r * 12 + j
            near[row : row + 1, :] = jnp.where(odd, west, east)
            far[row : row + 1, :] = jnp.where(odd, east, west)


def leavers(movers, counts, direction):
    cells = lax.rem(movers[direction, 0], COLS)
    slots = movers[direction, 1]
    n = cells.shape[1]
    number = iota((SLAB, n), 1)
    here = (iota((SLAB, n), 0) - 1 == cells) & (number < counts[direction, 0, 0])
    slot = jnp.sum(jnp.where(here, slots + 1, 0), axis=1, keepdims=True)
    which = jnp.sum(jnp.where(here, number, 0), axis=1, keepdims=True)
    return slot, which


def unpacked_lists(rows):
    lane = iota(rows[0].shape, 1)
    lists = []
    for half in range(2):
        value = rows[half * 4 + 3]
        for k in range(3):
            moved = pltpu.roll(rows[half * 4 + k], 32 * k + 32, 1)
            value = jnp.where(lane // 32 == k, moved, value)
        lists.append(value.astype(jnp.int32))
    return lists


def own_rows(
    particles, pairs, count, near, far, movers, counts, ext, lists, totals, to_near, to_far, on_first, on_second
):
    odd = lax.rem(lax.axis_index("span"), 2) == 1
    zeros = jnp.zeros((8, LANES), jnp.float32)
    for r in range(2):
        for j in range(COMPS):
            ext[j, r, 0:8, :] = zeros
            ext[j, r, 40:48, :] = zeros
            ext[j, r, 48:56, :] = zeros
            ext[j, r, 9:41, :] = particles[j, r]
            at = slice(r * 12 + j, r * 12 + j + 1)
            ext[j, r, 8:9, :] = jnp.where(odd, near[at, :], far[at, :])
            ext[j, r, 41:42, :] = jnp.where(odd, far[at, :], near[at, :])
    sides = jnp.where(odd, near[...], far[...]), jnp.where(odd, far[...], near[...])
    for r in range(2):
        lists[0, r, 32:40, :] = jnp.zeros((8, LANES), jnp.int32)
        lists[1, r, 32:40, :] = jnp.zeros((8, LANES), jnp.int32)
        lists[2, r, 32:40, :] = jnp.zeros((8, LANES), jnp.int32)
        lists[0, r, 1:33, :] = pairs[0, r]
        lists[1, r, 1:33, :] = pairs[1, r]
        lists[2, r, 1:33, :] = jnp.broadcast_to(to_column(count[r : r + 1, :], COLS), (COLS, LANES))
        for side, at in zip(sides, (0, 33)):
            rows = [side[r * 12 + j : r * 12 + j + 1, :] for j in range(9)]
            first, second = unpacked_lists(rows[:8])
            lists[0, r, at : at + 1, :] = first
            lists[1, r, at : at + 1, :] = second
            lists[2, r, at : at + 1, :] = jnp.broadcast_to(rows[8][:, LIVE : LIVE + 1], (1, LANES)).astype(jnp.int32)
    totals[...] = jnp.zeros(totals.shape, jnp.float32)
    for r in range(2):
        headings = (0, 1, 2, 3, 4) if r == 0 else (0, 2)
        first_index = lists[0, r]
        heading = lists[1, r] // LANES
        target = lax.rem(lists[1, r], LANES)
        listed = iota((SLAB, LANES), 1) < lists[2, r]
        if r == 1:
            listed = listed & ((heading == 0) | (heading == 2))
        first = [pick(ext[j, r, BASE : BASE + SLAB, :], first_index) for j in range(COMPS)]
        second = second_states(ext, r, heading, target, headings)
        row_shift, col_shift = shifts(heading)
        f, s = pair_terms(first, second, row_shift, col_shift, listed)
        keep(on_first, r * 8 * SLAB, f)
        keep(on_second, r * 8 * SLAB, s)

    for r in range(2):
        headings = (0, 1, 2, 3, 4) if r == 0 else (0, 2)

        def source(c, _, r=r, headings=headings):
            f = on_first[pl.ds(r * 8 * SLAB + c, 8, stride=SLAB), :]
            s = on_second[pl.ds(r * 8 * SLAB + c, 8, stride=SLAB), :]
            first_row = lists[0, r, pl.ds(c, 1), :]
            second_row = lists[1, r, pl.ds(c, 1), :]
            heading = second_row // LANES
            target = lax.rem(second_row, LANES)
            hot = jnp.concatenate([one_hot(first_row), one_hot(target)], 1)
            blank = jnp.zeros((8, LANES), jnp.float32)
            left = jnp.concatenate(
                [jnp.concatenate([f if d == 0 else blank, jnp.where(heading == d, s, 0.0)], 1) for d in headings],
                0,
            )
            out = spread(left, hot)
            for at, d in enumerate(headings):
                add_tile(totals, r + row_steps[d], c + col_steps[d], out[at * 8 : at * 8 + 8])
            return 0

        lax.fori_loop(0, SOURCES, source, 0, unroll=2)

    turn = lax.rem(lax.axis_index("blade"), 2)
    lane = iota((SLAB, LANES), 1)
    for out, row in ((to_near, 1 - turn), (to_far, turn)):
        slots0, which0 = leavers(movers, counts, 1)
        slots1, which1 = leavers(movers, counts, 0)
        slot = jnp.where(row == 1, slots1, slots0)
        which = jnp.where(row == 1, which1, which0)
        at_slot = jnp.broadcast_to(jnp.maximum(slot - 1, 0), (SLAB, LANES))
        info = jnp.where(lane == LIVE + 7, slot.astype(jnp.float32), which.astype(jnp.float32))
        for j in range(7):
            part = totals[pl.ds((row * SLAB + 1) * 8 + j, SLAB - 2, stride=8), :]
            part = jnp.concatenate([part, jnp.zeros((2, LANES), jnp.float32)], 0)
            info = jnp.where(lane == LIVE + j, pick(part, at_slot), info)
        for j in range(COMPS):
            value = ext[j, row, BASE : BASE + SLAB, :]
            if j < 8:
                extra = lists[j // 4, row].astype(jnp.float32)
                if j % 4 != 3:
                    extra = pltpu.roll(extra, LIVE - 32 * (j % 4), 1)
            elif j == 8:
                extra = lists[2, row].astype(jnp.float32)
            else:
                extra = info
            out[j] = jnp.where(lane < LIVE, value, extra)


def across_rows(
    ext, lists, partial, near, far, filled, movers, counts, arrivals, out, around, totals, on_first, on_second
):
    turn = lax.rem(lax.axis_index("blade"), 2) == 1
    zeros = jnp.zeros((8, LANES), jnp.float32)
    for j in range(COMPS):
        around[0, j, 0:8, :] = zeros
        around[0, j, 48:56, :] = zeros
        around[1, j, 0:8, :] = zeros
        around[1, j, 48:56, :] = zeros
        around[0, j, 8:48, :] = jnp.where(turn, near[j], far[j])
        around[1, j, 8:48, :] = jnp.where(turn, far[j], near[j])
    totals[...] = partial[...]
    lane = iota((SLAB, LANES), 1)

    def behind(j, shift=0):
        return around[0, j, BASE + shift : BASE + shift + SLAB, :]

    def ahead(j, shift=0):
        return around[1, j, BASE + shift : BASE + shift + SLAB, :]

    first_list, second_list = unpacked_lists([behind(j) for j in range(8)])
    count_behind = behind(8)[:, LIVE : LIVE + 1].astype(jnp.int32)
    sources = (
        (behind, lambda j, k: ext[j, 0, BASE + k : BASE + k + SLAB, :], first_list, second_list, count_behind),
        (lambda j: ext[j, 1, BASE : BASE + SLAB, :], ahead, lists[0, 1], lists[1, 1], lists[2, 1]),
    )
    kept = []
    for r, (mine, others, firsts, seconds, count) in enumerate(sources):
        heading = seconds // LANES
        target = lax.rem(seconds, LANES)
        listed = (lane < count) & ((heading == 1) | (heading == 3) | (heading == 4))
        first = [pick(mine(j), firsts) for j in range(COMPS)]
        second = []
        for j in range(COMPS):
            value = pick(others(j, 0), target)
            for d in (3, 4):
                value = jnp.where(heading == d, pick(others(j, col_steps[d]), target), value)
            second.append(value)
        _, col_shift = shifts(heading)
        f, s = pair_terms(first, second, 1.0, col_shift, listed)
        keep(on_first, r * 8 * SLAB, f)
        keep(on_second, r * 8 * SLAB, s)
        kept.append((firsts, heading, target))

    spare = 16 * SLAB
    on_first[spare : spare + SLAB, :] = kept[0][1].astype(jnp.float32)
    on_first[spare + SLAB : spare + 2 * SLAB, :] = kept[0][2].astype(jnp.float32)

    def source(c, _):
        f = on_first[pl.ds(8 * SLAB + c, 8, stride=SLAB), :]
        s = on_second[pl.ds(c, 8, stride=SLAB), :]
        heading = on_first[pl.ds(spare + c, 1), :].astype(jnp.int32)
        target = on_first[pl.ds(spare + SLAB + c, 1), :].astype(jnp.int32)
        first_row = lists[0, 1, pl.ds(c, 1), :]
        hot = jnp.concatenate([one_hot(first_row), one_hot(target)], 1)
        blank = jnp.zeros((8, LANES), jnp.float32)
        left = jnp.concatenate(
            [jnp.concatenate([f, blank], 1)]
            + [jnp.concatenate([blank, jnp.where(heading == d, s, 0.0)], 1) for d in (1, 3, 4)],
            0,
        )
        got = spread(left, hot)
        add_tile(totals, 1, c, got[0:8])
        for at, d in enumerate((1, 3, 4)):
            add_tile(totals, 0, c + col_steps[d], got[8 + at * 8 : 16 + at * 8])
        return 0

    lax.fori_loop(0, SOURCES, source, 0, unroll=2)

    placed = []
    for side in range(2):
        state_of = behind if side == 0 else ahead
        info = state_of(9)
        slot = info[:, LIVE + 7 : LIVE + 8].astype(jnp.int32)
        which = info[:, LIVE + 8 : LIVE + 9].astype(jnp.int32)
        leaves = slot > 0
        at_slot = jnp.broadcast_to(jnp.maximum(slot - 1, 0), (SLAB, LANES))
        leaving_totals = []
        if side == 0:
            hit = kept[0][0] == slot - 1
            for j in range(7):
                term = jnp.where(hit, on_first[j * SLAB : (j + 1) * SLAB, :], 0.0)
                leaving_totals.append(jnp.sum(term, axis=1, keepdims=True))
        else:
            heading, target = kept[1][1], kept[1][2]
            masks = {}
            for d in (1, 3, 4):
                there = pltpu.roll(slot.astype(jnp.int32) + jnp.zeros((SLAB, LANES), jnp.int32), (-col_steps[d]) % SLAB, 0)
                masks[d] = (heading == d) & (target == there - 1)
            for j in range(7):
                term = on_second[(8 + j) * SLAB : (9 + j) * SLAB, :]
                total = jnp.where(masks[1], term, 0.0)
                total = total + pltpu.roll(jnp.where(masks[3], term, 0.0), 1, 0)
                total = total + pltpu.roll(jnp.where(masks[4], term, 0.0), SLAB - 1, 0)
                leaving_totals.append(jnp.sum(total, axis=1, keepdims=True))
        leaving_totals = [t + info[:, LIVE + j : LIVE + j + 1] for j, t in enumerate(leaving_totals)]
        state = [pick(state_of(j), at_slot) for j in range(COMPS)]
        moved = stepped(state, leaving_totals, leaves)
        moved[0] = moved[0] + (-1.0 if side == 0 else 1.0)
        cells = to_column(lax.rem(arrivals[side, 0], COLS), 16)
        slots = to_column(arrivals[side, 1], 16)
        hit = slots == iota((16, LANES), 1)
        number = jnp.sum(jnp.where(hit, iota((16, LANES), 0) + 1, 0), axis=0, keepdims=True) - 1
        cell = jnp.sum(jnp.where(hit, cells, 0), axis=0, keepdims=True)
        cell = jnp.where(number >= 0, cell, -1)
        match = (which == number) & leaves
        values = [jnp.sum(jnp.where(match, m, 0.0), axis=0, keepdims=True) for m in moved]
        placed.append((cell, values))

    column = iota((COLS, LANES), 0)
    lane = iota((COLS, LANES), 1)
    for r in range(2):
        slot, _ = leavers(movers, counts, 1 - r)
        slot = slot[1 : 1 + COLS]
        live = lane < to_column(filled[r : r + 1, :], COLS)
        state = [ext[j, r, 9:41, :] for j in range(COMPS)]
        sums = [totals[pl.ds((r * SLAB + 2) * 8 + j, COLS, stride=8), :] for j in range(7)]
        rows = stepped(state, sums, live)
        stay = lane != slot - 1
        cell, values = placed[r]
        lands = column == cell
        for j in range(COMPS):
            out[j, r] = jnp.where(lands, values[j], jnp.where(stay, rows[j], 0.0))


def swapped(block, axis, start):
    pairs = []
    for i in range(start, lax.axis_size(axis) - 1, 2):
        pairs += [(i, i + 1), (i + 1, i)]
    return lax.ppermute(block, axis, pairs)


vmem = functools.partial(pl.BlockSpec, memory_space=pltpu.VMEM)
smem = functools.partial(pl.BlockSpec, memory_space=pltpu.SMEM)
params = pltpu.CompilerParams(vmem_limit_bytes=24 * 1024 * 1024)


def shape(*dims, dtype=jnp.float32):
    return jax.ShapeDtypeStruct(dims, dtype)


def body(particles, filled, contact_pairs, contact_count, movers_out, movers_in, move_count):
    columns = pl.pallas_call(
        pack_columns,
        grid=(1,),
        in_specs=[
            pl.BlockSpec((COMPS, 2, 8, LANES), lambda i: (0, 0, 0, 0)),
            pl.BlockSpec((COMPS, 2, 8, LANES), lambda i: (0, 0, 3, 0)),
            pl.BlockSpec((2, 2, 8, LANES), lambda i: (0, 0, 0, 0)),
            pl.BlockSpec((2, 2, 8, LANES), lambda i: (0, 0, 3, 0)),
            pl.BlockSpec((2, COLS), lambda i: (0, 0)),
        ],
        out_specs=[pl.BlockSpec((24, LANES), lambda i: (0, 0))] * 2,
        out_shape=[shape(24, LANES)] * 2,
        compiler_params=params,
        name="pack_columns",
    )
    near, far = columns(particles, particles, contact_pairs, contact_pairs, contact_count)
    near = swapped(near, "span", 0)
    far = swapped(far, "span", 1)
    ext, lists, partial, to_near, to_far = pl.pallas_call(
        own_rows,
        in_specs=[vmem()] * 6 + [smem()],
        out_specs=[vmem()] * 5,
        out_shape=[
            shape(COMPS, 2, EXT, LANES),
            shape(3, 2, SLAB, LANES, dtype=jnp.int32),
            shape(2 * SLAB * 8, LANES),
            shape(COMPS, SLAB, LANES),
            shape(COMPS, SLAB, LANES),
        ],
        scratch_shapes=[pltpu.VMEM((16 * SLAB, LANES), jnp.float32)] * 2,
        compiler_params=params,
        name="own_rows",
    )(particles, contact_pairs, contact_count, near, far, movers_out, move_count)
    near = swapped(to_near, "blade", 0)
    far = swapped(to_far, "blade", 1)
    return pl.pallas_call(
        across_rows,
        in_specs=[vmem()] * 7 + [smem()] + [vmem()],
        out_specs=vmem(),
        out_shape=shape(COMPS, 2, COLS, LANES),
        scratch_shapes=[
            pltpu.VMEM((2, COMPS, EXT, LANES), jnp.float32),
            pltpu.VMEM((2 * SLAB * 8, LANES), jnp.float32),
            pltpu.VMEM((18 * SLAB, LANES), jnp.float32),
            pltpu.VMEM((16 * SLAB, LANES), jnp.float32),
        ],
        compiler_params=params,
        name="across_rows",
    )(ext, lists, partial, near, far, filled, movers_out, move_count, movers_in)


def solution(mesh):
    return jax.shard_map(
        body,
        mesh=mesh,
        in_specs=(
            P(None, "blade", "span", None),
            P("blade", "span"),
            P(None, "blade", "span", None),
            P("blade", "span"),
            P(None, None, "blade", "span"),
            P(None, None, "blade", "span"),
            P(None, "blade", "span"),
        ),
        out_specs=P(None, "blade", "span", None),
        check_vma=False,
    )
```

time: 129 us -> 47.6 us (0.37)
  the two profiles are of different devices: /device:TPU:416 before, /device:TPU:161 now
where the time goes in v1:
time: 47.6 us; the launch traced here: 47.1 us
  starting transfers between devices  20.1 us (42%)
  Pallas kernels  15.7 us (33%)
  waiting for transfers between devices  7.87 us (17%)
  local copies, waits for them, and re-layouts  3.31 us (7%)
    ppermute x4, starting transfers between devices, swapped(): return lax.ppermute(block, axis, pairs)  20.1 us
    pallas_call x1, Pallas kernels, body(): pl.pallas_call(own_rows, in_specs=[vmem()] * 6 + [smem()], out_specs=[vme...  8.65 us
    ppermute x4, waiting for transfers between devices, swapped(): return lax.ppermute(block, axis, pairs)  7.87 us
    pallas_call x1, Pallas kernels, body(): pl.pallas_call(across_rows, in_specs=[vmem()] * 7 + [smem()] + [vmem()],...  6.91 us
    unnamed x21, local copies, waits for them, and re-layouts  3.31 us
  transfers between devices with their start and end apart: 4, of which 2 were waited for; matrix products, arithmetic and copies ran while one was open for 0% of the time, Pallas kernels for 0%

profile of v1, /device:TPU:161, one launch (start us, length us, event | category | flops | bytes accessed | tf_op | source)
XLA Modules:
  0.0 47.1 jit_solution(1454131603673009503)
XLA Ops:
  0.0 0.0 copy-start
  0.0 1.0 %copy-done = f32[11,2,32,128]{3,2,1,0:T(8,128)S(1)} copy-done((f32[11,2,32,128]{3,2,1,0:T(8,128)S(1)}, f32[11,2,32,128]{3,2,1,0:T(8,128)}, u32[]{:S(2)}) %copy-start) | copy-done | bytes 360472
  1.0 0.0 copy-start.2
  1.0 0.8 %copy-done.2 = s32[2,2,32,128]{3,2,1,0:T(8,128)S(1)} copy-done((s32[2,2,32,128]{3,2,1,0:T(8,128)S(1)}, s32[2,2,32,128]{3,2,1,0:T(8,128)}, u32[]{:S(2)}) %copy-start.2) | copy-done | bytes 65560
  1.8 0.0 copy-start.5
  1.8 0.7 %copy-done.5 = s32[2,32]{1,0:T(2,128)S(1)} copy-done((s32[2,32]{1,0:T(2,128)S(1)}, s32[2,32]{1,0:T(2,128)}, u32[]{:S(2)}) %copy-start.5) | copy-done | bytes 280
  2.5 0.0 copy-start.1
  2.5 0.0 copy-start.3
  2.5 0.1 pack_columns.1
  2.6 0.0 copy-start.9
  2.7 0.0 copy-start.4
  2.7 2.6 %collective-permute-start = (f32[24,128]{1,0:T(8,128)S(1)}, f32[24,128]{1,0:T(8,128)S(1)}, u32[]{:S(2)}, u32[]{:S(2)}) collective-permute-start(f32[24,128]{1,0:T(8,128)S(1)} %get-tuple-element.12), channel_id=1, source_target_pairs={{0,1},{1,0},{2,3},{3,2},{4,5},{5,4},{6,7},{7,6},{8,9},{9,8},{10,11... | collective-permute-start | bytes 36872 | tf_op jit(solution)/shard_map/ppermute | solution.py:412
  5.3 0.0 copy-start.6
  5.3 7.8 %collective-permute-start.1 = (f32[24,128]{1,0:T(8,128)S(1)}, f32[24,128]{1,0:T(8,128)S(1)}, u32[]{:S(2)}, u32[]{:S(2)}) collective-permute-start(f32[24,128]{1,0:T(8,128)S(1)} %get-tuple-element.13), channel_id=1, source_target_pairs={{1,2},{2,1},{3,4},{4,3},{5,6},{6,5},{9,10},{10,9},{11,12},{12,11},... | collective-permute-start | bytes 36872 | tf_op jit(solution)/shard_map/ppermute | solution.py:412
  13.1 0.0 copy-done.9
  13.1 0.1 copy.8.counts
  13.2 0.0 collective-permute-done.near
  13.2 1.3 %collective-permute-done.1.far = f32[24,128]{1,0:T(8,128)S(1)} collective-permute-done((f32[24,128]{1,0:T(8,128)S(1)}, f32[24,128]{1,0:T(8,128)S(1)}, u32[]{:S(2)}, u32[]{:S(2)}) %collective-permute-start.1) | collective-permute-done | bytes 12320 | tf_op jit(solution)/shard_map/ppermute | solution.py:412
  14.5 0.0 copy-done.1
  14.5 0.0 copy-done.3
  14.5 0.0 copy-done.4
  14.5 0.0 copy-done.6
  14.5 8.6 %own_rows.1 = (f32[11,2,56,128]{3,2,1,0:T(8,128)S(1)}, s32[3,2,40,128]{3,2,1,0:T(8,128)S(1)}, f32[640,128]{1,0:T(8,128)S(1)}, f32[11,40,128]{2,1,0:T(8,128)S(1)}, f32[11,40,128]{2,1,0:T(8,128)S(1)}) custom-call(f32[11,2,32,128]{3,2,1,0:T(8,128)S(1)} %copy-done.1, s32[2,2,32,128]{3,2,1,0:T(8,128)S(1)} %copy-done.3, s32[2,32]{1,0:T(2,128)S(1)} %copy-done.6, ...), custom_call_target="tpu_custom_call" | custom-call | tf_op jit(solution)/shard_map/own_rows/pallas_call | solution.py:443
  23.1 3.1 %collective-permute-start.2 = (f32[11,40,128]{2,1,0:T(8,128)S(1)}, f32[11,40,128]{2,1,0:T(8,128)S(1)}, u32[]{:S(2)}, u32[]{:S(2)}) collective-permute-start(f32[11,40,128]{2,1,0:T(8,128)S(1)} %get-tuple-element.17), channel_id=1, source_target_pairs={{0,8},{8,0},{16,24},{24,16},{32,40},{40,32},{48,56},{56,48},{64,72... | collective-permute-start | bytes 675848 | tf_op jit(solution)/shard_map/ppermute | solution.py:412
  26.3 6.6 %collective-permute-start.3 = (f32[11,40,128]{2,1,0:T(8,128)S(1)}, f32[11,40,128]{2,1,0:T(8,128)S(1)}, u32[]{:S(2)}, u32[]{:S(2)}) collective-permute-start(f32[11,40,128]{2,1,0:T(8,128)S(1)} %get-tuple-element.18), channel_id=1, source_target_pairs={{8,16},{16,8},{24,32},{32,24},{40,48},{48,40},{56,64},{64,56},{72,... | collective-permute-start | bytes 675848 | tf_op jit(solution)/shard_map/ppermute | solution.py:412
  32.9 0.0 collective-permute-done.2.near
  32.9 6.6 %collective-permute-done.3.far = f32[11,40,128]{2,1,0:T(8,128)S(1)} collective-permute-done((f32[11,40,128]{2,1,0:T(8,128)S(1)}, f32[11,40,128]{2,1,0:T(8,128)S(1)}, u32[]{:S(2)}, u32[]{:S(2)}) %collective-permute-start.3) | collective-permute-done | bytes 225312 | tf_op jit(solution)/shard_map/ppermute | solution.py:412
  39.5 0.0 copy-start.7
  39.5 0.0 copy-start.8
  39.5 0.7 %copy-done.7 = s32[2,2,1,16]{3,2,1,0:T(1,128)S(1)} copy-done((s32[2,2,1,16]{3,2,1,0:T(1,128)S(1)}, s32[2,2,1,16]{3,2,1,0:T(1,128)}, u32[]{:S(2)}) %copy-start.7) | copy-done | bytes 280
  40.2 0.0 copy-done.8
  40.2 6.9 %across_rows.1 = f32[11,2,32,128]{3,2,1,0:T(8,128)} custom-call(f32[11,2,56,128]{3,2,1,0:T(8,128)S(1)} %get-tuple-element.14.ext, s32[3,2,40,128]{3,2,1,0:T(8,128)S(1)} %get-tuple-element.15.lists, f32[640,128]{1,0:T(8,128)S(1)} %get-tuple-element.16.partial, f32[11,40,128]{2,1,0:T(8,128)S(1)} %collective-permute-done.2.near, ...), custom_call_target="tpu_custom_call" | custom-call | tf_op jit(solution)/shard_map/across_rows/pallas_call | solution.py:460
Async XLA Ops:
  0.0 1.0 %copy-start = (f32[11,2,32,128]{3,2,1,0:T(8,128)S(1)}, f32[11,2,32,128]{3,2,1,0:T(8,128)}, u32[]{:S(2)}) copy-start(f32[11,2,32,128]{3,2,1,0:T(8,128)} %particles.1) | copy-start | bytes 1081348
  1.0 0.8 %copy-start.2 = (s32[2,2,32,128]{3,2,1,0:T(8,128)S(1)}, s32[2,2,32,128]{3,2,1,0:T(8,128)}, u32[]{:S(2)}) copy-start(s32[2,2,32,128]{3,2,1,0:T(8,128)} %pairs.1) | copy-start | bytes 196612
  1.8 0.7 %copy-start.5 = (s32[2,32]{1,0:T(2,128)S(1)}, s32[2,32]{1,0:T(2,128)}, u32[]{:S(2)}) copy-start(s32[2,32]{1,0:T(2,128)} %count.3) | copy-start | bytes 772
  2.5 12.0 %copy-start.1 = (f32[11,2,32,128]{3,2,1,0:T(8,128)S(1)}, f32[11,2,32,128]{3,2,1,0:T(8,128)}, u32[]{:S(2)}) copy-start(f32[11,2,32,128]{3,2,1,0:T(8,128)} %particles.1) | copy-start | bytes 1081348
  2.5 12.0 %copy-start.3 = (s32[2,2,32,128]{3,2,1,0:T(8,128)S(1)}, s32[2,2,32,128]{3,2,1,0:T(8,128)}, u32[]{:S(2)}) copy-start(s32[2,2,32,128]{3,2,1,0:T(8,128)} %pairs.1) | copy-start | bytes 196612
  2.6 10.5 %copy-start.9 = (s32[2,1,1]{0,2,1:T(1,128)S(1)}, s32[2,1,1]{0,2,1:T(1,128)}, u32[]{:S(2)}) copy-start(s32[2,1,1]{0,2,1:T(1,128)} %param.13) | copy-start | bytes 28
  2.7 11.8 %copy-start.4 = (s32[2,2,1,16]{3,2,1,0:T(1,128)S(1)}, s32[2,2,1,16]{3,2,1,0:T(1,128)}, u32[]{:S(2)}) copy-start(s32[2,2,1,16]{3,2,1,0:T(1,128)} %movers.3) | copy-start | bytes 772
  2.7 10.5 %collective-permute-start = (f32[24,128]{1,0:T(8,128)S(1)}, f32[24,128]{1,0:T(8,128)S(1)}, u32[]{:S(2)}, u32[]{:S(2)}) collective-permute-start(f32[24,128]{1,0:T(8,128)S(1)} %get-tuple-element.12), channel_id=1, source_target_pairs={{0,1},{1,0},{2,3},{3,2},{4,5},{5,4},{6,7},{7,6},{8,9},{9,8},{10,11... | collective-permute-start | bytes 36872 | tf_op jit(solution)/shard_map/ppermute | solution.py:412
  5.3 9.2 %copy-start.6 = (s32[2,32]{1,0:T(2,128)S(1)}, s32[2,32]{1,0:T(2,128)}, u32[]{:S(2)}) copy-start(s32[2,32]{1,0:T(2,128)} %count.3) | copy-start | bytes 772
  5.3 9.2 %collective-permute-start.1 = (f32[24,128]{1,0:T(8,128)S(1)}, f32[24,128]{1,0:T(8,128)S(1)}, u32[]{:S(2)}, u32[]{:S(2)}) collective-permute-start(f32[24,128]{1,0:T(8,128)S(1)} %get-tuple-element.13), channel_id=1, source_target_pairs={{1,2},{2,1},{3,4},{4,3},{5,6},{6,5},{9,10},{10,9},{11,12},{12,11},... | collective-permute-start | bytes 36872 | tf_op jit(solution)/shard_map/ppermute | solution.py:412
  23.1 9.8 %collective-permute-start.2 = (f32[11,40,128]{2,1,0:T(8,128)S(1)}, f32[11,40,128]{2,1,0:T(8,128)S(1)}, u32[]{:S(2)}, u32[]{:S(2)}) collective-permute-start(f32[11,40,128]{2,1,0:T(8,128)S(1)} %get-tuple-element.17), channel_id=1, source_target_pairs={{0,8},{8,0},{16,24},{24,16},{32,40},{40,32},{48,56},{56,48},{64,72... | collective-permute-start | bytes 675848 | tf_op jit(solution)/shard_map/ppermute | solution.py:412
  26.3 13.2 %collective-permute-start.3 = (f32[11,40,128]{2,1,0:T(8,128)S(1)}, f32[11,40,128]{2,1,0:T(8,128)S(1)}, u32[]{:S(2)}, u32[]{:S(2)}) collective-permute-start(f32[11,40,128]{2,1,0:T(8,128)S(1)} %get-tuple-element.18), channel_id=1, source_target_pairs={{8,16},{16,8},{24,32},{32,24},{40,48},{48,40},{56,64},{64,56},{72,... | collective-permute-start | bytes 675848 | tf_op jit(solution)/shard_map/ppermute | solution.py:412
  39.5 0.7 %copy-start.7 = (s32[2,2,1,16]{3,2,1,0:T(1,128)S(1)}, s32[2,2,1,16]{3,2,1,0:T(1,128)}, u32[]{:S(2)}) copy-start(s32[2,2,1,16]{3,2,1,0:T(1,128)} %arrivals.1) | copy-start | bytes 772
  39.5 0.7 %copy-start.8 = (s32[2,32]{1,0:T(2,128)S(1)}, s32[2,32]{1,0:T(2,128)}, u32[]{:S(2)}) copy-start(s32[2,32]{1,0:T(2,128)} %filled.1) | copy-start | bytes 772

commit v2 on v1

v2 whole, which is shorter than its diff:
```python
import jax
import jax.numpy as jnp
from jax import lax
from jax.experimental import pallas as pl
from jax.experimental.pallas import tpu as pltpu
from jax.sharding import PartitionSpec as P

spring = 4.0
normal_damp = 0.5
tangent_damp = 0.3
conduct = 40.0
timestep = 0.05
density = 100.0
gravity = 9.81
soft_len = 0.05

COMPS = 11
LANES = 128
LIVE = 96
COLS = 32
SLAB = 40
EXT = 56
BASE = 8
SOURCES = 34
EDGE = COMPS * COLS
PAYLOAD = EDGE + 24
row_steps = (0, 1, 0, 1, 1)
col_steps = (0, 0, 1, 1, -1)


def iota(shape, dim):
    return lax.broadcasted_iota(jnp.int32, shape, dim)


def pick(values, index):
    return jnp.take_along_axis(values, index, axis=1, mode="promise_in_bounds")


def to_column(row, size):
    n = row.shape[1]
    spread = jnp.where(iota((size, n), 0) == iota((size, n), 1), row, 0)
    return jnp.sum(spread, axis=1, keepdims=True)


def cross(a, b):
    return (
        a[1] * b[2] - a[2] * b[1],
        a[2] * b[0] - a[0] * b[2],
        a[0] * b[1] - a[1] * b[0],
    )


def pair_terms(first, second, row_shift, col_shift, listed):
    gap = (second[0] + row_shift - first[0], second[1] + col_shift - first[1], second[2] - first[2])
    dist = jnp.sqrt(gap[0] * gap[0] + gap[1] * gap[1] + gap[2] * gap[2] + soft_len * soft_len)
    inverse = 1.0 / dist
    n = tuple(g * inverse for g in gap)
    r1, r2 = first[9], second[9]
    intersection = r1 + r2 - dist
    spin = tuple(r1 * first[6 + i] + r2 * second[6 + i] for i in range(3))
    turn = cross(spin, n)
    w = tuple(second[3 + i] - first[3 + i] - turn[i] for i in range(3))
    u = w[0] * n[0] + w[1] * n[1] + w[2] * n[2]
    fric = tuple(tangent_damp * (w[i] - u * n[i]) for i in range(3))
    push = normal_damp * u - spring * intersection
    force = tuple(push * n[i] + fric[i] for i in range(3))
    torque = cross(n, fric)
    denom = jnp.where(listed, r1 + r2, 1.0)
    heat = 2.0 * conduct * r1 * r2 / denom * (second[10] - first[10])
    on_first = [*force, *(r1 * t for t in torque), heat]
    on_second = [*(-f for f in force), *(r2 * t for t in torque), -heat]
    return (
        [jnp.where(listed, t, 0.0) for t in on_first],
        [jnp.where(listed, t, 0.0) for t in on_second],
    )


def stepped(state, totals, live):
    r = state[9] + jnp.where(live, 0.0, 1.0)
    mass = density * r * r * r
    per_mass = timestep / mass
    per_inertia = timestep / (0.4 * mass * r * r)
    v = [state[3] + per_mass * totals[0], state[4] + per_mass * totals[1]]
    v.append(state[5] + per_mass * totals[2] - timestep * gravity)
    spin = [state[6 + i] + per_inertia * totals[3 + i] for i in range(3)]
    x = [state[i] + timestep * v[i] for i in range(3)]
    warmth = state[10] + per_mass * totals[6]
    return [jnp.where(live, t, 0.0) for t in [*x, *v, *spin, state[9], warmth]]


def shifts(heading):
    row_shift = jnp.where((heading == 0) | (heading == 2), 0.0, 1.0)
    col_shift = jnp.where(
        (heading == 2) | (heading == 3), 1.0, jnp.where(heading == 4, -1.0, 0.0)
    )
    return row_shift, col_shift


def keep(ref, base, terms):
    n = terms[0].shape[0]
    for j in range(7):
        ref[base + j * n : base + (j + 1) * n, :] = terms[j]
    ref[base + 7 * n : base + 8 * n, :] = jnp.zeros((n, LANES), jnp.float32)


def halves(x):
    high = x.astype(jnp.bfloat16).astype(jnp.float32)
    return jnp.concatenate([high, x - high], 0).astype(jnp.bfloat16)


def one_hot(index_row):
    hot = iota((LANES, LANES), 0) == index_row
    return jnp.where(hot, 1.0, 0.0).astype(jnp.bfloat16)


def spread(left, first_row, second_row):
    hot = jnp.concatenate([one_hot(first_row), one_hot(second_row)], 1)
    out = lax.dot_general(
        halves(left), hot, (((1,), (1,)), ((), ())), preferred_element_type=jnp.float32
    )
    rows = left.shape[0]
    return out[:rows] + out[rows:]


def packed(j, value, lists, count, info):
    lane = iota(value.shape, 1)
    if j < 8:
        extra = lists[j // 4].astype(jnp.float32)
        if j % 4 != 3:
            extra = pltpu.roll(extra, LIVE - 32 * (j % 4), 1)
    elif j == 8:
        extra = count.astype(jnp.float32)
    elif j == 9 and info is not None:
        extra = info
    else:
        return value
    return jnp.where(lane < LIVE, value, extra)


def unpacked(rows):
    lane = iota(rows[0].shape, 1)
    lists = []
    for half in range(2):
        value = rows[half * 4 + 3]
        for k in range(3):
            moved = pltpu.roll(rows[half * 4 + k], 32 * k + 32, 1)
            value = jnp.where(lane // 32 == k, moved, value)
        lists.append(value.astype(jnp.int32))
    return lists


def lane_of(value, k):
    return value[:, LIVE + k : LIVE + k + 1]


def pack_columns(particles, pairs, count, far, near, p_west, p_east, c_west, c_east, n_all, sems):
    last = COLS - 8
    copies = [
        pltpu.make_async_copy(particles.at[:, :, 0:8, :], p_west, sems.at[0]),
        pltpu.make_async_copy(particles.at[:, :, last:COLS, :], p_east, sems.at[1]),
        pltpu.make_async_copy(pairs.at[:, :, 0:8, :], c_west, sems.at[2]),
        pltpu.make_async_copy(pairs.at[:, :, last:COLS, :], c_east, sems.at[3]),
        pltpu.make_async_copy(count, n_all, sems.at[4]),
    ]
    for copy in copies:
        copy.start()
    near[...] = jnp.zeros(near.shape, jnp.float32)
    far[...] = jnp.zeros(far.shape, jnp.float32)
    odd = lax.rem(lax.axis_index("span"), 2) == 1
    for copy in copies:
        copy.wait()
    for r in range(2):
        n_row = n_all[r : r + 1, :]
        sides = []
        for p, c, at, cell in ((p_west, c_west, 0, 0), (p_east, c_east, 7, COLS - 1)):
            n = jnp.sum(jnp.where(iota((1, COLS), 1) == cell, n_row, 0), axis=1, keepdims=True)
            lists = [c[k, r, at : at + 1, :] for k in range(2)]
            sides.append([packed(j, p[j, r, at : at + 1, :], lists, n, None) for j in range(COMPS)])
        for j in range(COMPS):
            west, east = sides[0][j], sides[1][j]
            row = r * 12 + j
            near[row : row + 1, :] = jnp.where(odd, west, east)
            far[row : row + 1, :] = jnp.where(odd, east, west)


def leavers(movers, counts, row):
    direction = 1 - row
    cells = lax.rem(movers[direction, 0], COLS)
    slots = movers[direction, 1]
    n = cells.shape[1]
    number = iota((COLS, n), 1)
    here = (iota((COLS, n), 0) == cells) & (number < counts[direction, 0, 0])
    slot = jnp.sum(jnp.where(here, slots + 1, 0), axis=1, keepdims=True)
    which = jnp.sum(jnp.where(here, number, 0), axis=1, keepdims=True)
    return slot, which


def roll_cells(value, step):
    return pltpu.roll(value, step % value.shape[0], 0)


def inner_terms(
    particles, pairs, count, movers, counts, on_first, on_second, to_near, to_far, ext, infos
):
    lane = iota((COLS, LANES), 1)
    column = iota((COLS, LANES), 0)
    zeros = jnp.zeros((8, LANES), jnp.float32)
    for r in range(2):
        for j in range(COMPS):
            ext[j, r, 0:8, :] = zeros
            ext[j, r, 40:48, :] = zeros
            ext[j, r, 8:40, :] = particles[j, r]
    counted = [to_column(count[r : r + 1, :], COLS) for r in range(2)]
    hits = []
    for r in range(2):
        headings = (0, 1, 2, 3, 4) if r == 0 else (0, 2)
        first_index = pairs[0, r]
        heading = pairs[1, r] // LANES
        target = lax.rem(pairs[1, r], LANES)
        outside = (column == COLS - 1) & ((heading == 2) | (heading == 3)) | (column == 0) & (heading == 4)
        listed = (lane < counted[r]) & ~outside
        if r == 1:
            listed = listed & ((heading == 0) | (heading == 2))
        first = [pick(particles[j, r], first_index) for j in range(COMPS)]
        second = []
        for j in range(COMPS):
            value = None
            for d in headings:
                at = BASE + col_steps[d]
                got = pick(ext[j, r + row_steps[d], at : at + COLS, :], target)
                value = got if value is None else jnp.where(heading == d, got, value)
            second.append(value)
        row_shift, col_shift = shifts(heading)
        f, s = pair_terms(first, second, row_shift, col_shift, listed)
        keep(on_first, r * 8 * COLS, f)
        keep(on_second, r * 8 * COLS, s)
        hits.append((first_index, heading, target))

    for r in range(2):
        slot, which = leavers(movers, counts, r)
        wide = jnp.broadcast_to(slot - 1, (COLS, LANES))
        first_index, heading, target = hits[r]
        own_first = first_index == wide
        own_second = (heading == 0) & (target == wide)
        from_left = (heading == 2) & (target == roll_cells(wide, -1))
        if r == 1:
            _, above, aim = hits[0]
            straight = (above == 1) & (aim == wide)
            slant = (above == 3) & (aim == roll_cells(wide, -1))
            back = (above == 4) & (aim == roll_cells(wide, 1))
        info = jnp.where(lane == LIVE + 7, slot.astype(jnp.float32), which.astype(jnp.float32))
        for j in range(7):
            base = (r * 8 + j) * COLS
            f = on_first[base : base + COLS, :]
            s = on_second[base : base + COLS, :]
            total = jnp.where(own_first, f, 0.0) + jnp.where(own_second, s, 0.0)
            right = jnp.where(from_left, s, 0.0)
            if r == 1:
                u = on_second[j * COLS : (j + 1) * COLS, :]
                total = total + jnp.where(straight, u, 0.0)
                right = right + jnp.where(slant, u, 0.0)
                total = total + roll_cells(jnp.where(back, u, 0.0), -1)
            total = total + roll_cells(right, 1)
            info = jnp.where(lane == LIVE + j, jnp.sum(total, axis=1, keepdims=True), info)
        infos[r] = info

    turn = lax.rem(lax.axis_index("blade"), 2)
    for out, row in ((to_near, 1 - turn), (to_far, turn)):
        n = jnp.where(row == 1, counted[1], counted[0])
        lists = [pairs[k, row] for k in range(2)]
        for j in range(COMPS):
            value = packed(j, particles[j, row], lists, jnp.broadcast_to(n, (COLS, LANES)), infos[row])
            out[j * COLS : (j + 1) * COLS, :] = value


def edge_terms(
    got_near, got_far, sent_near, sent_far, infos, near_in, far_in, to_far, to_near, edges, edge_first, edge_second
):
    to_near[0:EDGE, :] = near_in[0:EDGE, :]
    to_far[0:EDGE, :] = far_in[0:EDGE, :]
    odd = lax.rem(lax.axis_index("span"), 2) == 1
    west = jnp.where(odd, got_near[...], got_far[...])
    east = jnp.where(odd, got_far[...], got_near[...])
    west_own = jnp.where(odd, sent_near[...], sent_far[...])
    east_own = jnp.where(odd, sent_far[...], sent_near[...])
    for k, side in enumerate((west, west_own, east_own, east)):
        for r in range(2):
            edges[pl.ds(4 * r + k, 12, stride=8), :] = side[r * 12 : r * 12 + 12]
    tile = [edges[j * 8 : j * 8 + 8, :] for j in range(COMPS)]
    first_index, second_index = unpacked(tile[:8])
    heading = second_index // LANES
    target = lax.rem(second_index, LANES)
    spot = iota((8, LANES), 0)
    lane = iota((8, LANES), 1)
    even = lax.rem(spot, 2) == 0
    listed = lane < lane_of(tile[8], 0).astype(jnp.int32)
    listed = listed & (
        ((heading == 2) & even)
        | ((heading == 3) & even & (spot < 4))
        | ((heading == 4) & ~even & (spot < 4))
    )
    first = [pick(t, first_index) for t in tile]
    second = []
    for t in tile:
        beside = pick(roll_cells(t, -1), target)
        below = pick(jnp.where(even, roll_cells(t, -5), roll_cells(t, -3)), target)
        second.append(jnp.where(heading == 2, beside, below))
    row_shift, col_shift = shifts(heading)
    f, s = pair_terms(first, second, row_shift, col_shift, listed)
    keep(edge_first, 0, f)
    keep(edge_second, 0, s)

    slots = [[lane_of(infos[r, c : c + 1, :], 7).astype(jnp.int32) for c in (0, COLS - 1)] for r in range(2)]

    def at_spots(*choices):
        value = jnp.zeros((8, LANES), jnp.int32)
        for k, slot in choices:
            value = jnp.where(spot == k, slot, value)
        return value - 1

    mine = first_index == at_spots((1, slots[0][0]), (2, slots[0][1]), (6, slots[1][1]))
    beside = (heading == 2) & (target == at_spots((0, slots[0][0]), (4, slots[1][0])))
    below = (heading != 2) & (target == at_spots((0, slots[1][0]), (3, slots[1][1])))
    sums = [jnp.zeros((8, LANES), jnp.float32)] * 3
    for j in range(7):
        for k, (hit, term) in enumerate(((mine, f[j]), (beside, s[j]), (below, s[j]))):
            total = jnp.sum(jnp.where(hit, term, 0.0), axis=1, keepdims=True)
            sums[k] = jnp.where(lane == LIVE + j, total, sums[k])
    fixes = (
        (sums[0][1:2] + sums[1][0:1], sums[0][2:3]),
        (sums[1][4:5] + sums[2][0:1], sums[0][6:7] + sums[2][3:4]),
    )
    turn = lax.rem(lax.axis_index("blade"), 2)
    for out, row in ((to_near, 1 - turn), (to_far, turn)):
        low = row == 1
        for k, c in enumerate((0, COLS - 1)):
            at = 9 * COLS + c
            out[at : at + 1, :] += jnp.where(low, fixes[1][k], fixes[0][k])
        out[EDGE : EDGE + 12, :] = jnp.where(low, east[12:24], east[0:12])
        out[EDGE + 12 : EDGE + 24, :] = jnp.where(low, west[12:24], west[0:12])


def own_sums(
    particles, pairs, count, filled, movers, counts, arrivals, on_first, on_second, edges, edge_first, edge_second,
    ext_in, sums, ext, first_low, lists_low, stays, landing, by_source0, by_source1,
):
    ext[...] = ext_in[...]
    sizes = (40, 16)
    for ref, size in ((by_source0, 40), (by_source1, 16)):
        ref[0:size, :] = jnp.zeros((size, LANES), jnp.float32)
        ref[33 * size : 34 * size, :] = jnp.zeros((size, LANES), jnp.float32)
    blank = jnp.zeros((8, LANES), jnp.float32)
    for r, (ref, headings) in enumerate(((by_source0, (0, 1, 2, 3, 4)), (by_source1, (0, 2)))):

        def source(c, _, r=r, ref=ref, headings=headings):
            f = on_first[pl.ds(r * 8 * COLS + c, 8, stride=COLS), :]
            s = on_second[pl.ds(r * 8 * COLS + c, 8, stride=COLS), :]
            second_row = pairs[1, r, pl.ds(c, 1), :]
            heading = second_row // LANES
            left = jnp.concatenate(
                [jnp.concatenate([f if d == 0 else blank, jnp.where(heading == d, s, 0.0)], 1) for d in headings],
                0,
            )
            out = spread(left, pairs[0, r, pl.ds(c, 1), :], lax.rem(second_row, LANES))
            size = sizes[r]
            ref[pl.ds(pl.multiple_of((c + 1) * size, 8), size), :] = out
            return 0

        lax.fori_loop(0, COLS, source, 0, unroll=4)
    tile = [edges[j * 8 : j * 8 + 8, :] for j in range(COMPS)]
    first_index, second_index = unpacked(tile[:8])
    heading = second_index // LANES
    target = lax.rem(second_index, LANES)
    for k in (0, 1, 2, 3, 4, 6):
        f = edge_first[pl.ds(k, 8, stride=8), :]
        s = edge_second[pl.ds(k, 8, stride=8), :]
        aim = heading[k : k + 1]
        left = jnp.concatenate(
            [
                jnp.concatenate([f, blank], 1),
                jnp.concatenate([blank, jnp.where(aim == 2, s, 0.0)], 1),
                jnp.concatenate([blank, jnp.where(aim == 2, 0.0, s)], 1),
                jnp.zeros((8, 2 * LANES), jnp.float32),
            ],
            0,
        )
        out = spread(left, first_index[k : k + 1], target[k : k + 1])
        if k == 0:
            by_source0[16:24, :] = out[8:16]
            by_source0[24:32, :] = out[16:24]
        elif k == 1:
            by_source0[40:48, :] += out[0:8]
        elif k == 2:
            by_source0[32 * 40 : 32 * 40 + 8, :] += out[0:8]
        elif k == 3:
            by_source0[33 * 40 + 32 : 33 * 40 + 40, :] = out[16:24]
        elif k == 4:
            by_source1[8:16, :] = out[8:16]
        else:
            by_source1[32 * 16 : 32 * 16 + 8, :] += out[0:8]

    def column(ref, size, tile_at, shift, j):
        return ref[pl.ds((1 + shift) * size + tile_at * 8 + j, COLS, stride=size), :]

    for j in range(7):
        sums[0, j] = column(by_source0, 40, 0, 0, j) + column(by_source0, 40, 2, -1, j)
        total = column(by_source1, 16, 0, 0, j) + column(by_source1, 16, 1, -1, j)
        total = total + column(by_source0, 40, 1, 0, j) + column(by_source0, 40, 3, -1, j)
        sums[1, j] = total + column(by_source0, 40, 4, 1, j)

    for r in range(2):
        for j in range(COMPS):
            for k, at in ((3, 40), (0, 41), (1, 42), (0, 7)):
                ext[j, r, at : at + 1, :] = tile[j][4 * r + k : 4 * r + k + 1]
    rows = jnp.concatenate([pairs[0, 1], first_index[7:8], first_index[4:5], jnp.zeros((6, LANES), jnp.int32)], 0)
    seconds = jnp.concatenate([pairs[1, 1], second_index[7:8], second_index[4:5], jnp.zeros((6, LANES), jnp.int32)], 0)
    edge_count = lane_of(tile[8], 0).astype(jnp.int32)
    n = jnp.concatenate(
        [to_column(count[1:2, :], COLS), edge_count[7:8], edge_count[4:5], jnp.zeros((6, 1), jnp.int32)], 0
    )
    lists_low[0] = rows
    lists_low[1] = jnp.where(iota((SLAB, LANES), 1) < n, seconds // LANES, -1)
    lists_low[2] = lax.rem(seconds, LANES)
    for j in range(COMPS):
        first_low[j] = pick(ext[j, 1, BASE : BASE + SLAB, :], rows)
    for r in range(2):
        slot, _ = leavers(movers, counts, r)
        lane = iota((COLS, LANES), 1)
        live = lane < to_column(filled[r : r + 1, :], COLS)
        stays[r] = jnp.where(live, jnp.where(lane != slot - 1, 2, 1), 0)
        cells = to_column(lax.rem(arrivals[r, 0], COLS), 16)
        slots = to_column(arrivals[r, 1], 16)
        hit = slots == iota((16, LANES), 1)
        number = jnp.sum(jnp.where(hit, iota((16, LANES), 0) + 1, 0), axis=0, keepdims=True) - 1
        cell = jnp.sum(jnp.where(hit, cells, 0), axis=0, keepdims=True)
        landing[8 * r : 8 * r + 1, :] = number
        landing[8 * r + 1 : 8 * r + 2, :] = jnp.where(number >= 0, cell, -1)


def across_rows(
    near, far, sums, ext, first_low, lists_low, stays, landing, out, around, on_first, on_second, indices, by_source
):
    turn = lax.rem(lax.axis_index("blade"), 2) == 1
    zeros = jnp.zeros((8, LANES), jnp.float32)
    for j in range(COMPS):
        rows = slice(j * COLS, (j + 1) * COLS)
        east, west = slice(EDGE + j, EDGE + j + 1), slice(EDGE + 12 + j, EDGE + 13 + j)
        for side, (yes, no) in enumerate(((near, far), (far, near))):
            main = jnp.where(turn, yes[rows, :], no[rows, :])
            right = jnp.where(turn, yes[east, :], no[east, :])
            left = jnp.where(turn, yes[west, :], no[west, :])
            around[side, j, 40:48, :] = zeros
            around[side, j, 8:40, :] = main
            around[side, j, 40:41, :] = right
            around[side, j, 41:42, :] = left
            around[side, j, 42:43, :] = main[0:1]
            around[side, j, 7:8, :] = left
    lane = iota((SLAB, LANES), 1)

    def behind(j):
        return around[0, j, BASE : BASE + SLAB, :]

    def ahead(j):
        return around[1, j, BASE : BASE + SLAB, :]

    firsts_behind, seconds_behind = unpacked([behind(j) for j in range(8)])
    heading_behind = jnp.where(lane < lane_of(behind(8), 0).astype(jnp.int32), seconds_behind // LANES, -1)
    kept = []
    for r in range(2):
        if r == 0:
            first = [pick(behind(j), firsts_behind) for j in range(COMPS)]
            heading, target = heading_behind, lax.rem(seconds_behind, LANES)
        else:
            first = [first_low[j] for j in range(COMPS)]
            heading, target = lists_low[1], lists_low[2]
        second = []
        for j in range(COMPS):
            value = None
            for d in (1, 3, 4):
                at = BASE + col_steps[d]
                others = ext[j, 0, at : at + SLAB, :] if r == 0 else around[1, j, at : at + SLAB, :]
                got = pick(others, target)
                value = got if value is None else jnp.where(heading == d, got, value)
            second.append(value)
        listed = (heading == 1) | (heading == 3) | (heading == 4)
        _, col_shift = shifts(heading)
        f, s = pair_terms(first, second, 1.0, col_shift, listed)
        keep(on_first, r * 8 * SLAB, f)
        keep(on_second, r * 8 * SLAB, s)
        kept.append((heading, target))
    indices[0] = kept[0][0]
    indices[1] = kept[0][1]
    blank = jnp.zeros((8, LANES), jnp.float32)

    def source(c, _):
        f = on_first[pl.ds(8 * SLAB + c, 8, stride=SLAB), :]
        s = on_second[pl.ds(c, 8, stride=SLAB), :]
        heading = indices[0, pl.ds(c, 1), :]
        left = jnp.concatenate(
            [jnp.concatenate([f, blank], 1)]
            + [jnp.concatenate([blank, jnp.where(heading == d, s, 0.0)], 1) for d in (1, 3, 4)],
            0,
        )
        got = spread(left, lists_low[0, pl.ds(c, 1), :], indices[1, pl.ds(c, 1), :])
        by_source[pl.ds(pl.multiple_of((c + 1) * 32, 8), 32), :] = got
        return 0

    lax.fori_loop(0, SOURCES, source, 0, unroll=UNROLL)
    by_source[0:32, :] = by_source[34 * 32 : 35 * 32, :]

    placed = []
    for side in range(2):
        state_of = behind if side == 0 else ahead
        info = state_of(9)[:COLS]
        slot = lane_of(info, 7).astype(jnp.int32)
        which = lane_of(info, 8).astype(jnp.int32)
        leaves = slot > 0
        leaving = []
        if side == 0:
            hit = firsts_behind[:COLS] == slot - 1
            for j in range(7):
                term = jnp.where(hit, on_first[j * SLAB : j * SLAB + COLS, :], 0.0)
                leaving.append(jnp.sum(term, axis=1, keepdims=True))
        else:
            heading, target = kept[1]
            wide = jnp.broadcast_to(slot - 1, (COLS, LANES))
            wide = jnp.concatenate([wide, jnp.full((8, LANES), -1, jnp.int32)], 0)
            up = roll_cells(wide, -1)
            up = jnp.where(iota((SLAB, LANES), 0) == 33, wide[0:1], up)
            masks = {
                1: (heading == 1) & (target == wide),
                3: (heading == 3) & (target == up),
                4: (heading == 4) & (target == roll_cells(wide, 1)),
            }
            first_cell = iota((COLS, LANES), 0) == 0
            for j in range(7):
                term = on_second[(8 + j) * SLAB : (9 + j) * SLAB, :]
                total = jnp.where(masks[1], term, 0.0)[:COLS]
                slant = jnp.where(masks[3], term, 0.0)
                slant = jnp.where(first_cell, slant[33:34], roll_cells(slant, 1)[:COLS])
                total = total + slant + roll_cells(jnp.where(masks[4], term, 0.0), -1)[:COLS]
                leaving.append(jnp.sum(total, axis=1, keepdims=True))
        leaving = [t + lane_of(info, j) for j, t in enumerate(leaving)]
        at_slot = jnp.broadcast_to(jnp.maximum(slot - 1, 0), (COLS, LANES))
        state = [pick(state_of(j)[:COLS], at_slot) for j in range(COMPS)]
        moved = stepped(state, leaving, leaves)
        moved[0] = moved[0] + (-1.0 if side == 0 else 1.0)
        match = (which == landing[8 * side : 8 * side + 1, :]) & leaves
        placed.append([jnp.sum(jnp.where(match, m, 0.0), axis=0, keepdims=True) for m in moved])

    column = iota((COLS, LANES), 0)
    for r in range(2):
        totals = []
        for j in range(7):
            total = sums[r, j]
            if r == 0:
                for k, shift in ((1, 0), (2, -1), (3, 1)):
                    total = total + by_source[pl.ds((1 + shift) * 32 + k * 8 + j, COLS, stride=32), :]
            else:
                total = total + by_source[pl.ds(32 + j, COLS, stride=32), :]
            totals.append(total)
        state = [ext[j, r, BASE : BASE + COLS, :] for j in range(COMPS)]
        rows = stepped(state, totals, stays[r] > 0)
        lands = column == landing[8 * r + 1 : 8 * r + 2, :]
        for j in range(COMPS):
            out[j, r] = jnp.where(lands, placed[r][j], jnp.where(stays[r] == 1, 0.0, rows[j]))


UNROLL = 2


def swapped(block, axis, start):
    pairs = []
    for i in range(start, lax.axis_size(axis) - 1, 2):
        pairs += [(i, i + 1), (i + 1, i)]
    return lax.ppermute(block, axis, pairs)


vmem = pl.BlockSpec(memory_space=pltpu.VMEM)
smem = pl.BlockSpec(memory_space=pltpu.SMEM)
hbm = pl.BlockSpec(memory_space=pltpu.HBM)
params = pltpu.CompilerParams(vmem_limit_bytes=24 * 1024 * 1024)


def shape(*dims, dtype=jnp.float32):
    return jax.ShapeDtypeStruct(dims, dtype)


def buffer(*dims, dtype=jnp.float32):
    return pltpu.VMEM(dims, dtype)


def body(particles, filled, contact_pairs, contact_count, movers_out, movers_in, move_count):
    ints = jnp.int32
    far, near = pl.pallas_call(
        pack_columns,
        in_specs=[hbm] * 3,
        out_specs=[vmem] * 2,
        out_shape=[shape(24, LANES)] * 2,
        scratch_shapes=[
            buffer(COMPS, 2, 8, LANES),
            buffer(COMPS, 2, 8, LANES),
            buffer(2, 2, 8, LANES, dtype=ints),
            buffer(2, 2, 8, LANES, dtype=ints),
            buffer(2, COLS, dtype=ints),
            pltpu.SemaphoreType.DMA((5,)),
        ],
        compiler_params=pltpu.CompilerParams(vmem_limit_bytes=60 * 1024 * 1024),
        name="pack_columns",
    )(particles, contact_pairs, contact_count)
    got_far = swapped(far, "span", 1)
    got_near = swapped(near, "span", 0)
    on_first, on_second, to_near, to_far, ext, infos = pl.pallas_call(
        inner_terms,
        in_specs=[vmem] * 4 + [smem],
        out_specs=[vmem] * 6,
        out_shape=[
            shape(16 * COLS, LANES),
            shape(16 * COLS, LANES),
            shape(PAYLOAD, LANES),
            shape(PAYLOAD, LANES),
            shape(COMPS, 2, EXT, LANES),
            shape(2, COLS, LANES),
        ],
        compiler_params=params,
        name="inner_terms",
    )(particles, contact_pairs, contact_count, movers_out, move_count)
    to_far, to_near, edges, edge_first, edge_second = pl.pallas_call(
        edge_terms,
        in_specs=[vmem] * 7,
        out_specs=[vmem] * 5,
        out_shape=[
            shape(PAYLOAD, LANES),
            shape(PAYLOAD, LANES),
            shape(96, LANES),
            shape(64, LANES),
            shape(64, LANES),
        ],
        compiler_params=params,
        name="edge_terms",
    )(got_near, got_far, near, far, infos, to_near, to_far)
    row_far = swapped(to_far, "blade", 1)
    row_near = swapped(to_near, "blade", 0)
    sums, ext, first_low, lists_low, stays, landing = pl.pallas_call(
        own_sums,
        in_specs=[vmem] * 5 + [smem] + [vmem] * 7,
        out_specs=[vmem] * 6,
        out_shape=[
            shape(2, 7, COLS, LANES),
            shape(COMPS, 2, EXT, LANES),
            shape(COMPS, SLAB, LANES),
            shape(3, SLAB, LANES, dtype=ints),
            shape(2, COLS, LANES, dtype=ints),
            shape(16, LANES, dtype=ints),
        ],
        scratch_shapes=[buffer(34 * 40, LANES), buffer(34 * 16, LANES)],
        compiler_params=params,
        name="own_sums",
    )(
        particles, contact_pairs, contact_count, filled, movers_out, move_count, movers_in,
        on_first, on_second, edges, edge_first, edge_second, ext,
    )
    return pl.pallas_call(
        across_rows,
        in_specs=[vmem] * 8,
        out_specs=vmem,
        out_shape=shape(COMPS, 2, COLS, LANES),
        scratch_shapes=[
            buffer(2, COMPS, EXT, LANES),
            buffer(16 * SLAB, LANES),
            buffer(16 * SLAB, LANES),
            buffer(2, SLAB, LANES, dtype=ints),
            buffer(35 * 32, LANES),
        ],
        compiler_params=params,
        name="across_rows",
    )(row_near, row_far, sums, ext, first_low, lists_low, stays, landing)


def solution(mesh):
    return jax.shard_map(
        body,
        mesh=mesh,
        in_specs=(
            P(None, "blade", "span", None),
            P("blade", "span"),
            P(None, "blade", "span", None),
            P("blade", "span"),
            P(None, None, "blade", "span"),
            P(None, None, "blade", "span"),
            P(None, "blade", "span"),
        ),
        out_specs=P(None, "blade", "span", None),
        check_vma=False,
    )
```

time: 47.6 us -> 36.8 us (0.77)
  waiting for transfers between devices: 7.87 us -> 0.21 us
  local copies, waits for them, and re-layouts: 3.31 us -> 0.81 us
  Pallas kernels: 15.7 us -> 15.2 us
    ppermute x4, waiting for transfers between devices: 7.87 us -> 0.21 us  [swapped(): return lax.ppermute(block, axis, pairs)]
    unnamed x21 -> x19, local copies, waits for them, and re-layouts: 3.31 us -> 0.81 us
    pallas_call x3 -> x5, Pallas kernels: 15.7 us -> 15.2 us  [the longest x1 6.09 us: body(): pl.pallas_call(across_rows, in_specs=[vmem] * 8, out_specs=vmem, out_shap...]
  transfers between devices with their start and end apart: 4 -> 4, of which waited for: 2 -> 1; matrix products, arithmetic and copies ran while one was open for 0% -> 0% of each run, Pallas kernels for 0% -> 19%
where the time goes in v2:
time: 36.8 us; the launch traced here: 36.5 us
  starting transfers between devices  20.1 us (55%)
  Pallas kernels  15.2 us (41%)
  local copies, waits for them, and re-layouts  0.81 us (2%)
    ppermute x4, starting transfers between devices, swapped(): return lax.ppermute(block, axis, pairs)  20.1 us
    pallas_call x1, Pallas kernels, body(): pl.pallas_call(across_rows, in_specs=[vmem] * 8, out_specs=vmem, out_shap...  6.09 us
    pallas_call x1, Pallas kernels, body(): pl.pallas_call(own_sums, in_specs=[vmem] * 5 + [smem] + [vmem] * 7, out_s...  4.81 us
    pallas_call x1, Pallas kernels, body(): pl.pallas_call(inner_terms, in_specs=[vmem] * 4 + [smem], out_specs=[vmem...  2.17 us
    pallas_call x1, Pallas kernels, body(): pl.pallas_call(pack_columns, in_specs=[hbm] * 3, out_specs=[vmem] * 2, ou...  1.8 us
    unnamed x19, local copies, waits for them, and re-layouts  0.81 us
  transfers between devices with their start and end apart: 4, of which 1 were waited for; matrix products, arithmetic and copies ran while one was open for 0% of the time, Pallas kernels for 19%

profile of v2, /device:TPU:161, one launch (start us, length us, event | category | flops | bytes accessed | tf_op | source)
XLA Modules:
  0.0 36.5 jit_solution(879522966981056609)
XLA Ops:
  0.0 0.0 copy-start.1
  0.0 0.0 copy-start
  0.0 1.8 %pack_columns.1 = (f32[24,128]{1,0:T(8,128)}, f32[24,128]{1,0:T(8,128)}) custom-call(f32[11,2,32,128]{3,2,1,0:T(8,128)} %particles.5, s32[2,2,32,128]{3,2,1,0:T(8,128)} %pairs.5, s32[2,32]{1,0:T(2,128)} %count.5), custom_call_target="tpu_custom_call" | custom-call | tf_op jit(solution)/shard_map/pack_columns/pallas_call | solution.py:595
  1.8 0.0 copy-start.8
  1.8 0.0 copy-start.5
  1.8 2.6 %collective-permute-start = (f32[24,128]{1,0:T(8,128)}, f32[24,128]{1,0:T(8,128)S(1)}, u32[]{:S(2)}, u32[]{:S(2)}) collective-permute-start(f32[24,128]{1,0:T(8,128)} %get-tuple-element.24.sent_near), channel_id=1, source_target_pairs={{0,1},{1,0},{2,3},{3,2},{4,5},{5,4},{6,7},{7,6},{8,9},{9,8},{10,11... | collective-permute-start | bytes 36872 | tf_op jit(solution)/shard_map/ppermute | solution.py:576
  4.4 0.0 copy-start.4
  4.4 7.8 %collective-permute-start.1 = (f32[24,128]{1,0:T(8,128)}, f32[24,128]{1,0:T(8,128)S(1)}, u32[]{:S(2)}, u32[]{:S(2)}) collective-permute-start(f32[24,128]{1,0:T(8,128)} %get-tuple-element.25.sent_far), channel_id=1, source_target_pairs={{1,2},{2,1},{3,4},{4,3},{5,6},{6,5},{9,10},{10,9},{11,12},{12,11},... | collective-permute-start | bytes 36872 | tf_op jit(solution)/shard_map/ppermute | solution.py:576
  12.3 0.0 copy-done.8
  12.3 0.1 copy.8.counts
  12.4 0.0 copy-done.1
  12.4 0.0 copy-done
  12.4 0.0 copy-done.5
  12.4 0.0 copy-done.4
  12.4 0.0 copy-start.2
  12.4 0.0 copy-start.3
  12.4 2.2 %inner_terms.1 = (f32[512,128]{1,0:T(8,128)S(1)}, f32[512,128]{1,0:T(8,128)S(1)}, f32[376,128]{1,0:T(8,128)S(1)}, f32[376,128]{1,0:T(8,128)S(1)}, f32[11,2,56,12...) custom-call(f32[11,2,32,128]{3,2,1,0:T(8,128)S(1)} %copy-done, s32[2,2,32,128]{3,2,1,0:T(8,128)S(1)} %copy-done.1, ...), custom_call_target="tpu_custom_call" | custom-call | tf_op jit(solution)/shard_map/inner_terms/pallas_call | solution.py:613
  14.6 0.0 collective-permute-done.got_near
  14.6 0.0 collective-permute-done.1.got_far
  14.6 0.0 copy-done.2
  14.6 0.0 copy-done.3
  14.6 0.3 edge_terms.1
  15.0 3.1 %collective-permute-start.2 = (f32[376,128]{1,0:T(8,128)S(1)}, f32[376,128]{1,0:T(8,128)S(1)}, u32[]{:S(2)}, u32[]{:S(2)}) collective-permute-start(f32[376,128]{1,0:T(8,128)S(1)} %get-tuple-element.29), channel_id=1, source_target_pairs={{0,8},{8,0},{16,24},{24,16},{32,40},{40,32},{48,56},{56,48},{64,72... | collective-permute-start | bytes 577544 | tf_op jit(solution)/shard_map/ppermute | solution.py:576
  18.1 6.6 %collective-permute-start.3 = (f32[376,128]{1,0:T(8,128)S(1)}, f32[376,128]{1,0:T(8,128)S(1)}, u32[]{:S(2)}, u32[]{:S(2)}) collective-permute-start(f32[376,128]{1,0:T(8,128)S(1)} %get-tuple-element.30), channel_id=1, source_target_pairs={{8,16},{16,8},{24,32},{32,24},{40,48},{48,40},{56,64},{64,56},{72,... | collective-permute-start | bytes 577544 | tf_op jit(solution)/shard_map/ppermute | solution.py:576
  24.7 0.0 copy-start.6
  24.7 0.0 copy-start.7
  24.7 0.7 %copy-done.6 = s32[2,2,1,16]{3,2,1,0:T(1,128)S(1)} copy-done((s32[2,2,1,16]{3,2,1,0:T(1,128)S(1)}, s32[2,2,1,16]{3,2,1,0:T(1,128)}, u32[]{:S(2)}) %copy-start.6) | copy-done | bytes 280
  25.4 0.0 copy-done.7
  25.4 4.8 %own_sums.1 = (f32[2,7,32,128]{3,2,1,0:T(8,128)S(1)}, f32[11,2,56,128]{3,2,1,0:T(8,128)S(1)}, f32[11,40,128]{2,1,0:T(8,128)S(1)}, s32[3,40,128]{2,1,0:T(8,128)S(...) custom-call(f32[11,2,32,128]{3,2,1,0:T(8,128)S(1)} %copy-done, s32[2,2,32,128]{3,2,1,0:T(8,128)S(1)} %copy-done.1, ...), custom_call_target="tpu_custom_call" | custom-call | tf_op jit(solution)/shard_map/own_sums/pallas_call | solution.py:644
  30.2 0.0 collective-permute-done.2.near
  30.2 0.2 collective-permute-done.3.far
  30.4 6.1 %across_rows.1 = f32[11,2,32,128]{3,2,1,0:T(8,128)} custom-call(f32[376,128]{1,0:T(8,128)S(1)} %collective-permute-done.2.near, f32[376,128]{1,0:T(8,128)S(1)} %collective-permute-done.3.far, f32[2,7,32,128]{3,2,1,0:T(8,128)S(1)} %get-tuple-element.37.sums, f32[11,2,56,128]{3,2,1,0:T(8,128)S(1)} %get-tuple-element.38.ext, ...), custom_call_target="tpu_custom_call" | custom-call | tf_op jit(solution)/shard_map/across_rows/pallas_call | solution.py:663
Async XLA Ops:
  0.0 12.4 %copy-start.1 = (s32[2,2,32,128]{3,2,1,0:T(8,128)S(1)}, s32[2,2,32,128]{3,2,1,0:T(8,128)}, u32[]{:S(2)}) copy-start(s32[2,2,32,128]{3,2,1,0:T(8,128)} %pairs.5) | copy-start | bytes 196612
  0.0 12.4 %copy-start = (f32[11,2,32,128]{3,2,1,0:T(8,128)S(1)}, f32[11,2,32,128]{3,2,1,0:T(8,128)}, u32[]{:S(2)}) copy-start(f32[11,2,32,128]{3,2,1,0:T(8,128)} %particles.5) | copy-start | bytes 1081348
  1.8 10.5 %copy-start.8 = (s32[2,1,1]{0,2,1:T(1,128)S(1)}, s32[2,1,1]{0,2,1:T(1,128)}, u32[]{:S(2)}) copy-start(s32[2,1,1]{0,2,1:T(1,128)} %param.13) | copy-start | bytes 28
  1.8 10.5 %copy-start.5 = (s32[2,2,1,16]{3,2,1,0:T(1,128)S(1)}, s32[2,2,1,16]{3,2,1,0:T(1,128)}, u32[]{:S(2)}) copy-start(s32[2,2,1,16]{3,2,1,0:T(1,128)} %movers.3) | copy-start | bytes 772
  1.8 12.7 %collective-permute-start = (f32[24,128]{1,0:T(8,128)}, f32[24,128]{1,0:T(8,128)S(1)}, u32[]{:S(2)}, u32[]{:S(2)}) collective-permute-start(f32[24,128]{1,0:T(8,128)} %get-tuple-element.24.sent_near), channel_id=1, source_target_pairs={{0,1},{1,0},{2,3},{3,2},{4,5},{5,4},{6,7},{7,6},{8,9},{9,8},{10,11... | collective-permute-start | bytes 36872 | tf_op jit(solution)/shard_map/ppermute | solution.py:576
  4.4 7.9 %copy-start.4 = (s32[2,32]{1,0:T(2,128)S(1)}, s32[2,32]{1,0:T(2,128)}, u32[]{:S(2)}) copy-start(s32[2,32]{1,0:T(2,128)} %count.5) | copy-start | bytes 772
  4.4 10.2 %collective-permute-start.1 = (f32[24,128]{1,0:T(8,128)}, f32[24,128]{1,0:T(8,128)S(1)}, u32[]{:S(2)}, u32[]{:S(2)}) collective-permute-start(f32[24,128]{1,0:T(8,128)} %get-tuple-element.25.sent_far), channel_id=1, source_target_pairs={{1,2},{2,1},{3,4},{4,3},{5,6},{6,5},{9,10},{10,9},{11,12},{12,11},... | collective-permute-start | bytes 36872 | tf_op jit(solution)/shard_map/ppermute | solution.py:576
  12.4 2.2 %copy-start.2 = (f32[24,128]{1,0:T(8,128)S(1)}, f32[24,128]{1,0:T(8,128)}, u32[]{:S(2)}) copy-start(f32[24,128]{1,0:T(8,128)} %get-tuple-element.25.sent_far) | copy-start | bytes 36868
  12.4 2.2 %copy-start.3 = (f32[24,128]{1,0:T(8,128)S(1)}, f32[24,128]{1,0:T(8,128)}, u32[]{:S(2)}) copy-start(f32[24,128]{1,0:T(8,128)} %get-tuple-element.24.sent_near) | copy-start | bytes 36868
  15.0 15.3 %collective-permute-start.2 = (f32[376,128]{1,0:T(8,128)S(1)}, f32[376,128]{1,0:T(8,128)S(1)}, u32[]{:S(2)}, u32[]{:S(2)}) collective-permute-start(f32[376,128]{1,0:T(8,128)S(1)} %get-tuple-element.29), channel_id=1, source_target_pairs={{0,8},{8,0},{16,24},{24,16},{32,40},{40,32},{48,56},{56,48},{64,72... | collective-permute-start | bytes 577544 | tf_op jit(solution)/shard_map/ppermute | solution.py:576
  18.1 12.4 %collective-permute-start.3 = (f32[376,128]{1,0:T(8,128)S(1)}, f32[376,128]{1,0:T(8,128)S(1)}, u32[]{:S(2)}, u32[]{:S(2)}) collective-permute-start(f32[376,128]{1,0:T(8,128)S(1)} %get-tuple-element.30), channel_id=1, source_target_pairs={{8,16},{16,8},{24,32},{32,24},{40,48},{48,40},{56,64},{64,56},{72,... | collective-permute-start | bytes 577544 | tf_op jit(solution)/shard_map/ppermute | solution.py:576
  24.7 0.7 %copy-start.6 = (s32[2,2,1,16]{3,2,1,0:T(1,128)S(1)}, s32[2,2,1,16]{3,2,1,0:T(1,128)}, u32[]{:S(2)}) copy-start(s32[2,2,1,16]{3,2,1,0:T(1,128)} %arrivals.1) | copy-start | bytes 772
  24.7 0.7 %copy-start.7 = (s32[2,32]{1,0:T(2,128)S(1)}, s32[2,32]{1,0:T(2,128)}, u32[]{:S(2)}) copy-start(s32[2,32]{1,0:T(2,128)} %filled.1) | copy-start | bytes 772

commit v3 on v2

--- a/solution.py
+++ b/solution.py
@@ -113,8 +113,8 @@
     return jnp.where(hot, 1.0, 0.0).astype(jnp.bfloat16)
 
 
-def spread(left, first_row, second_row):
-    hot = jnp.concatenate([one_hot(first_row), one_hot(second_row)], 1)
+def spread(left, *index_rows):
+    hot = jnp.concatenate([one_hot(row) for row in index_rows], 1)
     out = lax.dot_general(
         halves(left), hot, (((1,), (1,)), ((), ())), preferred_element_type=jnp.float32
     )
@@ -200,7 +200,8 @@
 
 
 def inner_terms(
-    particles, pairs, count, movers, counts, on_first, on_second, to_near, to_far, ext, infos
+    particles, pairs, count, filled, movers, arrivals, counts,
+    on_first, on_second, to_near, to_far, ext, infos, stays, landing,
 ):
     lane = iota((COLS, LANES), 1)
     column = iota((COLS, LANES), 0)
@@ -238,6 +239,15 @@
 
     for r in range(2):
         slot, which = leavers(movers, counts, r)
+        live = lane < to_column(filled[r : r + 1, :], COLS)
+        stays[r] = jnp.where(live, jnp.where(lane != slot - 1, 2, 1), 0)
+        cells = to_column(lax.rem(arrivals[r, 0], COLS), 16)
+        slots = to_column(arrivals[r, 1], 16)
+        hit = slots == iota((16, LANES), 1)
+        number = jnp.sum(jnp.where(hit, iota((16, LANES), 0) + 1, 0), axis=0, keepdims=True) - 1
+        cell = jnp.sum(jnp.where(hit, cells, 0), axis=0, keepdims=True)
+        landing[8 * r : 8 * r + 1, :] = number
+        landing[8 * r + 1 : 8 * r + 2, :] = jnp.where(number >= 0, cell, -1)
         wide = jnp.broadcast_to(slot - 1, (COLS, LANES))
         first_index, heading, target = hits[r]
         own_first = first_index == wide
@@ -341,8 +351,8 @@
 
 
 def own_sums(
-    particles, pairs, count, filled, movers, counts, arrivals, on_first, on_second, edges, edge_first, edge_second,
-    ext_in, sums, ext, first_low, lists_low, stays, landing, by_source0, by_source1,
+    particles, pairs, count, on_first, on_second, edges, edge_first, edge_second,
+    ext_in, sums, ext, first_low, lists_low, by_source0, by_source1,
 ):
     ext[...] = ext_in[...]
     sizes = (40, 16)
@@ -366,7 +376,7 @@
             ref[pl.ds(pl.multiple_of((c + 1) * size, 8), size), :] = out
             return 0
 
-        lax.fori_loop(0, COLS, source, 0, unroll=4)
+        lax.fori_loop(0, COLS, source, 0, unroll=32)
     tile = [edges[j * 8 : j * 8 + 8, :] for j in range(COMPS)]
     first_index, second_index = unpacked(tile[:8])
     heading = second_index // LANES
@@ -423,150 +433,139 @@
     lists_low[2] = lax.rem(seconds, LANES)
     for j in range(COMPS):
         first_low[j] = pick(ext[j, 1, BASE : BASE + SLAB, :], rows)
-    for r in range(2):
-        slot, _ = leavers(movers, counts, r)
-        lane = iota((COLS, LANES), 1)
-        live = lane < to_column(filled[r : r + 1, :], COLS)
-        stays[r] = jnp.where(live, jnp.where(lane != slot - 1, 2, 1), 0)
-        cells = to_column(lax.rem(arrivals[r, 0], COLS), 16)
-        slots = to_column(arrivals[r, 1], 16)
-        hit = slots == iota((16, LANES), 1)
-        number = jnp.sum(jnp.where(hit, iota((16, LANES), 0) + 1, 0), axis=0, keepdims=True) - 1
-        cell = jnp.sum(jnp.where(hit, cells, 0), axis=0, keepdims=True)
-        landing[8 * r : 8 * r + 1, :] = number
-        landing[8 * r + 1 : 8 * r + 2, :] = jnp.where(number >= 0, cell, -1)
-
-
-def across_rows(
-    near, far, sums, ext, first_low, lists_low, stays, landing, out, around, on_first, on_second, indices, by_source
-):
-    turn = lax.rem(lax.axis_index("blade"), 2) == 1
+
+
+def surround(around, source):
     zeros = jnp.zeros((8, LANES), jnp.float32)
     for j in range(COMPS):
-        rows = slice(j * COLS, (j + 1) * COLS)
-        east, west = slice(EDGE + j, EDGE + j + 1), slice(EDGE + 12 + j, EDGE + 13 + j)
-        for side, (yes, no) in enumerate(((near, far), (far, near))):
-            main = jnp.where(turn, yes[rows, :], no[rows, :])
-            right = jnp.where(turn, yes[east, :], no[east, :])
-            left = jnp.where(turn, yes[west, :], no[west, :])
-            around[side, j, 40:48, :] = zeros
-            around[side, j, 8:40, :] = main
-            around[side, j, 40:41, :] = right
-            around[side, j, 41:42, :] = left
-            around[side, j, 42:43, :] = main[0:1]
-            around[side, j, 7:8, :] = left
+        main = source[j * COLS : (j + 1) * COLS, :]
+        right = source[EDGE + j : EDGE + j + 1, :]
+        left = source[EDGE + 12 + j : EDGE + 13 + j, :]
+        around[j, 40:48, :] = zeros
+        around[j, 8:40, :] = main
+        around[j, 40:41, :] = right
+        around[j, 41:42, :] = left
+        around[j, 42:43, :] = main[0:1]
+        around[j, 7:8, :] = left
+
+
+def row_terms(first, others, heading, target):
+    second = []
+    for j in range(COMPS):
+        value = None
+        for d in (1, 3, 4):
+            got = pick(others(j, col_steps[d]), target)
+            value = got if value is None else jnp.where(heading == d, got, value)
+        second.append(value)
+    listed = (heading == 1) | (heading == 3) | (heading == 4)
+    _, col_shift = shifts(heading)
+    return pair_terms(first, second, 1.0, col_shift, listed)
+
+
+def finish(side, info, state, leaving, totals, ext, stays, landing, write):
+    slot = lane_of(info, 7).astype(jnp.int32)
+    which = lane_of(info, 8).astype(jnp.int32)
+    leaves = slot > 0
+    leaving = [t + lane_of(info, j) for j, t in enumerate(leaving)]
+    at_slot = jnp.broadcast_to(jnp.maximum(slot - 1, 0), (COLS, LANES))
+    moved = stepped([pick(v, at_slot) for v in state], leaving, leaves)
+    moved[0] = moved[0] + (-1.0 if side == 0 else 1.0)
+    match = (which == landing[8 * side : 8 * side + 1, :]) & leaves
+    rows = stepped([ext[j, side, BASE : BASE + COLS, :] for j in range(COMPS)], totals, stays[side] > 0)
+    lands = iota((COLS, LANES), 0) == landing[8 * side + 1 : 8 * side + 2, :]
+    for j in range(COMPS):
+        value = jnp.sum(jnp.where(match, moved[j], 0.0), axis=0, keepdims=True)
+        write(side, j, jnp.where(lands, value, jnp.where(stays[side] == 1, 0.0, rows[j])))
+
+
+def from_behind(source, sums, ext, stays, landing, write, around, terms, indices, by_source):
+    surround(around, source)
     lane = iota((SLAB, LANES), 1)
-
-    def behind(j):
-        return around[0, j, BASE : BASE + SLAB, :]
-
-    def ahead(j):
-        return around[1, j, BASE : BASE + SLAB, :]
-
-    firsts_behind, seconds_behind = unpacked([behind(j) for j in range(8)])
-    heading_behind = jnp.where(lane < lane_of(behind(8), 0).astype(jnp.int32), seconds_behind // LANES, -1)
-    kept = []
-    for r in range(2):
-        if r == 0:
-            first = [pick(behind(j), firsts_behind) for j in range(COMPS)]
-            heading, target = heading_behind, lax.rem(seconds_behind, LANES)
-        else:
-            first = [first_low[j] for j in range(COMPS)]
-            heading, target = lists_low[1], lists_low[2]
-        second = []
-        for j in range(COMPS):
-            value = None
-            for d in (1, 3, 4):
-                at = BASE + col_steps[d]
-                others = ext[j, 0, at : at + SLAB, :] if r == 0 else around[1, j, at : at + SLAB, :]
-                got = pick(others, target)
-                value = got if value is None else jnp.where(heading == d, got, value)
-            second.append(value)
-        listed = (heading == 1) | (heading == 3) | (heading == 4)
-        _, col_shift = shifts(heading)
-        f, s = pair_terms(first, second, 1.0, col_shift, listed)
-        keep(on_first, r * 8 * SLAB, f)
-        keep(on_second, r * 8 * SLAB, s)
-        kept.append((heading, target))
-    indices[0] = kept[0][0]
-    indices[1] = kept[0][1]
-    blank = jnp.zeros((8, LANES), jnp.float32)
-
-    def source(c, _):
-        f = on_first[pl.ds(8 * SLAB + c, 8, stride=SLAB), :]
-        s = on_second[pl.ds(c, 8, stride=SLAB), :]
-        heading = indices[0, pl.ds(c, 1), :]
-        left = jnp.concatenate(
-            [jnp.concatenate([f, blank], 1)]
-            + [jnp.concatenate([blank, jnp.where(heading == d, s, 0.0)], 1) for d in (1, 3, 4)],
-            0,
-        )
-        got = spread(left, lists_low[0, pl.ds(c, 1), :], indices[1, pl.ds(c, 1), :])
-        by_source[pl.ds(pl.multiple_of((c + 1) * 32, 8), 32), :] = got
-        return 0
-
-    lax.fori_loop(0, SOURCES, source, 0, unroll=UNROLL)
-    by_source[0:32, :] = by_source[34 * 32 : 35 * 32, :]
-
-    placed = []
-    for side in range(2):
-        state_of = behind if side == 0 else ahead
-        info = state_of(9)[:COLS]
-        slot = lane_of(info, 7).astype(jnp.int32)
-        which = lane_of(info, 8).astype(jnp.int32)
-        leaves = slot > 0
-        leaving = []
-        if side == 0:
-            hit = firsts_behind[:COLS] == slot - 1
-            for j in range(7):
-                term = jnp.where(hit, on_first[j * SLAB : j * SLAB + COLS, :], 0.0)
-                leaving.append(jnp.sum(term, axis=1, keepdims=True))
-        else:
-            heading, target = kept[1]
-            wide = jnp.broadcast_to(slot - 1, (COLS, LANES))
-            wide = jnp.concatenate([wide, jnp.full((8, LANES), -1, jnp.int32)], 0)
-            up = roll_cells(wide, -1)
-            up = jnp.where(iota((SLAB, LANES), 0) == 33, wide[0:1], up)
-            masks = {
-                1: (heading == 1) & (target == wide),
-                3: (heading == 3) & (target == up),
-                4: (heading == 4) & (target == roll_cells(wide, 1)),
-            }
-            first_cell = iota((COLS, LANES), 0) == 0
-            for j in range(7):
-                term = on_second[(8 + j) * SLAB : (9 + j) * SLAB, :]
-                total = jnp.where(masks[1], term, 0.0)[:COLS]
-                slant = jnp.where(masks[3], term, 0.0)
-                slant = jnp.where(first_cell, slant[33:34], roll_cells(slant, 1)[:COLS])
-                total = total + slant + roll_cells(jnp.where(masks[4], term, 0.0), -1)[:COLS]
-                leaving.append(jnp.sum(total, axis=1, keepdims=True))
-        leaving = [t + lane_of(info, j) for j, t in enumerate(leaving)]
-        at_slot = jnp.broadcast_to(jnp.maximum(slot - 1, 0), (COLS, LANES))
-        state = [pick(state_of(j)[:COLS], at_slot) for j in range(COMPS)]
-        moved = stepped(state, leaving, leaves)
-        moved[0] = moved[0] + (-1.0 if side == 0 else 1.0)
-        match = (which == landing[8 * side : 8 * side + 1, :]) & leaves
-        placed.append([jnp.sum(jnp.where(match, m, 0.0), axis=0, keepdims=True) for m in moved])
-
-    column = iota((COLS, LANES), 0)
-    for r in range(2):
-        totals = []
-        for j in range(7):
-            total = sums[r, j]
-            if r == 0:
-                for k, shift in ((1, 0), (2, -1), (3, 1)):
-                    total = total + by_source[pl.ds((1 + shift) * 32 + k * 8 + j, COLS, stride=32), :]
-            else:
-                total = total + by_source[pl.ds(32 + j, COLS, stride=32), :]
-            totals.append(total)
-        state = [ext[j, r, BASE : BASE + COLS, :] for j in range(COMPS)]
-        rows = stepped(state, totals, stays[r] > 0)
-        lands = column == landing[8 * r + 1 : 8 * r + 2, :]
-        for j in range(COMPS):
-            out[j, r] = jnp.where(lands, placed[r][j], jnp.where(stays[r] == 1, 0.0, rows[j]))
-
-
-UNROLL = 2
+    rows = [around[j, BASE : BASE + SLAB, :] for j in range(COMPS)]
+    firsts, seconds = unpacked(rows[:8])
+    heading = jnp.where(lane < lane_of(rows[8], 0).astype(jnp.int32), seconds // LANES, -1)
+    target = lax.rem(seconds, LANES)
+    first = [pick(v, firsts) for v in rows]
+    f, s = row_terms(first, lambda j, k: ext[j, 0, BASE + k : BASE + k + SLAB, :], heading, target)
+    keep(terms, 0, s)
+    indices[0] = heading
+    indices[1] = target
+    for c in range(SOURCES):
+        term = terms[pl.ds(c, 8, stride=SLAB), :]
+        aim = indices[0, c : c + 1, :]
+        left = jnp.concatenate([jnp.where(aim == d, term, 0.0) for d in (1, 3, 4)], 0)
+        by_source[(c + 1) * 24 : (c + 2) * 24, :] = spread(left, indices[1, c : c + 1, :])
+    by_source[0:24, :] = by_source[34 * 24 : 35 * 24, :]
+    info = rows[9][:COLS]
+    hit = firsts[:COLS] == lane_of(info, 7).astype(jnp.int32) - 1
+    leaving = [jnp.sum(jnp.where(hit, f[j][:COLS], 0.0), axis=1, keepdims=True) for j in range(7)]
+    totals = []
+    for j in range(7):
+        total = sums[0, j]
+        for k, shift in ((0, 0), (1, -1), (2, 1)):
+            total = total + by_source[pl.ds((1 + shift) * 24 + k * 8 + j, COLS, stride=24), :]
+        totals.append(total)
+    state = [v[:COLS] for v in rows]
+    finish(0, info, state, leaving, totals, ext, stays, landing, write)
+
+
+def from_ahead(source, sums, ext, first_low, lists_low, stays, landing, write, around, terms, by_source):
+    surround(around, source)
+    heading, target = lists_low[1], lists_low[2]
+    first = [first_low[j] for j in range(COMPS)]
+    f, s = row_terms(first, lambda j, k: around[j, BASE + k : BASE + k + SLAB, :], heading, target)
+    keep(terms, 0, f)
+    for c in range(COLS):
+        by_source[c * 8 : c * 8 + 8, :] = spread(terms[pl.ds(c, 8, stride=SLAB), :], lists_low[0, c : c + 1, :])
+    info = around[9, BASE : BASE + COLS, :]
+    wide = jnp.broadcast_to(lane_of(info, 7).astype(jnp.int32) - 1, (COLS, LANES))
+    wide = jnp.concatenate([wide, jnp.full((8, LANES), -1, jnp.int32)], 0)
+    up = jnp.where(iota((SLAB, LANES), 0) == 33, wide[0:1], roll_cells(wide, -1))
+    straight = (heading == 1) & (target == wide)
+    slanting = (heading == 3) & (target == up)
+    back = (heading == 4) & (target == roll_cells(wide, 1))
+    first_cell = iota((COLS, LANES), 0) == 0
+    leaving = []
+    for j in range(7):
+        slant = jnp.where(slanting, s[j], 0.0)
+        slant = jnp.where(first_cell, slant[33:34], roll_cells(slant, 1)[:COLS])
+        total = jnp.where(straight, s[j], 0.0)[:COLS] + slant
+        total = total + roll_cells(jnp.where(back, s[j], 0.0), -1)[:COLS]
+        leaving.append(jnp.sum(total, axis=1, keepdims=True))
+    totals = [sums[1, j] + by_source[pl.ds(j, COLS, stride=8), :] for j in range(7)]
+    state = [around[j, BASE : BASE + COLS, :] for j in range(COMPS)]
+    finish(1, info, state, leaving, totals, ext, stays, landing, write)
+
+
+def far_row(far, sums, ext, first_low, lists_low, stays, landing, half, around, terms, indices, by_source):
+    odd = lax.rem(lax.axis_index("blade"), 2) == 1
+
+    def write(side, j, value):
+        half[j] = value
+
+    @pl.when(odd)
+    def _():
+        from_ahead(far, sums, ext, first_low, lists_low, stays, landing, write, around, terms, by_source)
+
+    @pl.when(jnp.logical_not(odd))
+    def _():
+        from_behind(far, sums, ext, stays, landing, write, around, terms, indices, by_source)
+
+
+def near_row(near, half, sums, ext, first_low, lists_low, stays, landing, out, around, terms, indices, by_source):
+    odd = lax.rem(lax.axis_index("blade"), 2) == 1
+
+    def write(side, j, value):
+        out[j, side] = value
+        out[j, 1 - side] = half[j]
+
+    @pl.when(odd)
+    def _():
+        from_behind(near, sums, ext, stays, landing, write, around, terms, indices, by_source)
+
+    @pl.when(jnp.logical_not(odd))
+    def _():
+        from_ahead(near, sums, ext, first_low, lists_low, stays, landing, write, around, terms, by_source)
 
 
 def swapped(block, axis, start):
@@ -605,15 +604,15 @@
             buffer(2, COLS, dtype=ints),
             pltpu.SemaphoreType.DMA((5,)),
         ],
-        compiler_params=pltpu.CompilerParams(vmem_limit_bytes=60 * 1024 * 1024),
+        compiler_params=params,
         name="pack_columns",
-    )(particles, contact_pairs, contact_count)
+    )(*(pltpu.with_memory_space_constraint(x, pltpu.HBM) for x in (particles, contact_pairs, contact_count)))
     got_far = swapped(far, "span", 1)
     got_near = swapped(near, "span", 0)
-    on_first, on_second, to_near, to_far, ext, infos = pl.pallas_call(
+    on_first, on_second, to_near, to_far, ext, infos, stays, landing = pl.pallas_call(
         inner_terms,
-        in_specs=[vmem] * 4 + [smem],
-        out_specs=[vmem] * 6,
+        in_specs=[vmem] * 6 + [smem],
+        out_specs=[vmem] * 8,
         out_shape=[
             shape(16 * COLS, LANES),
             shape(16 * COLS, LANES),
@@ -621,10 +620,12 @@
             shape(PAYLOAD, LANES),
             shape(COMPS, 2, EXT, LANES),
             shape(2, COLS, LANES),
+            shape(2, COLS, LANES, dtype=ints),
+            shape(16, LANES, dtype=ints),
         ],
         compiler_params=params,
         name="inner_terms",
-    )(particles, contact_pairs, contact_count, movers_out, move_count)
+    )(particles, contact_pairs, contact_count, filled, movers_out, movers_in, move_count)
     to_far, to_near, edges, edge_first, edge_second = pl.pallas_call(
         edge_terms,
         in_specs=[vmem] * 7,
@@ -641,40 +642,45 @@
     )(got_near, got_far, near, far, infos, to_near, to_far)
     row_far = swapped(to_far, "blade", 1)
     row_near = swapped(to_near, "blade", 0)
-    sums, ext, first_low, lists_low, stays, landing = pl.pallas_call(
+    sums, ext, first_low, lists_low = pl.pallas_call(
         own_sums,
-        in_specs=[vmem] * 5 + [smem] + [vmem] * 7,
-        out_specs=[vmem] * 6,
+        in_specs=[vmem] * 9,
+        out_specs=[vmem] * 4,
         out_shape=[
             shape(2, 7, COLS, LANES),
             shape(COMPS, 2, EXT, LANES),
             shape(COMPS, SLAB, LANES),
             shape(3, SLAB, LANES, dtype=ints),
-            shape(2, COLS, LANES, dtype=ints),
-            shape(16, LANES, dtype=ints),
         ],
         scratch_shapes=[buffer(34 * 40, LANES), buffer(34 * 16, LANES)],
         compiler_params=params,
         name="own_sums",
-    )(
-        particles, contact_pairs, contact_count, filled, movers_out, move_count, movers_in,
-        on_first, on_second, edges, edge_first, edge_second, ext,
-    )
+    )(particles, contact_pairs, contact_count, on_first, on_second, edges, edge_first, edge_second, ext)
+    own = (sums, ext, first_low, lists_low, stays, landing)
+    scratch = [
+        buffer(COMPS, EXT, LANES),
+        buffer(8 * SLAB, LANES),
+        buffer(2, SLAB, LANES, dtype=ints),
+        buffer(35 * 24, LANES),
+    ]
+    half = pl.pallas_call(
+        far_row,
+        in_specs=[vmem] * 7,
+        out_specs=vmem,
+        out_shape=shape(COMPS, COLS, LANES),
+        scratch_shapes=scratch,
+        compiler_params=params,
+        name="far_row",
+    )(row_far, *own)
     return pl.pallas_call(
-        across_rows,
+        near_row,
         in_specs=[vmem] * 8,
         out_specs=vmem,
         out_shape=shape(COMPS, 2, COLS, LANES),
-        scratch_shapes=[
-            buffer(2, COMPS, EXT, LANES),
-            buffer(16 * SLAB, LANES),
-            buffer(16 * SLAB, LANES),
-            buffer(2, SLAB, LANES, dtype=ints),
-            buffer(35 * 32, LANES),
-        ],
+        scratch_shapes=scratch,
         compiler_params=params,
-        name="across_rows",
-    )(row_near, row_far, sums, ext, first_low, lists_low, stays, landing)
+        name="near_row",
+    )(row_near, half, *own)
 
 
 def solution(mesh):

time: 36.8 us -> 30.8 us (0.84)
  Pallas kernels: 15.2 us -> 8.39 us
  waiting for transfers between devices: 0.21 us -> 2.18 us
  local copies, waits for them, and re-layouts: 0.81 us -> 0.13 us
  starting transfers between devices: 20.1 us -> 19.7 us
    pallas_call x3 -> x4, Pallas kernels: 13.1 us -> 6.86 us  [the longest x1 2.18 us: body(): pl.pallas_call(inner_terms, in_specs=[vmem] * 6 + [smem], out_specs=[vmem...]
    ppermute x4, waiting for transfers between devices: 0.21 us -> 2.18 us  [swapped(): return lax.ppermute(block, axis, pairs)]
    unnamed x19 -> x15, local copies, waits for them, and re-layouts: 0.81 us -> 0.13 us
    pallas_call x1, Pallas kernels: 1.8 us -> 1.2 us  [body(): pl.pallas_call(pack_columns, in_specs=[hbm] * 3, out_specs=[vmem] * 2, ou...]
    ppermute x4, starting transfers between devices: 20.1 us -> 19.7 us  [swapped(): return lax.ppermute(block, axis, pairs)]
  transfers between devices with their start and end apart: 4 -> 4, of which waited for: 1 -> 2; matrix products, arithmetic and copies ran while one was open for 0% -> 0% of each run, Pallas kernels for 19% -> 17%
where the time goes in v3:
time: 30.8 us; the launch traced here: 30.6 us
  starting transfers between devices  19.7 us (64%)
  Pallas kernels  8.39 us (27%)
  waiting for transfers between devices  2.18 us (7%)
    ppermute x4, starting transfers between devices, swapped(): return lax.ppermute(block, axis, pairs)  19.7 us
    pallas_call x1, Pallas kernels, body(): pl.pallas_call(inner_terms, in_specs=[vmem] * 6 + [smem], out_specs=[vmem...  2.18 us
    ppermute x4, waiting for transfers between devices, swapped(): return lax.ppermute(block, axis, pairs)  2.18 us
    pallas_call x1, Pallas kernels, body(): pl.pallas_call(own_sums, in_specs=[vmem] * 9, out_specs=[vmem] * 4, out_s...  1.9 us
    pallas_call x1, Pallas kernels, body(): pl.pallas_call(near_row, in_specs=[vmem] * 8, out_specs=vmem, out_shape=s...  1.56 us
    pallas_call x1, Pallas kernels, body(): pl.pallas_call(far_row, in_specs=[vmem] * 7, out_specs=vmem, out_shape=sh...  1.22 us
    pallas_call x1, Pallas kernels, body(): pl.pallas_call(pack_columns, in_specs=[hbm] * 3, out_specs=[vmem] * 2, ou...  1.2 us
  transfers between devices with their start and end apart: 4, of which 2 were waited for; matrix products, arithmetic and copies ran while one was open for 0% of the time, Pallas kernels for 17%

profile of v3, /device:TPU:161, one launch (start us, length us, event | category | flops | bytes accessed | tf_op | source)
XLA Modules:
  0.0 30.6 jit_solution(17215220217023649878)
XLA Ops:
  0.0 0.0 copy-start.1
  0.0 0.0 copy-start
  0.0 0.0 copy-start.5
  0.0 1.2 %pack_columns.1 = (f32[24,128]{1,0:T(8,128)S(1)}, f32[24,128]{1,0:T(8,128)S(1)}) custom-call(f32[11,2,32,128]{3,2,1,0:T(8,128)} %particles.5, s32[2,2,32,128]{3,2,1,0:T(8,128)} %pairs.5, s32[2,32]{1,0:T(2,128)} %count.5), custom_call_target="tpu_custom_call" | custom-call | tf_op jit(solution)/shard_map/pack_columns/pallas_call | solution.py:594
  1.2 0.0 copy-start.6
  1.2 0.0 copy-start.4
  1.2 0.0 copy-start.3
  1.3 2.7 %collective-permute-start = (f32[24,128]{1,0:T(8,128)S(1)}, f32[24,128]{1,0:T(8,128)S(1)}, u32[]{:S(2)}, u32[]{:S(2)}) collective-permute-start(f32[24,128]{1,0:T(8,128)S(1)} %get-tuple-element.24.sent_near), channel_id=1, source_target_pairs={{0,1},{1,0},{2,3},{3,2},{4,5},{5,4},{6,7},{7,6},{8,9},{9,8},{10,11... | collective-permute-start | bytes 36872 | tf_op jit(solution)/shard_map/ppermute | solution.py:575
  4.0 0.0 copy-start.2
  4.0 7.8 %collective-permute-start.1 = (f32[24,128]{1,0:T(8,128)S(1)}, f32[24,128]{1,0:T(8,128)S(1)}, u32[]{:S(2)}, u32[]{:S(2)}) collective-permute-start(f32[24,128]{1,0:T(8,128)S(1)} %get-tuple-element.25.sent_far), channel_id=1, source_target_pairs={{1,2},{2,1},{3,4},{4,3},{5,6},{6,5},{9,10},{10,9},{11,12},{12,11},... | collective-permute-start | bytes 36872 | tf_op jit(solution)/shard_map/ppermute | solution.py:575
  11.8 0.0 copy-done.6
  11.8 0.1 copy.8.counts
  11.9 0.0 copy-done.1
  11.9 0.0 copy-done
  11.9 0.0 copy-done.5
  11.9 0.0 copy-done.4
  11.9 0.0 copy-done.3
  11.9 0.0 copy-done.2
  12.0 2.2 %inner_terms.1 = (f32[512,128]{1,0:T(8,128)S(1)}, f32[512,128]{1,0:T(8,128)S(1)}, f32[376,128]{1,0:T(8,128)S(1)}, f32[376,128]{1,0:T(8,128)S(1)}, f32[11,2,56,12...) custom-call(f32[11,2,32,128]{3,2,1,0:T(8,128)S(1)} %copy-done, ...), custom_call_target="tpu_custom_call" | custom-call | tf_op jit(solution)/shard_map/inner_terms/pallas_call | solution.py:612
  14.1 0.0 collective-permute-done.got_near
  14.1 0.0 collective-permute-done.1.got_far
  14.2 0.3 %edge_terms.1 = (f32[376,128]{1,0:T(8,128)S(1)}, f32[376,128]{1,0:T(8,128)S(1)}, f32[96,128]{1,0:T(8,128)S(1)}, f32[64,128]{1,0:T(8,128)S(1)}, f32[64,128]{1,0:T(8,128)S(1)}) custom-call(f32[24,128]{1,0:T(8,128)S(1)} %collective-permute-done.got_near, f32[24,128]{1,0:T(8,128)S(1)} %collective-permute-done.1.got_far, ...), custom_call_target="tpu_custom_call" | custom-call | tf_op jit(solution)/shard_map/edge_terms/pallas_call | solution.py:629
  14.5 7.3 %collective-permute-start.3 = (f32[376,128]{1,0:T(8,128)S(1)}, f32[376,128]{1,0:T(8,128)S(1)}, u32[]{:S(2)}, u32[]{:S(2)}) collective-permute-start(f32[376,128]{1,0:T(8,128)S(1)} %get-tuple-element.30), channel_id=1, source_target_pairs={{8,16},{16,8},{24,32},{32,24},{40,48},{48,40},{56,64},{64,56},{72,... | collective-permute-start | bytes 577544 | tf_op jit(solution)/shard_map/ppermute | solution.py:575
  21.8 1.9 %collective-permute-start.2 = (f32[376,128]{1,0:T(8,128)S(1)}, f32[376,128]{1,0:T(8,128)S(1)}, u32[]{:S(2)}, u32[]{:S(2)}) collective-permute-start(f32[376,128]{1,0:T(8,128)S(1)} %get-tuple-element.29), channel_id=1, source_target_pairs={{0,8},{8,0},{16,24},{24,16},{32,40},{40,32},{48,56},{56,48},{64,72... | collective-permute-start | bytes 577544 | tf_op jit(solution)/shard_map/ppermute | solution.py:575
  23.7 1.9 %own_sums.1 = (f32[2,7,32,128]{3,2,1,0:T(8,128)S(1)}, f32[11,2,56,128]{3,2,1,0:T(8,128)S(1)}, f32[11,40,128]{2,1,0:T(8,128)S(1)}, s32[3,40,128]{2,1,0:T(8,128)S(1)}) custom-call(f32[11,2,32,128]{3,2,1,0:T(8,128)S(1)} %copy-done, s32[2,2,32,128]{3,2,1,0:T(8,128)S(1)} %copy-done.1, s32[2,32]{1,0:T(2,128)S(1)} %copy-done.2, ...), custom_call_target="tpu_custom_call" | custom-call | tf_op jit(solution)/shard_map/own_sums/pallas_call | solution.py:645
  25.6 0.7 %collective-permute-done.3.far = f32[376,128]{1,0:T(8,128)S(1)} collective-permute-done((f32[376,128]{1,0:T(8,128)S(1)}, f32[376,128]{1,0:T(8,128)S(1)}, u32[]{:S(2)}, u32[]{:S(2)}) %collective-permute-start.3) | collective-permute-done | bytes 192544 | tf_op jit(solution)/shard_map/ppermute | solution.py:575
  26.4 1.2 %far_row.1.half = f32[11,32,128]{2,1,0:T(8,128)S(1)} custom-call(f32[376,128]{1,0:T(8,128)S(1)} %collective-permute-done.3.far, f32[2,7,32,128]{3,2,1,0:T(8,128)S(1)} %get-tuple-element.37.sums, f32[11,2,56,128]{3,2,1,0:T(8,128)S(1)} %get-tuple-element.38.ext, f32[11,40,128]{2,1,0:T(8,128)S(1)} %get-tuple-element.39.first_low, ...), custom_call_target="tpu_custom_call" | custom-call | tf_op jit(solution)/shard_map/far_row/pallas_call | solution.py:666
  27.6 1.4 %collective-permute-done.2.near = f32[376,128]{1,0:T(8,128)S(1)} collective-permute-done((f32[376,128]{1,0:T(8,128)S(1)}, f32[376,128]{1,0:T(8,128)S(1)}, u32[]{:S(2)}, u32[]{:S(2)}) %collective-permute-start.2) | collective-permute-done | bytes 192544 | tf_op jit(solution)/shard_map/ppermute | solution.py:575
  29.0 1.6 %near_row.1 = f32[11,2,32,128]{3,2,1,0:T(8,128)} custom-call(f32[376,128]{1,0:T(8,128)S(1)} %collective-permute-done.2.near, f32[11,32,128]{2,1,0:T(8,128)S(1)} %far_row.1.half, f32[2,7,32,128]{3,2,1,0:T(8,128)S(1)} %get-tuple-element.37.sums, f32[11,2,56,128]{3,2,1,0:T(8,128)S(1)} %get-tuple-element.38.ext, f32[11,40,128]{2,1,0:T(8,128)S(1)} %get-tuple-element.39.first_low, ...), custom_call_target="tpu_custom_call" | custom-call | tf_op jit(solution)/shard_map/near_row/pallas_call | solution.py:675
Async XLA Ops:
  0.0 11.9 %copy-start.1 = (s32[2,2,32,128]{3,2,1,0:T(8,128)S(1)}, s32[2,2,32,128]{3,2,1,0:T(8,128)}, u32[]{:S(2)}) copy-start(s32[2,2,32,128]{3,2,1,0:T(8,128)} %pairs.5) | copy-start | bytes 196612
  0.0 11.9 %copy-start = (f32[11,2,32,128]{3,2,1,0:T(8,128)S(1)}, f32[11,2,32,128]{3,2,1,0:T(8,128)}, u32[]{:S(2)}) copy-start(f32[11,2,32,128]{3,2,1,0:T(8,128)} %particles.5) | copy-start | bytes 1081348
  0.0 11.9 %copy-start.5 = (s32[2,32]{1,0:T(2,128)S(1)}, s32[2,32]{1,0:T(2,128)}, u32[]{:S(2)}) copy-start(s32[2,32]{1,0:T(2,128)} %filled.1) | copy-start | bytes 772
  1.2 10.6 %copy-start.6 = (s32[2,1,1]{0,2,1:T(1,128)S(1)}, s32[2,1,1]{0,2,1:T(1,128)}, u32[]{:S(2)}) copy-start(s32[2,1,1]{0,2,1:T(1,128)} %param.13) | copy-start | bytes 28
  1.2 10.7 %copy-start.4 = (s32[2,2,1,16]{3,2,1,0:T(1,128)S(1)}, s32[2,2,1,16]{3,2,1,0:T(1,128)}, u32[]{:S(2)}) copy-start(s32[2,2,1,16]{3,2,1,0:T(1,128)} %arrivals.1) | copy-start | bytes 772
  1.2 10.7 %copy-start.3 = (s32[2,2,1,16]{3,2,1,0:T(1,128)S(1)}, s32[2,2,1,16]{3,2,1,0:T(1,128)}, u32[]{:S(2)}) copy-start(s32[2,2,1,16]{3,2,1,0:T(1,128)} %movers.1) | copy-start | bytes 772
  1.3 12.9 %collective-permute-start = (f32[24,128]{1,0:T(8,128)S(1)}, f32[24,128]{1,0:T(8,128)S(1)}, u32[]{:S(2)}, u32[]{:S(2)}) collective-permute-start(f32[24,128]{1,0:T(8,128)S(1)} %get-tuple-element.24.sent_near), channel_id=1, source_target_pairs={{0,1},{1,0},{2,3},{3,2},{4,5},{5,4},{6,7},{7,6},{8,9},{9,8},{10,11... | collective-permute-start | bytes 36872 | tf_op jit(solution)/shard_map/ppermute | solution.py:575
  4.0 8.0 %copy-start.2 = (s32[2,32]{1,0:T(2,128)S(1)}, s32[2,32]{1,0:T(2,128)}, u32[]{:S(2)}) copy-start(s32[2,32]{1,0:T(2,128)} %count.5) | copy-start | bytes 772
  4.0 10.2 %collective-permute-start.1 = (f32[24,128]{1,0:T(8,128)S(1)}, f32[24,128]{1,0:T(8,128)S(1)}, u32[]{:S(2)}, u32[]{:S(2)}) collective-permute-start(f32[24,128]{1,0:T(8,128)S(1)} %get-tuple-element.25.sent_far), channel_id=1, source_target_pairs={{1,2},{2,1},{3,4},{4,3},{5,6},{6,5},{9,10},{10,9},{11,12},{12,11},... | collective-permute-start | bytes 36872 | tf_op jit(solution)/shard_map/ppermute | solution.py:575
  14.5 11.9 %collective-permute-start.3 = (f32[376,128]{1,0:T(8,128)S(1)}, f32[376,128]{1,0:T(8,128)S(1)}, u32[]{:S(2)}, u32[]{:S(2)}) collective-permute-start(f32[376,128]{1,0:T(8,128)S(1)} %get-tuple-element.30), channel_id=1, source_target_pairs={{8,16},{16,8},{24,32},{32,24},{40,48},{48,40},{56,64},{64,56},{72,... | collective-permute-start | bytes 577544 | tf_op jit(solution)/shard_map/ppermute | solution.py:575
  21.8 7.2 %collective-permute-start.2 = (f32[376,128]{1,0:T(8,128)S(1)}, f32[376,128]{1,0:T(8,128)S(1)}, u32[]{:S(2)}, u32[]{:S(2)}) collective-permute-start(f32[376,128]{1,0:T(8,128)S(1)} %get-tuple-element.29), channel_id=1, source_target_pairs={{0,8},{8,0},{16,24},{24,16},{32,40},{40,32},{48,56},{56,48},{64,72... | collective-permute-start | bytes 577544 | tf_op jit(solution)/shard_map/ppermute | solution.py:575

commit v4 on v3

--- a/solution.py
+++ b/solution.py
@@ -154,11 +154,11 @@
 
 
 def pack_columns(particles, pairs, count, far, near, p_west, p_east, c_west, c_east, n_all, sems):
-    last = COLS - 8
+    last = COLS - 1
     copies = [
-        pltpu.make_async_copy(particles.at[:, :, 0:8, :], p_west, sems.at[0]),
+        pltpu.make_async_copy(particles.at[:, :, 0:1, :], p_west, sems.at[0]),
         pltpu.make_async_copy(particles.at[:, :, last:COLS, :], p_east, sems.at[1]),
-        pltpu.make_async_copy(pairs.at[:, :, 0:8, :], c_west, sems.at[2]),
+        pltpu.make_async_copy(pairs.at[:, :, 0:1, :], c_west, sems.at[2]),
         pltpu.make_async_copy(pairs.at[:, :, last:COLS, :], c_east, sems.at[3]),
         pltpu.make_async_copy(count, n_all, sems.at[4]),
     ]
@@ -172,7 +172,7 @@
     for r in range(2):
         n_row = n_all[r : r + 1, :]
         sides = []
-        for p, c, at, cell in ((p_west, c_west, 0, 0), (p_east, c_east, 7, COLS - 1)):
+        for p, c, at, cell in ((p_west, c_west, 0, 0), (p_east, c_east, 0, COLS - 1)):
             n = jnp.sum(jnp.where(iota((1, COLS), 1) == cell, n_row, 0), axis=1, keepdims=True)
             lists = [c[k, r, at : at + 1, :] for k in range(2)]
             sides.append([packed(j, p[j, r, at : at + 1, :], lists, n, None) for j in range(COMPS)])
@@ -222,19 +222,26 @@
         listed = (lane < counted[r]) & ~outside
         if r == 1:
             listed = listed & ((heading == 0) | (heading == 2))
-        first = [pick(particles[j, r], first_index) for j in range(COMPS)]
-        second = []
-        for j in range(COMPS):
-            value = None
-            for d in headings:
-                at = BASE + col_steps[d]
-                got = pick(ext[j, r + row_steps[d], at : at + COLS, :], target)
-                value = got if value is None else jnp.where(heading == d, got, value)
-            second.append(value)
         row_shift, col_shift = shifts(heading)
-        f, s = pair_terms(first, second, row_shift, col_shift, listed)
-        keep(on_first, r * 8 * COLS, f)
-        keep(on_second, r * 8 * COLS, s)
+        for g in range(0, COLS, 8):
+            rows = slice(g, g + 8)
+            first = [pick(particles[j, r, rows, :], first_index[rows]) for j in range(COMPS)]
+            second = []
+            for j in range(COMPS):
+                value = None
+                for d in headings:
+                    at = BASE + col_steps[d] + g
+                    got = pick(ext[j, r + row_steps[d], at : at + 8, :], target[rows])
+                    value = got if value is None else jnp.where(heading[rows] == d, got, value)
+                second.append(value)
+            f, s = pair_terms(first, second, row_shift[rows], col_shift[rows], listed[rows])
+            for ref, terms in ((on_first, f), (on_second, s)):
+                for j in range(7):
+                    at = (r * 8 + j) * COLS + g
+                    ref[at : at + 8, :] = terms[j]
+        for ref in (on_first, on_second):
+            at = (r * 8 + 7) * COLS
+            ref[at : at + COLS, :] = jnp.zeros((COLS, LANES), jnp.float32)
         hits.append((first_index, heading, target))
 
     for r in range(2):
@@ -450,16 +457,21 @@
 
 
 def row_terms(first, others, heading, target):
-    second = []
-    for j in range(COMPS):
-        value = None
-        for d in (1, 3, 4):
-            got = pick(others(j, col_steps[d]), target)
-            value = got if value is None else jnp.where(heading == d, got, value)
-        second.append(value)
-    listed = (heading == 1) | (heading == 3) | (heading == 4)
     _, col_shift = shifts(heading)
-    return pair_terms(first, second, 1.0, col_shift, listed)
+    pieces = []
+    for g in range(0, SLAB, 8):
+        rows = slice(g, g + 8)
+        aim = heading[rows]
+        second = []
+        for j in range(COMPS):
+            value = None
+            for d in (1, 3, 4):
+                got = pick(others(j, BASE + col_steps[d] + g), target[rows])
+                value = got if value is None else jnp.where(aim == d, got, value)
+            second.append(value)
+        listed = (aim == 1) | (aim == 3) | (aim == 4)
+        pieces.append(pair_terms([first(j, rows) for j in range(COMPS)], second, 1.0, col_shift[rows], listed))
+    return [[jnp.concatenate([piece[k][j] for piece in pieces], 0) for j in range(7)] for k in range(2)]
 
 
 def finish(side, info, state, leaving, totals, ext, stays, landing, write):
@@ -485,8 +497,9 @@
     firsts, seconds = unpacked(rows[:8])
     heading = jnp.where(lane < lane_of(rows[8], 0).astype(jnp.int32), seconds // LANES, -1)
     target = lax.rem(seconds, LANES)
-    first = [pick(v, firsts) for v in rows]
-    f, s = row_terms(first, lambda j, k: ext[j, 0, BASE + k : BASE + k + SLAB, :], heading, target)
+    f, s = row_terms(
+        lambda j, at: pick(rows[j][at], firsts[at]), lambda j, at: ext[j, 0, at : at + 8, :], heading, target
+    )
     keep(terms, 0, s)
     indices[0] = heading
     indices[1] = target
@@ -512,8 +525,9 @@
 def from_ahead(source, sums, ext, first_low, lists_low, stays, landing, write, around, terms, by_source):
     surround(around, source)
     heading, target = lists_low[1], lists_low[2]
-    first = [first_low[j] for j in range(COMPS)]
-    f, s = row_terms(first, lambda j, k: around[j, BASE + k : BASE + k + SLAB, :], heading, target)
+    f, s = row_terms(
+        lambda j, at: first_low[j, at, :], lambda j, at: around[j, at : at + 8, :], heading, target
+    )
     keep(terms, 0, f)
     for c in range(COLS):
         by_source[c * 8 : c * 8 + 8, :] = spread(terms[pl.ds(c, 8, stride=SLAB), :], lists_low[0, c : c + 1, :])
@@ -597,10 +611,10 @@
         out_specs=[vmem] * 2,
         out_shape=[shape(24, LANES)] * 2,
         scratch_shapes=[
-            buffer(COMPS, 2, 8, LANES),
-            buffer(COMPS, 2, 8, LANES),
-            buffer(2, 2, 8, LANES, dtype=ints),
-            buffer(2, 2, 8, LANES, dtype=ints),
+            buffer(COMPS, 2, 1, LANES),
+            buffer(COMPS, 2, 1, LANES),
+            buffer(2, 2, 1, LANES, dtype=ints),
+            buffer(2, 2, 1, LANES, dtype=ints),
             buffer(2, COLS, dtype=ints),
             pltpu.SemaphoreType.DMA((5,)),
         ],

time: 30.8 us -> 30.6 us (level)
  the two profiles are of different devices: /device:TPU:161 before, /device:TPU:352 now
where the time goes in v4:
time: 30.6 us; the launch traced here: 30.3 us
  starting transfers between devices  15 us (49%)
  waiting for transfers between devices  7.58 us (25%)
  Pallas kernels  7.5 us (25%)
    ppermute x4, starting transfers between devices, swapped(): return lax.ppermute(block, axis, pairs)  15 us
    ppermute x4, waiting for transfers between devices, swapped(): return lax.ppermute(block, axis, pairs)  7.58 us
    pallas_call x1, Pallas kernels, body(): pl.pallas_call(own_sums, in_specs=[vmem] * 9, out_specs=[vmem] * 4, out_s...  1.9 us
    pallas_call x1, Pallas kernels, body(): pl.pallas_call(near_row, in_specs=[vmem] * 8, out_specs=vmem, out_shape=s...  1.56 us
    pallas_call x1, Pallas kernels, body(): pl.pallas_call(inner_terms, in_specs=[vmem] * 6 + [smem], out_specs=[vmem...  1.53 us
    pallas_call x1, Pallas kernels, body(): pl.pallas_call(far_row, in_specs=[vmem] * 7, out_specs=vmem, out_shape=sh...  1.18 us
    pallas_call x1, Pallas kernels, body(): pl.pallas_call(pack_columns, in_specs=[hbm] * 3, out_specs=[vmem] * 2, ou...  1 us
  transfers between devices with their start and end apart: 4, of which 3 were waited for; matrix products, arithmetic and copies ran while one was open for 0% of the time, Pallas kernels for 15%

profile of v4, /device:TPU:352, one launch (start us, length us, event | category | flops | bytes accessed | tf_op | source)
XLA Modules:
  0.0 30.3 jit_solution(16827437763258566959)
XLA Ops:
  0.0 0.0 copy-start.1
  0.0 0.0 copy-start
  0.0 0.0 copy-start.5
  0.0 1.0 %pack_columns.1 = (f32[24,128]{1,0:T(8,128)S(1)}, f32[24,128]{1,0:T(8,128)S(1)}) custom-call(f32[11,2,32,128]{3,2,1,0:T(8,128)} %particles.5, s32[2,2,32,128]{3,2,1,0:T(8,128)} %pairs.5, s32[2,32]{1,0:T(2,128)} %count.5), custom_call_target="tpu_custom_call" | custom-call | tf_op jit(solution)/shard_map/pack_columns/pallas_call | solution.py:608
  1.0 0.0 copy-start.6
  1.0 0.0 copy-start.4
  1.0 0.0 copy-start.3
  1.1 2.1 %collective-permute-start = (f32[24,128]{1,0:T(8,128)S(1)}, f32[24,128]{1,0:T(8,128)S(1)}, u32[]{:S(2)}, u32[]{:S(2)}) collective-permute-start(f32[24,128]{1,0:T(8,128)S(1)} %get-tuple-element.24.sent_near), channel_id=1, source_target_pairs={{0,1},{1,0},{2,3},{3,2},{4,5},{5,4},{6,7},{7,6},{8,9},{9,8},{10,11... | collective-permute-start | bytes 36872 | tf_op jit(solution)/shard_map/ppermute | solution.py:589
  3.1 0.0 copy-start.2
  3.1 3.5 %collective-permute-start.1 = (f32[24,128]{1,0:T(8,128)S(1)}, f32[24,128]{1,0:T(8,128)S(1)}, u32[]{:S(2)}, u32[]{:S(2)}) collective-permute-start(f32[24,128]{1,0:T(8,128)S(1)} %get-tuple-element.25.sent_far), channel_id=1, source_target_pairs={{1,2},{2,1},{3,4},{4,3},{5,6},{6,5},{9,10},{10,9},{11,12},{12,11},... | collective-permute-start | bytes 36872 | tf_op jit(solution)/shard_map/ppermute | solution.py:589
  6.6 0.0 copy-done.6
  6.6 0.1 copy.8.counts
  6.7 0.0 copy-done.1
  6.7 0.0 copy-done
  6.7 0.0 copy-done.5
  6.7 0.0 copy-done.4
  6.7 0.0 copy-done.3
  6.7 0.0 copy-done.2
  6.7 1.5 %inner_terms.1 = (f32[512,128]{1,0:T(8,128)S(1)}, f32[512,128]{1,0:T(8,128)S(1)}, f32[376,128]{1,0:T(8,128)S(1)}, f32[376,128]{1,0:T(8,128)S(1)}, f32[11,2,56,12...) custom-call(f32[11,2,32,128]{3,2,1,0:T(8,128)S(1)} %copy-done, ...), custom_call_target="tpu_custom_call" | custom-call | tf_op jit(solution)/shard_map/inner_terms/pallas_call | solution.py:626
  8.3 0.0 collective-permute-done.got_near
  8.3 3.8 %collective-permute-done.1.got_far = f32[24,128]{1,0:T(8,128)S(1)} collective-permute-done((f32[24,128]{1,0:T(8,128)S(1)}, f32[24,128]{1,0:T(8,128)S(1)}, u32[]{:S(2)}, u32[]{:S(2)}) %collective-permute-start.1) | collective-permute-done | bytes 12320 | tf_op jit(solution)/shard_map/ppermute | solution.py:589
  12.0 0.3 %edge_terms.1 = (f32[376,128]{1,0:T(8,128)S(1)}, f32[376,128]{1,0:T(8,128)S(1)}, f32[96,128]{1,0:T(8,128)S(1)}, f32[64,128]{1,0:T(8,128)S(1)}, f32[64,128]{1,0:T(8,128)S(1)}) custom-call(f32[24,128]{1,0:T(8,128)S(1)} %collective-permute-done.got_near, f32[24,128]{1,0:T(8,128)S(1)} %collective-permute-done.1.got_far, ...), custom_call_target="tpu_custom_call" | custom-call | tf_op jit(solution)/shard_map/edge_terms/pallas_call | solution.py:643
  12.4 7.6 %collective-permute-start.3 = (f32[376,128]{1,0:T(8,128)S(1)}, f32[376,128]{1,0:T(8,128)S(1)}, u32[]{:S(2)}, u32[]{:S(2)}) collective-permute-start(f32[376,128]{1,0:T(8,128)S(1)} %get-tuple-element.30), channel_id=1, source_target_pairs={{8,16},{16,8},{24,32},{32,24},{40,48},{48,40},{56,64},{64,56},{72,... | collective-permute-start | bytes 577544 | tf_op jit(solution)/shard_map/ppermute | solution.py:589
  20.0 1.9 %collective-permute-start.2 = (f32[376,128]{1,0:T(8,128)S(1)}, f32[376,128]{1,0:T(8,128)S(1)}, u32[]{:S(2)}, u32[]{:S(2)}) collective-permute-start(f32[376,128]{1,0:T(8,128)S(1)} %get-tuple-element.29), channel_id=1, source_target_pairs={{0,8},{8,0},{16,24},{24,16},{32,40},{40,32},{48,56},{56,48},{64,72... | collective-permute-start | bytes 577544 | tf_op jit(solution)/shard_map/ppermute | solution.py:589
  21.9 1.9 %own_sums.1 = (f32[2,7,32,128]{3,2,1,0:T(8,128)S(1)}, f32[11,2,56,128]{3,2,1,0:T(8,128)S(1)}, f32[11,40,128]{2,1,0:T(8,128)S(1)}, s32[3,40,128]{2,1,0:T(8,128)S(1)}) custom-call(f32[11,2,32,128]{3,2,1,0:T(8,128)S(1)} %copy-done, s32[2,2,32,128]{3,2,1,0:T(8,128)S(1)} %copy-done.1, s32[2,32]{1,0:T(2,128)S(1)} %copy-done.2, ...), custom_call_target="tpu_custom_call" | custom-call | tf_op jit(solution)/shard_map/own_sums/pallas_call | solution.py:659
  23.8 1.9 %collective-permute-done.3.far = f32[376,128]{1,0:T(8,128)S(1)} collective-permute-done((f32[376,128]{1,0:T(8,128)S(1)}, f32[376,128]{1,0:T(8,128)S(1)}, u32[]{:S(2)}, u32[]{:S(2)}) %collective-permute-start.3) | collective-permute-done | bytes 192544 | tf_op jit(solution)/shard_map/ppermute | solution.py:589
  25.7 1.2 %far_row.1.half = f32[11,32,128]{2,1,0:T(8,128)S(1)} custom-call(f32[376,128]{1,0:T(8,128)S(1)} %collective-permute-done.3.far, f32[2,7,32,128]{3,2,1,0:T(8,128)S(1)} %get-tuple-element.37.sums, f32[11,2,56,128]{3,2,1,0:T(8,128)S(1)} %get-tuple-element.38.ext, f32[11,40,128]{2,1,0:T(8,128)S(1)} %get-tuple-element.39.first_low, ...), custom_call_target="tpu_custom_call" | custom-call | tf_op jit(solution)/shard_map/far_row/pallas_call | solution.py:680
  26.9 1.9 %collective-permute-done.2.near = f32[376,128]{1,0:T(8,128)S(1)} collective-permute-done((f32[376,128]{1,0:T(8,128)S(1)}, f32[376,128]{1,0:T(8,128)S(1)}, u32[]{:S(2)}, u32[]{:S(2)}) %collective-permute-start.2) | collective-permute-done | bytes 192544 | tf_op jit(solution)/shard_map/ppermute | solution.py:589
  28.8 1.6 %near_row.1 = f32[11,2,32,128]{3,2,1,0:T(8,128)} custom-call(f32[376,128]{1,0:T(8,128)S(1)} %collective-permute-done.2.near, f32[11,32,128]{2,1,0:T(8,128)S(1)} %far_row.1.half, f32[2,7,32,128]{3,2,1,0:T(8,128)S(1)} %get-tuple-element.37.sums, f32[11,2,56,128]{3,2,1,0:T(8,128)S(1)} %get-tuple-element.38.ext, f32[11,40,128]{2,1,0:T(8,128)S(1)} %get-tuple-element.39.first_low, ...), custom_call_target="tpu_custom_call" | custom-call | tf_op jit(solution)/shard_map/near_row/pallas_call | solution.py:689
Async XLA Ops:
  0.0 6.7 %copy-start.1 = (s32[2,2,32,128]{3,2,1,0:T(8,128)S(1)}, s32[2,2,32,128]{3,2,1,0:T(8,128)}, u32[]{:S(2)}) copy-start(s32[2,2,32,128]{3,2,1,0:T(8,128)} %pairs.5) | copy-start | bytes 196612
  0.0 6.7 %copy-start = (f32[11,2,32,128]{3,2,1,0:T(8,128)S(1)}, f32[11,2,32,128]{3,2,1,0:T(8,128)}, u32[]{:S(2)}) copy-start(f32[11,2,32,128]{3,2,1,0:T(8,128)} %particles.5) | copy-start | bytes 1081348
  0.0 6.7 %copy-start.5 = (s32[2,32]{1,0:T(2,128)S(1)}, s32[2,32]{1,0:T(2,128)}, u32[]{:S(2)}) copy-start(s32[2,32]{1,0:T(2,128)} %filled.1) | copy-start | bytes 772
  1.0 5.6 %copy-start.6 = (s32[2,1,1]{0,2,1:T(1,128)S(1)}, s32[2,1,1]{0,2,1:T(1,128)}, u32[]{:S(2)}) copy-start(s32[2,1,1]{0,2,1:T(1,128)} %param.13) | copy-start | bytes 28
  1.0 5.7 %copy-start.4 = (s32[2,2,1,16]{3,2,1,0:T(1,128)S(1)}, s32[2,2,1,16]{3,2,1,0:T(1,128)}, u32[]{:S(2)}) copy-start(s32[2,2,1,16]{3,2,1,0:T(1,128)} %arrivals.1) | copy-start | bytes 772
  1.0 5.7 %copy-start.3 = (s32[2,2,1,16]{3,2,1,0:T(1,128)S(1)}, s32[2,2,1,16]{3,2,1,0:T(1,128)}, u32[]{:S(2)}) copy-start(s32[2,2,1,16]{3,2,1,0:T(1,128)} %movers.1) | copy-start | bytes 772
  1.1 7.2 %collective-permute-start = (f32[24,128]{1,0:T(8,128)S(1)}, f32[24,128]{1,0:T(8,128)S(1)}, u32[]{:S(2)}, u32[]{:S(2)}) collective-permute-start(f32[24,128]{1,0:T(8,128)S(1)} %get-tuple-element.24.sent_near), channel_id=1, source_target_pairs={{0,1},{1,0},{2,3},{3,2},{4,5},{5,4},{6,7},{7,6},{8,9},{9,8},{10,11... | collective-permute-start | bytes 36872 | tf_op jit(solution)/shard_map/ppermute | solution.py:589
  3.1 3.6 %copy-start.2 = (s32[2,32]{1,0:T(2,128)S(1)}, s32[2,32]{1,0:T(2,128)}, u32[]{:S(2)}) copy-start(s32[2,32]{1,0:T(2,128)} %count.5) | copy-start | bytes 772
  3.1 8.9 %collective-permute-start.1 = (f32[24,128]{1,0:T(8,128)S(1)}, f32[24,128]{1,0:T(8,128)S(1)}, u32[]{:S(2)}, u32[]{:S(2)}) collective-permute-start(f32[24,128]{1,0:T(8,128)S(1)} %get-tuple-element.25.sent_far), channel_id=1, source_target_pairs={{1,2},{2,1},{3,4},{4,3},{5,6},{6,5},{9,10},{10,9},{11,12},{12,11},... | collective-permute-start | bytes 36872 | tf_op jit(solution)/shard_map/ppermute | solution.py:589
  12.4 13.3 %collective-permute-start.3 = (f32[376,128]{1,0:T(8,128)S(1)}, f32[376,128]{1,0:T(8,128)S(1)}, u32[]{:S(2)}, u32[]{:S(2)}) collective-permute-start(f32[376,128]{1,0:T(8,128)S(1)} %get-tuple-element.30), channel_id=1, source_target_pairs={{8,16},{16,8},{24,32},{32,24},{40,48},{48,40},{56,64},{64,56},{72,... | collective-permute-start | bytes 577544 | tf_op jit(solution)/shard_map/ppermute | solution.py:589
  20.0 8.8 %collective-permute-start.2 = (f32[376,128]{1,0:T(8,128)S(1)}, f32[376,128]{1,0:T(8,128)S(1)}, u32[]{:S(2)}, u32[]{:S(2)}) collective-permute-start(f32[376,128]{1,0:T(8,128)S(1)} %get-tuple-element.29), channel_id=1, source_target_pairs={{0,8},{8,0},{16,24},{24,16},{32,40},{40,32},{48,56},{56,48},{64,72... | collective-permute-start | bytes 577544 | tf_op jit(solution)/shard_map/ppermute | solution.py:589

commit v5 on v4

--- a/solution.py
+++ b/solution.py
@@ -628,8 +628,8 @@
         in_specs=[vmem] * 6 + [smem],
         out_specs=[vmem] * 8,
         out_shape=[
-            shape(16 * COLS, LANES),
-            shape(16 * COLS, LANES),
+            shape(17 * COLS, LANES),
+            shape(17 * COLS, LANES),
             shape(PAYLOAD, LANES),
             shape(PAYLOAD, LANES),
             shape(COMPS, 2, EXT, LANES),
@@ -647,9 +647,9 @@
         out_shape=[
             shape(PAYLOAD, LANES),
             shape(PAYLOAD, LANES),
-            shape(96, LANES),
-            shape(64, LANES),
-            shape(64, LANES),
+            shape(104, LANES),
+            shape(72, LANES),
+            shape(72, LANES),
         ],
         compiler_params=params,
         name="edge_terms",
@@ -666,14 +666,14 @@
             shape(COMPS, SLAB, LANES),
             shape(3, SLAB, LANES, dtype=ints),
         ],
-        scratch_shapes=[buffer(34 * 40, LANES), buffer(34 * 16, LANES)],
+        scratch_shapes=[buffer(35 * 40, LANES), buffer(34 * 16, LANES)],
         compiler_params=params,
         name="own_sums",
     )(particles, contact_pairs, contact_count, on_first, on_second, edges, edge_first, edge_second, ext)
     own = (sums, ext, first_low, lists_low, stays, landing)
     scratch = [
         buffer(COMPS, EXT, LANES),
-        buffer(8 * SLAB, LANES),
+        buffer(9 * SLAB, LANES),
         buffer(2, SLAB, LANES, dtype=ints),
         buffer(35 * 24, LANES),
     ]

time: 30.6 us -> 30.6 us (level)
  the two profiles are of different devices: /device:TPU:352 before, /device:TPU:288 now
where the time goes in v5:
time: 30.6 us; the launch traced here: 30.3 us
  starting transfers between devices  13.3 us (43%)
  waiting for transfers between devices  9.24 us (30%)
  Pallas kernels  7.49 us (24%)
    ppermute x4, starting transfers between devices, swapped(): return lax.ppermute(block, axis, pairs)  13.3 us
    ppermute x4, waiting for transfers between devices, swapped(): return lax.ppermute(block, axis, pairs)  9.24 us
    pallas_call x1, Pallas kernels, body(): pl.pallas_call(own_sums, in_specs=[vmem] * 9, out_specs=[vmem] * 4, out_s...  1.88 us
    pallas_call x1, Pallas kernels, body(): pl.pallas_call(near_row, in_specs=[vmem] * 8, out_specs=vmem, out_shape=s...  1.56 us
    pallas_call x1, Pallas kernels, body(): pl.pallas_call(inner_terms, in_specs=[vmem] * 6 + [smem], out_specs=[vmem...  1.54 us
    pallas_call x1, Pallas kernels, body(): pl.pallas_call(far_row, in_specs=[vmem] * 7, out_specs=vmem, out_shape=sh...  1.18 us
    pallas_call x1, Pallas kernels, body(): pl.pallas_call(pack_columns, in_specs=[hbm] * 3, out_specs=[vmem] * 2, ou...  1 us
  transfers between devices with their start and end apart: 4, of which 3 were waited for; matrix products, arithmetic and copies ran while one was open for 0% of the time, Pallas kernels for 15%

profile of v5, /device:TPU:288, one launch (start us, length us, event | category | flops | bytes accessed | tf_op | source)
XLA Modules:
  0.0 30.3 jit_solution(15569003407873257583)
XLA Ops:
  0.0 0.0 copy-start.1
  0.0 0.0 copy-start
  0.0 0.0 copy-start.5
  0.0 1.0 %pack_columns.1 = (f32[24,128]{1,0:T(8,128)S(1)}, f32[24,128]{1,0:T(8,128)S(1)}) custom-call(f32[11,2,32,128]{3,2,1,0:T(8,128)} %particles.5, s32[2,2,32,128]{3,2,1,0:T(8,128)} %pairs.5, s32[2,32]{1,0:T(2,128)} %count.5), custom_call_target="tpu_custom_call" | custom-call | tf_op jit(solution)/shard_map/pack_columns/pallas_call | solution.py:608
  1.0 0.0 copy-start.6
  1.0 0.0 copy-start.4
  1.0 0.0 copy-start.3
  1.1 2.1 %collective-permute-start = (f32[24,128]{1,0:T(8,128)S(1)}, f32[24,128]{1,0:T(8,128)S(1)}, u32[]{:S(2)}, u32[]{:S(2)}) collective-permute-start(f32[24,128]{1,0:T(8,128)S(1)} %get-tuple-element.24.sent_near), channel_id=1, source_target_pairs={{0,1},{1,0},{2,3},{3,2},{4,5},{5,4},{6,7},{7,6},{8,9},{9,8},{10,11... | collective-permute-start | bytes 36872 | tf_op jit(solution)/shard_map/ppermute | solution.py:589
  3.1 0.0 copy-start.2
  3.1 1.9 %collective-permute-start.1 = (f32[24,128]{1,0:T(8,128)S(1)}, f32[24,128]{1,0:T(8,128)S(1)}, u32[]{:S(2)}, u32[]{:S(2)}) collective-permute-start(f32[24,128]{1,0:T(8,128)S(1)} %get-tuple-element.25.sent_far), channel_id=1, source_target_pairs={{1,2},{2,1},{3,4},{4,3},{5,6},{6,5},{9,10},{10,9},{11,12},{12,11},... | collective-permute-start | bytes 36872 | tf_op jit(solution)/shard_map/ppermute | solution.py:589
  5.1 0.0 copy-done.6
  5.1 0.1 copy.8.counts
  5.2 0.0 copy-done.1
  5.2 0.0 copy-done
  5.2 0.0 copy-done.5
  5.2 0.0 copy-done.4
  5.2 0.0 copy-done.3
  5.2 0.0 copy-done.2
  5.2 1.5 %inner_terms.1 = (f32[544,128]{1,0:T(8,128)S(1)}, f32[544,128]{1,0:T(8,128)S(1)}, f32[376,128]{1,0:T(8,128)S(1)}, f32[376,128]{1,0:T(8,128)S(1)}, f32[11,2,56,12...) custom-call(f32[11,2,32,128]{3,2,1,0:T(8,128)S(1)} %copy-done, ...), custom_call_target="tpu_custom_call" | custom-call | tf_op jit(solution)/shard_map/inner_terms/pallas_call | solution.py:626
  6.7 0.0 collective-permute-done.got_near
  6.7 5.4 %collective-permute-done.1.got_far = f32[24,128]{1,0:T(8,128)S(1)} collective-permute-done((f32[24,128]{1,0:T(8,128)S(1)}, f32[24,128]{1,0:T(8,128)S(1)}, u32[]{:S(2)}, u32[]{:S(2)}) %collective-permute-start.1) | collective-permute-done | bytes 12320 | tf_op jit(solution)/shard_map/ppermute | solution.py:589
  12.2 0.3 %edge_terms.1 = (f32[376,128]{1,0:T(8,128)S(1)}, f32[376,128]{1,0:T(8,128)S(1)}, f32[104,128]{1,0:T(8,128)S(1)}, f32[72,128]{1,0:T(8,128)S(1)}, f32[72,128]{1,0:T(8,128)S(1)}) custom-call(f32[24,128]{1,0:T(8,128)S(1)} %collective-permute-done.got_near, f32[24,128]{1,0:T(8,128)S(1)} %collective-permute-done.1.got_far, ...), custom_call_target="tpu_custom_call" | custom-call | tf_op jit(solution)/shard_map/edge_terms/pallas_call | solution.py:643
  12.5 7.4 %collective-permute-start.3 = (f32[376,128]{1,0:T(8,128)S(1)}, f32[376,128]{1,0:T(8,128)S(1)}, u32[]{:S(2)}, u32[]{:S(2)}) collective-permute-start(f32[376,128]{1,0:T(8,128)S(1)} %get-tuple-element.30), channel_id=1, source_target_pairs={{8,16},{16,8},{24,32},{32,24},{40,48},{48,40},{56,64},{64,56},{72,... | collective-permute-start | bytes 577544 | tf_op jit(solution)/shard_map/ppermute | solution.py:589
  20.0 1.9 %collective-permute-start.2 = (f32[376,128]{1,0:T(8,128)S(1)}, f32[376,128]{1,0:T(8,128)S(1)}, u32[]{:S(2)}, u32[]{:S(2)}) collective-permute-start(f32[376,128]{1,0:T(8,128)S(1)} %get-tuple-element.29), channel_id=1, source_target_pairs={{0,8},{8,0},{16,24},{24,16},{32,40},{40,32},{48,56},{56,48},{64,72... | collective-permute-start | bytes 577544 | tf_op jit(solution)/shard_map/ppermute | solution.py:589
  21.9 1.9 %own_sums.1 = (f32[2,7,32,128]{3,2,1,0:T(8,128)S(1)}, f32[11,2,56,128]{3,2,1,0:T(8,128)S(1)}, f32[11,40,128]{2,1,0:T(8,128)S(1)}, s32[3,40,128]{2,1,0:T(8,128)S(1)}) custom-call(f32[11,2,32,128]{3,2,1,0:T(8,128)S(1)} %copy-done, s32[2,2,32,128]{3,2,1,0:T(8,128)S(1)} %copy-done.1, s32[2,32]{1,0:T(2,128)S(1)} %copy-done.2, ...), custom_call_target="tpu_custom_call" | custom-call | tf_op jit(solution)/shard_map/own_sums/pallas_call | solution.py:659
  23.8 1.9 %collective-permute-done.3.far = f32[376,128]{1,0:T(8,128)S(1)} collective-permute-done((f32[376,128]{1,0:T(8,128)S(1)}, f32[376,128]{1,0:T(8,128)S(1)}, u32[]{:S(2)}, u32[]{:S(2)}) %collective-permute-start.3) | collective-permute-done | bytes 192544 | tf_op jit(solution)/shard_map/ppermute | solution.py:589
  25.7 1.2 %far_row.1.half = f32[11,32,128]{2,1,0:T(8,128)S(1)} custom-call(f32[376,128]{1,0:T(8,128)S(1)} %collective-permute-done.3.far, f32[2,7,32,128]{3,2,1,0:T(8,128)S(1)} %get-tuple-element.37.sums, f32[11,2,56,128]{3,2,1,0:T(8,128)S(1)} %get-tuple-element.38.ext, f32[11,40,128]{2,1,0:T(8,128)S(1)} %get-tuple-element.39.first_low, ...), custom_call_target="tpu_custom_call" | custom-call | tf_op jit(solution)/shard_map/far_row/pallas_call | solution.py:680
  26.9 1.9 %collective-permute-done.2.near = f32[376,128]{1,0:T(8,128)S(1)} collective-permute-done((f32[376,128]{1,0:T(8,128)S(1)}, f32[376,128]{1,0:T(8,128)S(1)}, u32[]{:S(2)}, u32[]{:S(2)}) %collective-permute-start.2) | collective-permute-done | bytes 192544 | tf_op jit(solution)/shard_map/ppermute | solution.py:589
  28.8 1.6 %near_row.1 = f32[11,2,32,128]{3,2,1,0:T(8,128)} custom-call(f32[376,128]{1,0:T(8,128)S(1)} %collective-permute-done.2.near, f32[11,32,128]{2,1,0:T(8,128)S(1)} %far_row.1.half, f32[2,7,32,128]{3,2,1,0:T(8,128)S(1)} %get-tuple-element.37.sums, f32[11,2,56,128]{3,2,1,0:T(8,128)S(1)} %get-tuple-element.38.ext, f32[11,40,128]{2,1,0:T(8,128)S(1)} %get-tuple-element.39.first_low, ...), custom_call_target="tpu_custom_call" | custom-call | tf_op jit(solution)/shard_map/near_row/pallas_call | solution.py:689
Async XLA Ops:
  0.0 5.2 %copy-start.1 = (s32[2,2,32,128]{3,2,1,0:T(8,128)S(1)}, s32[2,2,32,128]{3,2,1,0:T(8,128)}, u32[]{:S(2)}) copy-start(s32[2,2,32,128]{3,2,1,0:T(8,128)} %pairs.5) | copy-start | bytes 196612
  0.0 5.2 %copy-start = (f32[11,2,32,128]{3,2,1,0:T(8,128)S(1)}, f32[11,2,32,128]{3,2,1,0:T(8,128)}, u32[]{:S(2)}) copy-start(f32[11,2,32,128]{3,2,1,0:T(8,128)} %particles.5) | copy-start | bytes 1081348
  0.0 5.2 %copy-start.5 = (s32[2,32]{1,0:T(2,128)S(1)}, s32[2,32]{1,0:T(2,128)}, u32[]{:S(2)}) copy-start(s32[2,32]{1,0:T(2,128)} %filled.1) | copy-start | bytes 772
  1.0 4.0 %copy-start.6 = (s32[2,1,1]{0,2,1:T(1,128)S(1)}, s32[2,1,1]{0,2,1:T(1,128)}, u32[]{:S(2)}) copy-start(s32[2,1,1]{0,2,1:T(1,128)} %param.13) | copy-start | bytes 28
  1.0 4.1 %copy-start.4 = (s32[2,2,1,16]{3,2,1,0:T(1,128)S(1)}, s32[2,2,1,16]{3,2,1,0:T(1,128)}, u32[]{:S(2)}) copy-start(s32[2,2,1,16]{3,2,1,0:T(1,128)} %arrivals.1) | copy-start | bytes 772
  1.0 4.1 %copy-start.3 = (s32[2,2,1,16]{3,2,1,0:T(1,128)S(1)}, s32[2,2,1,16]{3,2,1,0:T(1,128)}, u32[]{:S(2)}) copy-start(s32[2,2,1,16]{3,2,1,0:T(1,128)} %movers.1) | copy-start | bytes 772
  1.1 5.7 %collective-permute-start = (f32[24,128]{1,0:T(8,128)S(1)}, f32[24,128]{1,0:T(8,128)S(1)}, u32[]{:S(2)}, u32[]{:S(2)}) collective-permute-start(f32[24,128]{1,0:T(8,128)S(1)} %get-tuple-element.24.sent_near), channel_id=1, source_target_pairs={{0,1},{1,0},{2,3},{3,2},{4,5},{5,4},{6,7},{7,6},{8,9},{9,8},{10,11... | collective-permute-start | bytes 36872 | tf_op jit(solution)/shard_map/ppermute | solution.py:589
  3.1 2.1 %copy-start.2 = (s32[2,32]{1,0:T(2,128)S(1)}, s32[2,32]{1,0:T(2,128)}, u32[]{:S(2)}) copy-start(s32[2,32]{1,0:T(2,128)} %count.5) | copy-start | bytes 772
  3.1 9.0 %collective-permute-start.1 = (f32[24,128]{1,0:T(8,128)S(1)}, f32[24,128]{1,0:T(8,128)S(1)}, u32[]{:S(2)}, u32[]{:S(2)}) collective-permute-start(f32[24,128]{1,0:T(8,128)S(1)} %get-tuple-element.25.sent_far), channel_id=1, source_target_pairs={{1,2},{2,1},{3,4},{4,3},{5,6},{6,5},{9,10},{10,9},{11,12},{12,11},... | collective-permute-start | bytes 36872 | tf_op jit(solution)/shard_map/ppermute | solution.py:589
  12.5 13.2 %collective-permute-start.3 = (f32[376,128]{1,0:T(8,128)S(1)}, f32[376,128]{1,0:T(8,128)S(1)}, u32[]{:S(2)}, u32[]{:S(2)}) collective-permute-start(f32[376,128]{1,0:T(8,128)S(1)} %get-tuple-element.30), channel_id=1, source_target_pairs={{8,16},{16,8},{24,32},{32,24},{40,48},{48,40},{56,64},{64,56},{72,... | collective-permute-start | bytes 577544 | tf_op jit(solution)/shard_map/ppermute | solution.py:589
  20.0 8.8 %collective-permute-start.2 = (f32[376,128]{1,0:T(8,128)S(1)}, f32[376,128]{1,0:T(8,128)S(1)}, u32[]{:S(2)}, u32[]{:S(2)}) collective-permute-start(f32[376,128]{1,0:T(8,128)S(1)} %get-tuple-element.29), channel_id=1, source_target_pairs={{0,8},{8,0},{16,24},{24,16},{32,40},{40,32},{48,56},{56,48},{64,72... | collective-permute-start | bytes 577544 | tf_op jit(solution)/shard_map/ppermute | solution.py:589

commit v6 on v5

--- a/solution.py
+++ b/solution.py
@@ -114,7 +114,10 @@
 
 
 def spread(left, *index_rows):
-    hot = jnp.concatenate([one_hot(row) for row in index_rows], 1)
+    return gather_sums(left, jnp.concatenate([one_hot(row) for row in index_rows], 1))
+
+
+def gather_sums(left, hot):
     out = lax.dot_general(
         halves(left), hot, (((1,), (1,)), ((), ())), preferred_element_type=jnp.float32
     )
@@ -359,7 +362,7 @@
 
 def own_sums(
     particles, pairs, count, on_first, on_second, edges, edge_first, edge_second,
-    ext_in, sums, ext, first_low, lists_low, by_source0, by_source1,
+    ext_in, sums, ext, first_low, lists_low, hot_low, by_source0, by_source1,
 ):
     ext[...] = ext_in[...]
     sizes = (40, 16)
@@ -438,6 +441,8 @@
     lists_low[0] = rows
     lists_low[1] = jnp.where(iota((SLAB, LANES), 1) < n, seconds // LANES, -1)
     lists_low[2] = lax.rem(seconds, LANES)
+    for c in range(COLS):
+        hot_low[c] = one_hot(pairs[0, 1, c : c + 1, :])
     for j in range(COMPS):
         first_low[j] = pick(ext[j, 1, BASE : BASE + SLAB, :], rows)
 
@@ -522,7 +527,7 @@
     finish(0, info, state, leaving, totals, ext, stays, landing, write)
 
 
-def from_ahead(source, sums, ext, first_low, lists_low, stays, landing, write, around, terms, by_source):
+def from_ahead(source, sums, ext, first_low, lists_low, hot_low, stays, landing, write, around, terms, by_source):
     surround(around, source)
     heading, target = lists_low[1], lists_low[2]
     f, s = row_terms(
@@ -530,7 +535,7 @@
     )
     keep(terms, 0, f)
     for c in range(COLS):
-        by_source[c * 8 : c * 8 + 8, :] = spread(terms[pl.ds(c, 8, stride=SLAB), :], lists_low[0, c : c + 1, :])
+        by_source[c * 8 : c * 8 + 8, :] = gather_sums(terms[pl.ds(c, 8, stride=SLAB), :], hot_low[c])
     info = around[9, BASE : BASE + COLS, :]
     wide = jnp.broadcast_to(lane_of(info, 7).astype(jnp.int32) - 1, (COLS, LANES))
     wide = jnp.concatenate([wide, jnp.full((8, LANES), -1, jnp.int32)], 0)
@@ -551,7 +556,7 @@
     finish(1, info, state, leaving, totals, ext, stays, landing, write)
 
 
-def far_row(far, sums, ext, first_low, lists_low, stays, landing, half, around, terms, indices, by_source):
+def far_row(far, sums, ext, first_low, lists_low, hot_low, stays, landing, half, around, terms, indices, by_source):
     odd = lax.rem(lax.axis_index("blade"), 2) == 1
 
     def write(side, j, value):
@@ -559,14 +564,14 @@
 
     @pl.when(odd)
     def _():
-        from_ahead(far, sums, ext, first_low, lists_low, stays, landing, write, around, terms, by_source)
+        from_ahead(far, sums, ext, first_low, lists_low, hot_low, stays, landing, write, around, terms, by_source)
 
     @pl.when(jnp.logical_not(odd))
     def _():
         from_behind(far, sums, ext, stays, landing, write, around, terms, indices, by_source)
 
 
-def near_row(near, half, sums, ext, first_low, lists_low, stays, landing, out, around, terms, indices, by_source):
+def near_row(near, half, sums, ext, first_low, lists_low, hot_low, stays, landing, out, around, terms, indices, by_source):
     odd = lax.rem(lax.axis_index("blade"), 2) == 1
 
     def write(side, j, value):
@@ -579,7 +584,7 @@
 
     @pl.when(jnp.logical_not(odd))
     def _():
-        from_ahead(near, sums, ext, first_low, lists_low, stays, landing, write, around, terms, by_source)
+        from_ahead(near, sums, ext, first_low, lists_low, hot_low, stays, landing, write, around, terms, by_source)
 
 
 def swapped(block, axis, start):
@@ -656,21 +661,22 @@
     )(got_near, got_far, near, far, infos, to_near, to_far)
     row_far = swapped(to_far, "blade", 1)
     row_near = swapped(to_near, "blade", 0)
-    sums, ext, first_low, lists_low = pl.pallas_call(
+    sums, ext, first_low, lists_low, hot_low = pl.pallas_call(
         own_sums,
         in_specs=[vmem] * 9,
-        out_specs=[vmem] * 4,
+        out_specs=[vmem] * 5,
         out_shape=[
             shape(2, 7, COLS, LANES),
             shape(COMPS, 2, EXT, LANES),
             shape(COMPS, SLAB, LANES),
             shape(3, SLAB, LANES, dtype=ints),
+            shape(COLS, LANES, LANES, dtype=jnp.bfloat16),
         ],
         scratch_shapes=[buffer(35 * 40, LANES), buffer(34 * 16, LANES)],
         compiler_params=params,
         name="own_sums",
     )(particles, contact_pairs, contact_count, on_first, on_second, edges, edge_first, edge_second, ext)
-    own = (sums, ext, first_low, lists_low, stays, landing)
+    own = (sums, ext, first_low, lists_low, hot_low, stays, landing)
     scratch = [
         buffer(COMPS, EXT, LANES),
         buffer(9 * SLAB, LANES),
@@ -679,7 +685,7 @@
     ]
     half = pl.pallas_call(
         far_row,
-        in_specs=[vmem] * 7,
+        in_specs=[vmem] * 8,
         out_specs=vmem,
         out_shape=shape(COMPS, COLS, LANES),
         scratch_shapes=scratch,
@@ -688,7 +694,7 @@
     )(row_far, *own)
     return pl.pallas_call(
         near_row,
-        in_specs=[vmem] * 8,
+        in_specs=[vmem] * 9,
         out_specs=vmem,
         out_shape=shape(COMPS, 2, COLS, LANES),
         scratch_shapes=scratch,

time: 30.6 us -> 30.5 us (level)
  transfers between devices with their start and end apart: 4 -> 4, of which waited for: 3 -> 3; matrix products, arithmetic and copies ran while one was open for 0% -> 0% of each run, Pallas kernels for 15% -> 16%
where the time goes in v6:
time: 30.5 us; the launch traced here: 30.3 us
  starting transfers between devices  13.3 us (44%)
  waiting for transfers between devices  9.03 us (30%)
  Pallas kernels  7.69 us (25%)
    ppermute x4, starting transfers between devices, swapped(): return lax.ppermute(block, axis, pairs)  13.3 us
    ppermute x4, waiting for transfers between devices, swapped(): return lax.ppermute(block, axis, pairs)  9.03 us
    pallas_call x1, Pallas kernels, body(): pl.pallas_call(own_sums, in_specs=[vmem] * 9, out_specs=[vmem] * 5, out_s...  2.09 us
    pallas_call x1, Pallas kernels, body(): pl.pallas_call(near_row, in_specs=[vmem] * 9, out_specs=vmem, out_shape=s...  1.54 us
    pallas_call x1, Pallas kernels, body(): pl.pallas_call(inner_terms, in_specs=[vmem] * 6 + [smem], out_specs=[vmem...  1.54 us
    pallas_call x1, Pallas kernels, body(): pl.pallas_call(far_row, in_specs=[vmem] * 8, out_specs=vmem, out_shape=sh...  1.18 us
    pallas_call x1, Pallas kernels, body(): pl.pallas_call(pack_columns, in_specs=[hbm] * 3, out_specs=[vmem] * 2, ou...  1 us
  transfers between devices with their start and end apart: 4, of which 3 were waited for; matrix products, arithmetic and copies ran while one was open for 0% of the time, Pallas kernels for 16%

profile of v6, /device:TPU:288, one launch (start us, length us, event | category | flops | bytes accessed | tf_op | source)
XLA Modules:
  0.0 30.3 jit_solution(8931831827268240127)
XLA Ops:
  0.0 0.0 copy-start.1
  0.0 0.0 copy-start
  0.0 0.0 copy-start.5
  0.0 1.0 %pack_columns.1 = (f32[24,128]{1,0:T(8,128)S(1)}, f32[24,128]{1,0:T(8,128)S(1)}) custom-call(f32[11,2,32,128]{3,2,1,0:T(8,128)} %particles.5, s32[2,2,32,128]{3,2,1,0:T(8,128)} %pairs.5, s32[2,32]{1,0:T(2,128)} %count.5), custom_call_target="tpu_custom_call" | custom-call | tf_op jit(solution)/shard_map/pack_columns/pallas_call | solution.py:613
  1.0 0.0 copy-start.6
  1.0 0.0 copy-start.4
  1.0 0.0 copy-start.3
  1.1 2.1 %collective-permute-start = (f32[24,128]{1,0:T(8,128)S(1)}, f32[24,128]{1,0:T(8,128)S(1)}, u32[]{:S(2)}, u32[]{:S(2)}) collective-permute-start(f32[24,128]{1,0:T(8,128)S(1)} %get-tuple-element.25.sent_near), channel_id=1, source_target_pairs={{0,1},{1,0},{2,3},{3,2},{4,5},{5,4},{6,7},{7,6},{8,9},{9,8},{10,11... | collective-permute-start | bytes 36872 | tf_op jit(solution)/shard_map/ppermute | solution.py:594
  3.1 0.0 copy-start.2
  3.1 1.9 %collective-permute-start.1 = (f32[24,128]{1,0:T(8,128)S(1)}, f32[24,128]{1,0:T(8,128)S(1)}, u32[]{:S(2)}, u32[]{:S(2)}) collective-permute-start(f32[24,128]{1,0:T(8,128)S(1)} %get-tuple-element.26.sent_far), channel_id=1, source_target_pairs={{1,2},{2,1},{3,4},{4,3},{5,6},{6,5},{9,10},{10,9},{11,12},{12,11},... | collective-permute-start | bytes 36872 | tf_op jit(solution)/shard_map/ppermute | solution.py:594
  5.1 0.0 copy-done.6
  5.1 0.1 copy.8.counts
  5.2 0.0 copy-done.1
  5.2 0.0 copy-done
  5.2 0.0 copy-done.5
  5.2 0.0 copy-done.4
  5.2 0.0 copy-done.3
  5.2 0.0 copy-done.2
  5.2 1.5 %inner_terms.1 = (f32[544,128]{1,0:T(8,128)S(1)}, f32[544,128]{1,0:T(8,128)S(1)}, f32[376,128]{1,0:T(8,128)S(1)}, f32[376,128]{1,0:T(8,128)S(1)}, f32[11,2,56,12...) custom-call(f32[11,2,32,128]{3,2,1,0:T(8,128)S(1)} %copy-done, ...), custom_call_target="tpu_custom_call" | custom-call | tf_op jit(solution)/shard_map/inner_terms/pallas_call | solution.py:631
  6.7 0.0 collective-permute-done.got_near
  6.7 5.4 %collective-permute-done.1.got_far = f32[24,128]{1,0:T(8,128)S(1)} collective-permute-done((f32[24,128]{1,0:T(8,128)S(1)}, f32[24,128]{1,0:T(8,128)S(1)}, u32[]{:S(2)}, u32[]{:S(2)}) %collective-permute-start.1) | collective-permute-done | bytes 12320 | tf_op jit(solution)/shard_map/ppermute | solution.py:594
  12.2 0.3 %edge_terms.1 = (f32[376,128]{1,0:T(8,128)S(1)}, f32[376,128]{1,0:T(8,128)S(1)}, f32[104,128]{1,0:T(8,128)S(1)}, f32[72,128]{1,0:T(8,128)S(1)}, f32[72,128]{1,0:T(8,128)S(1)}) custom-call(f32[24,128]{1,0:T(8,128)S(1)} %collective-permute-done.got_near, f32[24,128]{1,0:T(8,128)S(1)} %collective-permute-done.1.got_far, ...), custom_call_target="tpu_custom_call" | custom-call | tf_op jit(solution)/shard_map/edge_terms/pallas_call | solution.py:648
  12.5 7.4 %collective-permute-start.3 = (f32[376,128]{1,0:T(8,128)S(1)}, f32[376,128]{1,0:T(8,128)S(1)}, u32[]{:S(2)}, u32[]{:S(2)}) collective-permute-start(f32[376,128]{1,0:T(8,128)S(1)} %get-tuple-element.31), channel_id=1, source_target_pairs={{8,16},{16,8},{24,32},{32,24},{40,48},{48,40},{56,64},{64,56},{72,... | collective-permute-start | bytes 577544 | tf_op jit(solution)/shard_map/ppermute | solution.py:594
  20.0 1.9 %collective-permute-start.2 = (f32[376,128]{1,0:T(8,128)S(1)}, f32[376,128]{1,0:T(8,128)S(1)}, u32[]{:S(2)}, u32[]{:S(2)}) collective-permute-start(f32[376,128]{1,0:T(8,128)S(1)} %get-tuple-element.30), channel_id=1, source_target_pairs={{0,8},{8,0},{16,24},{24,16},{32,40},{40,32},{48,56},{56,48},{64,72... | collective-permute-start | bytes 577544 | tf_op jit(solution)/shard_map/ppermute | solution.py:594
  21.9 2.1 %own_sums.1 = (f32[2,7,32,128]{3,2,1,0:T(8,128)S(1)}, f32[11,2,56,128]{3,2,1,0:T(8,128)S(1)}, f32[11,40,128]{2,1,0:T(8,128)S(1)}, s32[3,40,128]{2,1,0:T(8,128)S(1)}, bf16[32,128,128]{2,1,0:T(8,128)(2,1)S(1)}) custom-call(f32[11,2,32,128]{3,2,1,0:T(8,128)S(1)} %copy-done, s32[2,2,32,128]{3,2,1,0:T(8,128)S(1)} %copy-done.1, s32[2,32]{1,0:T(2,128)S(1)} %copy-done.2, ...), custom_call_target="tpu_custom_call" | custom-call | tf_op jit(solution)/shard_map/own_sums/pallas_call | solution.py:664
  24.0 1.7 %collective-permute-done.3.far = f32[376,128]{1,0:T(8,128)S(1)} collective-permute-done((f32[376,128]{1,0:T(8,128)S(1)}, f32[376,128]{1,0:T(8,128)S(1)}, u32[]{:S(2)}, u32[]{:S(2)}) %collective-permute-start.3) | collective-permute-done | bytes 192544 | tf_op jit(solution)/shard_map/ppermute | solution.py:594
  25.7 1.2 %far_row.1.half = f32[11,32,128]{2,1,0:T(8,128)S(1)} custom-call(f32[376,128]{1,0:T(8,128)S(1)} %collective-permute-done.3.far, f32[2,7,32,128]{3,2,1,0:T(8,128)S(1)} %get-tuple-element.38.sums, f32[11,2,56,128]{3,2,1,0:T(8,128)S(1)} %get-tuple-element.39.ext, f32[11,40,128]{2,1,0:T(8,128)S(1)} %get-tuple-element.40.first_low, ...), custom_call_target="tpu_custom_call" | custom-call | tf_op jit(solution)/shard_map/far_row/pallas_call | solution.py:686
  26.9 1.9 %collective-permute-done.2.near = f32[376,128]{1,0:T(8,128)S(1)} collective-permute-done((f32[376,128]{1,0:T(8,128)S(1)}, f32[376,128]{1,0:T(8,128)S(1)}, u32[]{:S(2)}, u32[]{:S(2)}) %collective-permute-start.2) | collective-permute-done | bytes 192544 | tf_op jit(solution)/shard_map/ppermute | solution.py:594
  28.8 1.5 %near_row.1 = f32[11,2,32,128]{3,2,1,0:T(8,128)} custom-call(f32[376,128]{1,0:T(8,128)S(1)} %collective-permute-done.2.near, f32[11,32,128]{2,1,0:T(8,128)S(1)} %far_row.1.half, f32[2,7,32,128]{3,2,1,0:T(8,128)S(1)} %get-tuple-element.38.sums, f32[11,2,56,128]{3,2,1,0:T(8,128)S(1)} %get-tuple-element.39.ext, f32[11,40,128]{2,1,0:T(8,128)S(1)} %get-tuple-element.40.first_low, ...), custom_call_target="tpu_custom_call" | custom-call | tf_op jit(solution)/shard_map/near_row/pallas_call | solution.py:695
Async XLA Ops:
  0.0 5.2 %copy-start.1 = (s32[2,2,32,128]{3,2,1,0:T(8,128)S(1)}, s32[2,2,32,128]{3,2,1,0:T(8,128)}, u32[]{:S(2)}) copy-start(s32[2,2,32,128]{3,2,1,0:T(8,128)} %pairs.5) | copy-start | bytes 196612
  0.0 5.2 %copy-start = (f32[11,2,32,128]{3,2,1,0:T(8,128)S(1)}, f32[11,2,32,128]{3,2,1,0:T(8,128)}, u32[]{:S(2)}) copy-start(f32[11,2,32,128]{3,2,1,0:T(8,128)} %particles.5) | copy-start | bytes 1081348
  0.0 5.2 %copy-start.5 = (s32[2,32]{1,0:T(2,128)S(1)}, s32[2,32]{1,0:T(2,128)}, u32[]{:S(2)}) copy-start(s32[2,32]{1,0:T(2,128)} %filled.1) | copy-start | bytes 772
  1.0 4.0 %copy-start.6 = (s32[2,1,1]{0,2,1:T(1,128)S(1)}, s32[2,1,1]{0,2,1:T(1,128)}, u32[]{:S(2)}) copy-start(s32[2,1,1]{0,2,1:T(1,128)} %param.13) | copy-start | bytes 28
  1.0 4.1 %copy-start.4 = (s32[2,2,1,16]{3,2,1,0:T(1,128)S(1)}, s32[2,2,1,16]{3,2,1,0:T(1,128)}, u32[]{:S(2)}) copy-start(s32[2,2,1,16]{3,2,1,0:T(1,128)} %arrivals.1) | copy-start | bytes 772
  1.0 4.1 %copy-start.3 = (s32[2,2,1,16]{3,2,1,0:T(1,128)S(1)}, s32[2,2,1,16]{3,2,1,0:T(1,128)}, u32[]{:S(2)}) copy-start(s32[2,2,1,16]{3,2,1,0:T(1,128)} %movers.1) | copy-start | bytes 772
  1.1 5.7 %collective-permute-start = (f32[24,128]{1,0:T(8,128)S(1)}, f32[24,128]{1,0:T(8,128)S(1)}, u32[]{:S(2)}, u32[]{:S(2)}) collective-permute-start(f32[24,128]{1,0:T(8,128)S(1)} %get-tuple-element.25.sent_near), channel_id=1, source_target_pairs={{0,1},{1,0},{2,3},{3,2},{4,5},{5,4},{6,7},{7,6},{8,9},{9,8},{10,11... | collective-permute-start | bytes 36872 | tf_op jit(solution)/shard_map/ppermute | solution.py:594
  3.1 2.1 %copy-start.2 = (s32[2,32]{1,0:T(2,128)S(1)}, s32[2,32]{1,0:T(2,128)}, u32[]{:S(2)}) copy-start(s32[2,32]{1,0:T(2,128)} %count.5) | copy-start | bytes 772
  3.1 9.0 %collective-permute-start.1 = (f32[24,128]{1,0:T(8,128)S(1)}, f32[24,128]{1,0:T(8,128)S(1)}, u32[]{:S(2)}, u32[]{:S(2)}) collective-permute-start(f32[24,128]{1,0:T(8,128)S(1)} %get-tuple-element.26.sent_far), channel_id=1, source_target_pairs={{1,2},{2,1},{3,4},{4,3},{5,6},{6,5},{9,10},{10,9},{11,12},{12,11},... | collective-permute-start | bytes 36872 | tf_op jit(solution)/shard_map/ppermute | solution.py:594
  12.5 13.2 %collective-permute-start.3 = (f32[376,128]{1,0:T(8,128)S(1)}, f32[376,128]{1,0:T(8,128)S(1)}, u32[]{:S(2)}, u32[]{:S(2)}) collective-permute-start(f32[376,128]{1,0:T(8,128)S(1)} %get-tuple-element.31), channel_id=1, source_target_pairs={{8,16},{16,8},{24,32},{32,24},{40,48},{48,40},{56,64},{64,56},{72,... | collective-permute-start | bytes 577544 | tf_op jit(solution)/shard_map/ppermute | solution.py:594
  20.0 8.8 %collective-permute-start.2 = (f32[376,128]{1,0:T(8,128)S(1)}, f32[376,128]{1,0:T(8,128)S(1)}, u32[]{:S(2)}, u32[]{:S(2)}) collective-permute-start(f32[376,128]{1,0:T(8,128)S(1)} %get-tuple-element.30), channel_id=1, source_target_pairs={{0,8},{8,0},{16,24},{24,16},{32,40},{40,32},{48,56},{56,48},{64,72... | collective-permute-start | bytes 577544 | tf_op jit(solution)/shard_map/ppermute | solution.py:594
